TPU v7x, 256 devices: a whole 4x4x8 slice. The times are simulated.
256 devices in a mesh: space: 32 (over x_lo, z, core), mode: 8 (over y, x_hi).
Axes of the slice: x: 4 (x_hi: 2, x_lo: 2; x = x_hi * 2 + x_lo), y: 4, z: 8, core: 2. Of those that a mesh axis runs over, the one named last changes fastest.
Arguments:
- load: float32 [128, 64, 8, 256], P('mode', 'space'), may hold values from -48 to 48
- mean_coeff: float32 [64, 8, 256], P('space'), may hold values from 0.5 to 2
- kl_ratio: float32 [10, 64, 8, 256], P(None, 'space'), may hold values from -0.04 to 0.04
- chaos_table: int32 [128, 10], replicated, may hold values from 0 to 3, as said below
Outputs:
- solution: float32 [128, 64, 8, 256], P('mode', 'space')
- residual: float32 [128, 64, 8, 256], P('mode', 'space')
Inputs may be any that keep to these rules, and one draw needn't show every extreme that they name: `chaos_table`: the rows are distinct multi-indices of total degree at most 3; every multi-index of total degree at most 2 is a row, and exactly one row has an entry equal to 3.
All inputs are finite; a program needn't handle non-finite values.
Results may differ from a plain program's by a relative error of at most 0.00014.
Values sent between devices are 32-bit elements; how exact they have to be, the bound alone decides.
No kernel may reach another device: no remote copies, remote signals or barrier semaphores. Data moves between devices by JAX's collectives and lax.ppermute only.
A program may use at most 64 MiB of HBM per device.

v0:
```python
import jax
import jax.numpy as jnp
from jax import lax
from jax.sharding import PartitionSpec as P

ITERS = 2


theta_value = 24.5
delta_value = 23.5
reaction = 1.0


def with_halo(cells, sides, width):
    for axis, dim in sides:
        count = lax.axis_size(axis)
        ends = count - 1
        head = lax.slice_in_dim(cells, 0, width, axis=dim)
        tail = lax.slice_in_dim(cells, cells.shape[dim] - width, cells.shape[dim], axis=dim)
        cells = jnp.concatenate(
            [
                lax.ppermute(tail, axis, [(i, (i + 1) % count) for i in range(ends)]),
                cells,
                lax.ppermute(head, axis, [((i + 1) % count, i) for i in range(ends)]),
            ],
            axis=dim,
        )
    return cells


def coupling(chaos_table):
    modes = chaos_table.shape[0]
    differ = chaos_table[:, None, :] - chaos_table[None, :, :]
    distance = jnp.sum(jnp.abs(differ), axis=2)
    larger = jnp.maximum(chaos_table[:, None, :], chaos_table[None, :, :]).astype(jnp.float32)
    linked = (distance[:, :, None] == 1) & (jnp.abs(differ) == 1)
    values = jnp.where(linked, jnp.sqrt(larger), jnp.zeros_like(larger))
    values = jnp.transpose(values, (2, 0, 1))
    identity = jnp.eye(modes, dtype=jnp.float32)
    return jnp.concatenate([identity[None], values], axis=0)


def face_terms(padded):
    face_x = 0.5 * (padded[:, 1:, 1:-1, 1:-1] + padded[:, :-1, 1:-1, 1:-1])
    face_y = 0.5 * (padded[:, 1:-1, 1:, 1:-1] + padded[:, 1:-1, :-1, 1:-1])
    face_z = 0.5 * (padded[:, 1:-1, 1:-1, 1:] + padded[:, 1:-1, 1:-1, :-1])
    return (face_x, face_y, face_z)


def stencil(field_pad, face_x, face_y, face_z):
    flux_x = face_x * (field_pad[..., 1:, 1:-1, 1:-1] - field_pad[..., :-1, 1:-1, 1:-1])
    flux_y = face_y * (field_pad[..., 1:-1, 1:, 1:-1] - field_pad[..., 1:-1, :-1, 1:-1])
    flux_z = face_z * (field_pad[..., 1:-1, 1:-1, 1:] - field_pad[..., 1:-1, 1:-1, :-1])
    result = flux_x[..., :-1, :, :] - flux_x[..., 1:, :, :]
    result = result + (flux_y[..., :, :-1, :] - flux_y[..., :, 1:, :])
    return result + (flux_z[..., :-1] - flux_z[..., 1:])


def pad_sides(field):
    widths = [(0, 0)] * (field.ndim - 2) + [(1, 1), (1, 1)]
    return jnp.pad(field, widths)


def body(load, mean_coeff, kl_ratio, chaos_table):
    own_count = load.shape[0]
    all_modes = chaos_table.shape[0]
    terms_count = kl_ratio.shape[0] + 1
    couple = coupling(chaos_table)
    own_start = lax.axis_index("mode") * own_count
    coeffs = jnp.concatenate([mean_coeff[None], mean_coeff[None] * kl_ratio], axis=0)
    coeff_pad = with_halo(coeffs, (("space", 1),), 1)
    face_x, face_y, face_z = face_terms(pad_sides(coeff_pad))
    field_shape = load.shape
    own_rows = lax.dynamic_slice_in_dim(couple, own_start, own_count, 1)
    rows_flat = own_rows.reshape(terms_count * own_count, all_modes)
    sigma = theta_value / delta_value
    rho_now = 1.0 / sigma
    solution = jnp.zeros_like(load)
    residual = load
    search = load / theta_value
    for sweep in range(ITERS):
        solution = solution + search
        shard_piece = lax.all_gather(search, "mode", axis=0, tiled=True)
        count = shard_piece.shape[0]
        totals = jnp.dot(
            rows_flat,
            shard_piece.reshape(count, -1),
            precision=lax.Precision.HIGHEST,
            preferred_element_type=jnp.float32,
        )
        mixture = totals.reshape((terms_count, own_count) + field_shape[1:])
        padded = with_halo(mixture, (("space", 2),), 1)
        flows = stencil(pad_sides(padded), face_x[:, None], face_y[:, None], face_z[:, None])
        residual = residual - (reaction * search + jnp.sum(flows, axis=0))
        if sweep + 1 < ITERS:
            rho_next = 1.0 / (2.0 * sigma - rho_now)
            search = rho_next * rho_now * search + 2.0 * rho_next / delta_value * residual
            rho_now = rho_next
    return (solution, residual)


def solution(mesh):
    in_specs = (
        P("mode", "space", None, None),
        P("space", None, None),
        P(None, "space", None, None),
        P(),
    )
    out_specs = (P("mode", "space", None, None), P("mode", "space", None, None))
    return jax.shard_map(body, mesh=mesh, in_specs=in_specs, out_specs=out_specs, check_vma=False)
```

profile of v0, /device:TPU:97, one launch (start us, length us, event | category | flops | bytes accessed | tf_op | source)
XLA Modules:
  0.0 228.5 jit_solution(9183631509283126299)
XLA Ops:
  7.2 1.1 copy_multiply_fusion
  8.3 0.9 copy.23
  9.3 1.0 abs_reduce_fusion
  10.3 1.2 sqrt_select_fusion
  11.6 60.2 %all-gather.3.cloned.1.call-done = f32[128,2,8,256]{3,2,1,0:T(8,128)} async-done(((f32[16,2,8,256]{3,2,1,0:T(8,128)}), f32[128,2,8,256]{3,2,1,0:T(8,128)}) %all-gather.3.cloned.1.call-update) | async-done | bytes 2097168 | tf_op jit(solution)/shard_map/all_gather | solution.py:83
  71.7 2.0 copy.31
  73.7 2.5 %fusion.17 = f32[11,16,2,8,256]{4,1,3,2,0:T(8,128)S(1)} fusion(f32[128,2,8,256]{0,3,2,1:T(8,128)S(1)} %copy.31, s32[]{:T(128)S(6)} %select_n.9, f32[1,128,128]{2,1,0:T(8,128)S(1)} %fusion.30, f32[10,128,128]{2,1,0:T(8,128)S(1)} %sqrt_select_fusion), kind=kOutput, calls=%fused_computation.37 | convolution fusion | flops 1107318784 | bytes 5701636 | tf_op jit(solution)/shard_map/dot_general | solution.py:85
  76.7 5.4 %collective-permute-start.3 = (f32[11,16,1,8,256]{4,1,3,2,0:T(8,128)S(1)}, f32[11,16,1,8,256]{4,1,3,2,0:T(8,128)}, u32[]{:S(2)}, u32[]{:S(2)}) collective-permute-start(f32[11,16,1,8,256]{4,1,3,2,0:T(8,128)S(1)} %get-tuple-element.8), channel_id=1, source_target_pairs={{0,8},{8,16},{16,24},{24,32},{32,40},{40,48},{48,56},{56,64},{64,7... | collective-permute-start | bytes 4325384 | tf_op jit(solution)/shard_map/ppermute | solution.py:22
  82.0 1.9 collective-permute-start.2
  84.0 4.9 %collective-permute-start.1 = (f32[11,1,8,256]{3,2,1,0:T(8,128)S(1)}, f32[11,1,8,256]{3,2,1,0:T(8,128)S(1)}, u32[]{:S(2)}, u32[]{:S(2)}) collective-permute-start(f32[11,1,8,256]{3,2,1,0:T(8,128)S(1)} %get-tuple-element.12), channel_id=1, source_target_pairs={{0,8},{8,16},{16,24},{24,32},{32,40},{40,48},{48,56},{56,64},{64,7... | collective-permute-start | bytes 270344 | tf_op jit(solution)/shard_map/ppermute | solution.py:22
  88.9 2.1 collective-permute-start
  91.0 7.9 %collective-permute-done.1 = f32[11,1,8,256]{3,2,1,0:T(8,128)S(1)} collective-permute-done((f32[11,1,8,256]{3,2,1,0:T(8,128)S(1)}, f32[11,1,8,256]{3,2,1,0:T(8,128)S(1)}, u32[]{:S(2)}, u32[]{:S(2)}) %collective-permute-start.1) | collective-permute-done | bytes 90144 | tf_op jit(solution)/shard_map/ppermute | solution.py:22
  98.9 5.6 %collective-permute-done = f32[11,1,8,256]{3,2,1,0:T(8,128)S(1)} collective-permute-done((f32[11,1,8,256]{3,2,1,0:T(8,128)S(1)}, f32[11,1,8,256]{3,2,1,0:T(8,128)S(1)}, u32[]{:S(2)}, u32[]{:S(2)}) %collective-permute-start) | collective-permute-done | bytes 90144 | tf_op jit(solution)/shard_map/ppermute | solution.py:24
  105.4 6.5 %select_maximum_fusion.2 = f32[11,16,4,10,258]{4,1,3,2,0:T(8,128)S(1)} fusion(f32[11,16,1,8,256]{4,1,3,2,0:T(8,128)} %collective-permute-done.2, f32[11,16,2,8,256]{4,1,3,2,0:T(8,128)S(1)} %fusion.17, f32[11,16,1,8,256]{4,1,3,2,0:T(8,128)} %collective-permute-done.3), kind=kLoop, calls=%fused_computation.6 | loop fusion | flops 27244800 | bytes 13032448 | tf_op jit(solution)/shard_map/concatenate | solution.py:20
  111.9 1.8 fusion.8
  113.7 1.2 fusion.4
  114.9 2.9 %fusion.5 = f32[11,16,3,8,256]{4,1,3,2,0:T(8,128)S(1)} fusion(f32[11,16,1,8,256]{4,1,3,2,0:T(8,128)} %collective-permute-done.2, f32[11,16,2,8,256]{4,1,3,2,0:T(8,128)S(1)} %fusion.17, f32[11,16,1,8,256]{4,1,3,2,0:T(8,128)} %collective-permute-done.3, f32[11,3,8,256]{3,2,1,0:T(8,128)S(1)} %fusion.25), kind=kLoop, calls=%fused_computation.16 | loop fusion | flops 4325376 | bytes 10362880 | tf_op jit(solution)/shard_map/mul | solution.py:51
  117.9 1.4 fusion.13
  119.5 0.9 copy.26
  120.4 54.0 %all-gather.5.cloned.1.call-done = f32[128,2,8,256]{3,2,1,0:T(8,128)} async-done(((f32[16,2,8,256]{3,2,1,0:T(8,128)}), f32[128,2,8,256]{3,2,1,0:T(8,128)}) %all-gather.5.cloned.1.call-update) | async-done | bytes 2097168 | tf_op jit(solution)/shard_map/all_gather | solution.py:83
  174.4 2.0 copy.32
  176.4 2.5 %fusion.15 = f32[11,16,2,8,256]{4,1,3,2,0:T(8,128)S(1)} fusion(f32[128,2,8,256]{0,3,2,1:T(8,128)S(1)} %copy.32, s32[]{:T(128)S(6)} %select_n.9, f32[1,128,128]{2,1,0:T(8,128)S(1)} %fusion.30, f32[10,128,128]{2,1,0:T(8,128)S(1)} %sqrt_select_fusion), kind=kOutput, calls=%fused_computation.35 | convolution fusion | flops 1107318784 | bytes 5701636 | tf_op jit(solution)/shard_map/dot_general | solution.py:85
  179.3 5.4 %collective-permute-start.5 = (f32[11,16,1,8,256]{4,1,3,2,0:T(8,128)S(1)}, f32[11,16,1,8,256]{4,1,3,2,0:T(8,128)S(1)}, u32[]{:S(2)}, u32[]{:S(2)}) collective-permute-start(f32[11,16,1,8,256]{4,1,3,2,0:T(8,128)S(1)} %get-tuple-element.6), channel_id=1, source_target_pairs={{0,8},{8,16},{16,24},{24,32},{32,40},{40,48},{48,56},{56,64},{64,7... | collective-permute-start | bytes 4325384 | tf_op jit(solution)/shard_map/ppermute | solution.py:22
  184.6 2.3 collective-permute-start.4
  186.9 13.6 %collective-permute-done.5 = f32[11,16,1,8,256]{4,1,3,2,0:T(8,128)S(1)} collective-permute-done((f32[11,16,1,8,256]{4,1,3,2,0:T(8,128)S(1)}, f32[11,16,1,8,256]{4,1,3,2,0:T(8,128)S(1)}, u32[]{:S(2)}, u32[]{:S(2)}) %collective-permute-start.5) | collective-permute-done | bytes 1441824 | tf_op jit(solution)/shard_map/ppermute | solution.py:22
  200.6 5.9 %collective-permute-done.4 = f32[11,16,1,8,256]{4,1,3,2,0:T(8,128)} collective-permute-done((f32[11,16,1,8,256]{4,1,3,2,0:T(8,128)S(1)}, f32[11,16,1,8,256]{4,1,3,2,0:T(8,128)}, u32[]{:S(2)}, u32[]{:S(2)}) %collective-permute-start.4) | collective-permute-done | bytes 1441824 | tf_op jit(solution)/shard_map/ppermute | solution.py:24
  206.4 6.3 %select_maximum_fusion = f32[11,16,4,10,258]{4,1,3,2,0:T(8,128)S(1)} fusion(f32[11,16,1,8,256]{4,1,3,2,0:T(8,128)} %collective-permute-done.4, f32[11,16,2,8,256]{4,1,3,2,0:T(8,128)S(1)} %fusion.15, f32[11,16,1,8,256]{4,1,3,2,0:T(8,128)S(1)} %collective-permute-done.5), kind=kLoop, calls=%fused_computation.4 | loop fusion | flops 27244800 | bytes 13032448 | tf_op jit(solution)/shard_map/concatenate | solution.py:20
  212.7 1.8 fusion.7
  214.5 1.2 fusion.3
  215.7 2.5 %fusion.6 = f32[11,16,3,8,256]{4,1,3,2,0:T(8,128)S(1)} fusion(f32[11,16,1,8,256]{4,1,3,2,0:T(8,128)} %collective-permute-done.4, f32[11,16,2,8,256]{4,1,3,2,0:T(8,128)S(1)} %fusion.15, f32[11,16,1,8,256]{4,1,3,2,0:T(8,128)S(1)} %collective-permute-done.5, f32[11,3,8,256]{3,2,1,0:T(8,128)S(1)} %fusion.25), kind=kLoop, calls=%fused_computation.18 | loop fusion | flops 4325376 | bytes 10362880 | tf_op jit(solution)/shard_map/mul | solution.py:51
  218.2 1.4 fusion.10
  219.9 0.9 copy.29
  (39 shorter events, 3.1 us)
Async XLA Ops:
  7.2 64.6 %all-gather.3.cloned.1.call-start = ((), (), s32[]{:S(2)}) async-start(), calls=%async_computation | async-start | bytes 2359296 | tf_op jit(solution)/shard_map/all_gather | solution.py:83
  9.2 165.1 %all-gather.5.cloned.1.call-start = ((), (), s32[]{:S(2)}) async-start(), calls=%async_computation.1 | async-start | bytes 2359296 | tf_op jit(solution)/shard_map/all_gather | solution.py:83
  76.2 7.7 %copy-start.8 = (f32[2,8,256]{2,1,0:T(8,128)S(1)}, f32[2,8,256]{2,1,0:T(8,128)}, u32[]{:S(2)}) copy-start(f32[2,8,256]{2,1,0:T(8,128)} %param.5) | copy-start | bytes 49156
  76.2 7.7 %copy-start.9 = (f32[10,2,8,256]{3,2,1,0:T(8,128)S(1)}, f32[10,2,8,256]{3,2,1,0:T(8,128)}, u32[]{:S(2)}) copy-start(f32[10,2,8,256]{3,2,1,0:T(8,128)} %param.6) | copy-start | bytes 491524
  76.7 28.7 %collective-permute-start.3 = (f32[11,16,1,8,256]{4,1,3,2,0:T(8,128)S(1)}, f32[11,16,1,8,256]{4,1,3,2,0:T(8,128)}, u32[]{:S(2)}, u32[]{:S(2)}) collective-permute-start(f32[11,16,1,8,256]{4,1,3,2,0:T(8,128)S(1)} %get-tuple-element.8), channel_id=1, source_target_pairs={{0,8},{8,16},{16,24},{24,32},{32,40},{40,48},{48,56},{56,64},{64,7... | collective-permute-start | bytes 4325384 | tf_op jit(solution)/shard_map/ppermute | solution.py:22
  82.0 23.4 %collective-permute-start.2 = (f32[11,16,1,8,256]{4,1,3,2,0:T(8,128)S(1)}, f32[11,16,1,8,256]{4,1,3,2,0:T(8,128)}, u32[]{:S(2)}, u32[]{:S(2)}) collective-permute-start(f32[11,16,1,8,256]{4,1,3,2,0:T(8,128)S(1)} %get-tuple-element.9), channel_id=1, source_target_pairs={{8,0},{16,8},{24,16},{32,24},{40,32},{48,40},{56,48},{64,56},{72,6... | collective-permute-start | bytes 4325384 | tf_op jit(solution)/shard_map/ppermute | solution.py:24
  84.0 14.9 %collective-permute-start.1 = (f32[11,1,8,256]{3,2,1,0:T(8,128)S(1)}, f32[11,1,8,256]{3,2,1,0:T(8,128)S(1)}, u32[]{:S(2)}, u32[]{:S(2)}) collective-permute-start(f32[11,1,8,256]{3,2,1,0:T(8,128)S(1)} %get-tuple-element.12), channel_id=1, source_target_pairs={{0,8},{8,16},{16,24},{24,32},{32,40},{40,48},{48,56},{56,64},{64,7... | collective-permute-start | bytes 270344 | tf_op jit(solution)/shard_map/ppermute | solution.py:22
  88.9 15.7 %collective-permute-start = (f32[11,1,8,256]{3,2,1,0:T(8,128)S(1)}, f32[11,1,8,256]{3,2,1,0:T(8,128)S(1)}, u32[]{:S(2)}, u32[]{:S(2)}) collective-permute-start(f32[11,1,8,256]{3,2,1,0:T(8,128)S(1)} %get-tuple-element.13), channel_id=1, source_target_pairs={{8,0},{16,8},{24,16},{32,24},{40,32},{48,40},{56,48},{64,56},{72,6... | collective-permute-start | bytes 270344 | tf_op jit(solution)/shard_map/ppermute | solution.py:24
  105.1 8.6 %copy-start.2 = (f32[11,2,8,257]{3,2,1,0:T(8,128)}, f32[11,2,8,257]{3,2,1,0:T(8,128)S(1)}, u32[]{:S(2)}) copy-start(f32[11,2,8,257]{3,2,1,0:T(8,128)S(1)} %fusion.24) | copy-start | bytes 542788
  105.4 6.5 %copy-start = (f32[11,2,9,256]{3,2,1,0:T(8,128)}, f32[11,2,9,256]{3,2,1,0:T(8,128)S(1)}, u32[]{:S(2)}) copy-start(f32[11,2,9,256]{3,2,1,0:T(8,128)S(1)} %fusion.23) | copy-start | bytes 608260
  117.8 1.4 copy-start.6
  119.3 1.1 copy-start.4
  179.3 21.3 %collective-permute-start.5 = (f32[11,16,1,8,256]{4,1,3,2,0:T(8,128)S(1)}, f32[11,16,1,8,256]{4,1,3,2,0:T(8,128)S(1)}, u32[]{:S(2)}, u32[]{:S(2)}) collective-permute-start(f32[11,16,1,8,256]{4,1,3,2,0:T(8,128)S(1)} %get-tuple-element.6), channel_id=1, source_target_pairs={{0,8},{8,16},{16,24},{24,32},{32,40},{40,48},{48,56},{56,64},{64,7... | collective-permute-start | bytes 4325384 | tf_op jit(solution)/shard_map/ppermute | solution.py:22
  184.6 28.1 %copy-start.1 = (f32[11,2,9,256]{3,2,1,0:T(8,128)S(1)}, f32[11,2,9,256]{3,2,1,0:T(8,128)}, u32[]{:S(2)}) copy-start(f32[11,2,9,256]{3,2,1,0:T(8,128)} %copy-done) | copy-start | bytes 608260
  184.6 21.8 %collective-permute-start.4 = (f32[11,16,1,8,256]{4,1,3,2,0:T(8,128)S(1)}, f32[11,16,1,8,256]{4,1,3,2,0:T(8,128)}, u32[]{:S(2)}, u32[]{:S(2)}) collective-permute-start(f32[11,16,1,8,256]{4,1,3,2,0:T(8,128)S(1)} %get-tuple-element.7), channel_id=1, source_target_pairs={{8,0},{16,8},{24,16},{32,24},{40,32},{48,40},{56,48},{64,56},{72,6... | collective-permute-start | bytes 4325384 | tf_op jit(solution)/shard_map/ppermute | solution.py:24
  212.7 1.8 copy-start.3
  218.2 1.5 copy-start.5
  218.2 1.5 copy-start.7
Sparse Core Ops, SparseCore 0:
  11.2 60.4 all-gather.2
  120.5 53.8 all-gather.4
where the time goes:
time: 229 us; the launch traced here: 228 us
  waiting for transfers between devices  147 us (64%)
  other arithmetic  31.6 us (14%)
  starting transfers between devices  21.9 us (10%)
  between operations  14.5 us (6%)
  local copies, waits for them, and re-layouts  8.27 us (4%)
  matrix products  4.97 us (2%)
    all_gather x2, waiting for transfers between devices, body(): shard_piece = lax.all_gather(search, 'mode', axis=0, tiled=True)  114 us
    ppermute x3, waiting for transfers between devices, with_halo(): lax.ppermute(tail, axis, [(i, (i + 1) % count) for i in range(ends)])  21.6 us
    ppermute x3, starting transfers between devices, with_halo(): lax.ppermute(tail, axis, [(i, (i + 1) % count) for i in range(ends)])  15.6 us
    concatenate x3, other arithmetic, with_halo(): jnp.concatenate([lax.ppermute(tail, axis, [(i, (i + 1) % count) for i in...  13.1 us
    ppermute x3, waiting for transfers between devices, with_halo(): lax.ppermute(head, axis, [((i + 1) % count, i) for i in range(ends)])  11.5 us
    ppermute x3, starting transfers between devices, with_halo(): lax.ppermute(head, axis, [((i + 1) % count, i) for i in range(ends)])  6.3 us
    mul x2, other arithmetic, stencil(): face_x * (field_pad[..., 1:, 1:-1, 1:-1] - field_pad[..., :-1, 1:-1, 1:-1])  5.4 us
    dot_general x2, matrix products, body(): jnp.dot(rows_flat, shard_piece.reshape(count, -1), precision=lax.Precisio...  4.97 us
  transfers between devices with their start and end apart: 8, of which 6 were waited for; matrix products, arithmetic and copies ran while one was open for 1% of the time, Pallas kernels for 0%

commit v1 on v0

v1 whole, which is shorter than its diff:
```python
import functools

import jax
import jax.numpy as jnp
from jax import lax
from jax.experimental import pallas as pl
from jax.experimental.pallas import tpu as pltpu
from jax.sharding import PartitionSpec as P

ITERS = 2
THETA = 24.5
DELTA = 23.5
KL = 10
MODES = 128
GROUPS = 8
OWN = MODES // GROUPS
NX_OWN = 2
NY = 8
NZ = 256
ROWS = NX_OWN * NY
ZC = NZ // GROUPS
HALO = 2
ZW = ZC + 2 * HALO
PLANE = NY * ZW
SLAB = NX_OWN * PLANE
SLAB_TILES = -(-SLAB // 128)
SLAB_LANES = SLAB_TILES * 128
WIDE_TILES = -(-3 * SLAB // 128)
WIDE = WIDE_TILES * 128
COEF_ROWS = 16
SEND_ROWS = SLAB_TILES * OWN + COEF_ROWS
OUT_TILES = ROWS * ZC // 128
SQRT2 = 2.0**0.5
SQRT6 = 6.0**0.5
VMEM = 40 * 1024 * 1024


def lanes(shape):
    return lax.broadcasted_iota(jnp.int32, shape, len(shape) - 1)


def mode_scale(table):
    t = table
    f = jnp.where(t >= 3, SQRT6, jnp.where(t == 2, SQRT2, 1.0)).astype(jnp.float32)
    return jnp.max(f, axis=1, keepdims=True)


def pack_kernel(load_ref, mean_ref, ratio_ref, table_ref, out_ref, halves):
    me = lax.axis_index("mode")
    flip = 1 - lax.rem(lax.axis_index("space"), 2)
    scale = mode_scale(table_ref[pl.ds(pl.multiple_of(me * OWN, OWN), OWN), :])
    lane = lanes((OWN, 128))
    out_ref[...] = jnp.zeros_like(out_ref)
    for h in range(NZ // 128):
        halves[h] = load_ref[:, 128 * h : 128 * h + 128]
    for p in range(ROWS):
        plane, y = p // NY, p % NY
        row = (plane + flip * (1 - 2 * plane)) * NY + y
        v = [halves[h, pl.ds(row, OWN, stride=ROWS), :] * scale for h in range(NZ // 128)]
        v = jnp.concatenate(v, axis=1)
        j, q = divmod(p * ZW, 128)
        for d in range(GROUPS):
            w = pltpu.roll(v, (q - (ZC * d - HALO)) % NZ, 1)
            lo = q + (HALO if d == 0 else 0)
            hi = q + ZW - (HALO if d == GROUPS - 1 else 0)
            for part in range(2):
                a, b = max(lo - 128 * part, 0), min(hi - 128 * part, 128)
                if b <= a:
                    continue
                at = slice((j + part) * OWN, (j + part + 1) * OWN)
                keep = (lane >= a) & (lane < b)
                out_ref[d, at, :] = jnp.where(keep, w[:, 128 * part : 128 * part + 128], out_ref[d, at, :])
    top = SLAB_TILES * OWN
    lane8 = lanes((COEF_ROWS, 128))
    for i in range(2):
        p = 2 * me + i
        plane, y = p // NY, lax.rem(p, NY)
        row = (plane + flip * (1 - 2 * plane)) * NY + y
        mean = mean_ref[pl.ds(row, 1), :]
        terms = [mean * ratio_ref[pl.ds(row + k * ROWS, 1), :] for k in range(KL)]
        c = jnp.concatenate(terms + [mean] + [jnp.zeros_like(mean)] * (COEF_ROWS - KL - 1), axis=0)
        q = i * ZW
        for d in range(GROUPS):
            w = pltpu.roll(c, (q - (ZC * d - HALO)) % NZ, 1)[:, :128]
            lo = q + (HALO if d == 0 else 0)
            hi = q + ZW - (HALO if d == GROUPS - 1 else 0)
            keep = (lane8 >= lo) & (lane8 < hi)
            out_ref[d, top:, :] = jnp.where(keep, w, out_ref[d, top:, :])


def neighbours(x, masks):
    width = x.shape[-1]
    total = pltpu.roll(x, 1, 1) + pltpu.roll(x, width - 1, 1)
    total = total + (pltpu.roll(x, ZW, 1) * masks[0] + pltpu.roll(x, width - ZW, 1) * masks[1])
    return total + (pltpu.roll(x, PLANE, 1) + pltpu.roll(x, width - PLANE, 1))


def slab_fields(ref):
    return jnp.concatenate(
        [ref[:, OWN * j : OWN * (j + 1), :].reshape(MODES, 128) for j in range(SLAB_TILES)], axis=1
    )


def slab_coefs(ref):
    top = SLAB_TILES * OWN
    lane = lanes((COEF_ROWS, SLAB_LANES))
    total = jnp.zeros((COEF_ROWS, SLAB_LANES), jnp.float32)
    for m in range(GROUPS):
        part = jnp.concatenate(
            [ref[m, top:, :], jnp.zeros((COEF_ROWS, SLAB_LANES - 128), jnp.float32)], axis=1
        )
        at = 2 * ZW * m
        total = total + pltpu.roll(part, at, 1) if at else total + part
    return total


def turned(x):
    lane = lanes(x.shape)
    out = jnp.where(lane < PLANE, pltpu.roll(x, SLAB_LANES - PLANE, 1), pltpu.roll(x, PLANE, 1))
    return jnp.where(lane < SLAB, out, 0.0)


def join(dst, inner, own, outer):
    start = SLAB // 128 * 128
    shift = SLAB - start
    own = pltpu.roll(own, shift, 1)
    lane = lanes((inner.shape[0], 128))
    dst[:, :start] = inner[:, :start]
    dst[:, start : start + 128] = jnp.where(lane < shift, inner[:, start : start + 128], own[:, :128])
    dst[:, start + 128 : start + SLAB_LANES] = own[:, 128:]
    dst[:, 2 * SLAB : 2 * SLAB + SLAB_LANES] = outer


def build_links(table_ref, links, pad):
    pad[...] = jnp.zeros_like(pad)
    pad[:, :KL] = table_ref[...].astype(jnp.float32)
    rows = pad[...]
    cols = jnp.transpose(rows)
    apart = jnp.zeros((MODES, MODES), jnp.float32)
    for k in range(KL):
        apart = apart + jnp.abs(rows[:, k : k + 1] - cols[k : k + 1, :])
    near = apart == 1.0
    for k in range(KL):
        mine = rows[:, k : k + 1]
        d = mine - cols[k : k + 1, :]
        t = jnp.where(near, jnp.where(d == -1.0, 1.0, jnp.where(d == 1.0, mine + jnp.zeros_like(d), 0.0)), 0.0)
        t = t.astype(jnp.bfloat16)
        links[MODES * k : MODES * (k + 1), :MODES] = t
        links[MODES * k : MODES * (k + 1), MODES:] = t


def step_kernel(own_ref, inner_ref, outer_ref, table_ref, out_ref, u, v, pc, qc, sol, res, coef, ecoef, links, pad, mixed, masks):
    build_links(table_ref, links, pad)
    join(u, turned(slab_fields(inner_ref)), slab_fields(own_ref), turned(slab_fields(outer_ref)))
    join(coef, turned(slab_coefs(inner_ref)), slab_coefs(own_ref), turned(slab_coefs(outer_ref)))
    lane = lanes((8, WIDE))
    first = jnp.zeros((8, WIDE), jnp.bool_)
    last = jnp.zeros((8, WIDE), jnp.bool_)
    for t in range(6):
        first = first | ((lane >= PLANE * t) & (lane < PLANE * t + ZW))
        last = last | ((lane >= PLANE * (t + 1) - ZW) & (lane < PLANE * (t + 1)))
    masks[0] = jnp.where(first, 0.0, 1.0)
    masks[1] = jnp.where(last, 0.0, 1.0)
    for r in range(0, COEF_ROWS, 8):
        c = coef[r : r + 8, :]
        ecoef[r : r + 8, :] = neighbours(c, masks) + 6.0 * c

    def spread(src, dst):
        def one(r, carry):
            at = pl.ds(pl.multiple_of(8 * r, 8), 8)
            dst[at, :] = neighbours(src[at, :], masks)
            return carry

        lax.fori_loop(0, MODES // 8, one, 0)

    def mix(src, at):
        x = src[:, at]
        high = x.astype(jnp.bfloat16)
        low = (x - high.astype(jnp.float32)).astype(jnp.bfloat16)
        pair = jnp.concatenate([high, low], axis=0)
        mixed[...] = jnp.dot(links[...], pair, preferred_element_type=jnp.float32)

    def weigh(src, at, weights, r):
        rows = slice(r, r + 32)
        total = src[rows, at] * weights[KL : KL + 1, at]
        for k in range(KL):
            total = total + mixed[MODES * k + r : MODES * k + r + 32, :] * weights[k : k + 1, at]
        return total

    def operate(wide, narrow):
        spread(u, v)

        def first_pass(c, both):
            at = pl.ds(pl.multiple_of(256 * c, 256), 256)
            mix(u, at)
            for r in range(0, MODES, 32):
                pc[r : r + 32, at] = weigh(u, at, coef, r)
                if both:
                    qc[r : r + 32, at] = weigh(u, at, ecoef, r)

        def second_pass(c):
            at = pl.ds(pl.multiple_of(256 * c, 256), 256)
            mix(v, at)
            for r in range(0, MODES, 32):
                qc[r : r + 32, at] = qc[r : r + 32, at] - weigh(v, at, coef, r)

        lax.fori_loop(wide[0], wide[1], lambda c, carry: (first_pass(c, True), carry)[1], 0)
        lax.fori_loop(narrow[0], narrow[1], lambda c, carry: (second_pass(c), carry)[1], 0)

    sigma = THETA / DELTA
    rho = 1.0 / sigma
    rho_next = 1.0 / (2.0 * sigma - rho)
    valid = coef[KL : KL + 1, :] > 0.0

    operate((0, 7), (1, 6))

    def close_first(r, carry):
        at = pl.ds(pl.multiple_of(8 * r, 8), 8)
        x = u[at, :]
        au = x + 0.5 * (qc[at, :] - neighbours(pc[at, :], masks))
        begin = x * (1.0 / THETA)
        r1 = x - au * (1.0 / THETA)
        search = (rho_next * rho) * begin + (2.0 * rho_next / DELTA) * r1
        search = jnp.where(valid, search, 0.0)
        lane = lanes((8, WIDE))
        search = jnp.where((lane >= PLANE) & (lane < 5 * PLANE), search, 0.0)
        res[at, :] = r1
        sol[at, :] = begin + search
        u[at, :] = search
        return carry

    lax.fori_loop(0, MODES // 8, close_first, 0)
    operate((1, 6), (2, 5))

    def close_second(r, carry):
        at = pl.ds(pl.multiple_of(8 * r, 8), 8)
        x = u[at, :]
        au = x + 0.5 * (qc[at, :] - neighbours(pc[at, :], masks))
        res[at, :] = res[at, :] - au
        return carry

    lax.fori_loop(0, MODES // 8, close_second, 0)

    lane16 = lanes((OWN, 128))

    def ship(g, carry):
        at = pl.ds(pl.multiple_of(OWN * g, OWN), OWN)
        for f, field in enumerate((sol, res)):
            for j in range(OUT_TILES):
                tile = jnp.zeros((OWN, 128), jnp.float32)
                for i in range(128 // ZC):
                    p = j * (128 // ZC) + i
                    start = SLAB + p * ZW + HALO
                    base, off = start // 128 * 128, start % 128
                    if off + ZC <= 128:
                        w = field[at, base : base + 128]
                        w = pltpu.roll(w, (ZC * i - off) % 128, 1)
                    else:
                        w = field[at, base : base + 256]
                        w = pltpu.roll(w, (ZC * i - off) % 256, 1)[:, :128]
                    tile = w if i == 0 else jnp.where(lane16 >= ZC * i, w, tile)
                out_ref[g, (f * OUT_TILES + j) * OWN : (f * OUT_TILES + j + 1) * OWN, :] = tile
        return carry

    lax.fori_loop(0, GROUPS, ship, 0)


def unpack_kernel(in_ref, table_ref, sol_ref, res_ref, halves):
    me = lax.axis_index("mode")
    flip = 1 - lax.rem(lax.axis_index("space"), 2)
    scale = 1.0 / mode_scale(table_ref[pl.ds(pl.multiple_of(me * OWN, OWN), OWN), :])
    lane = lanes((OWN, 128))
    per = 128 // ZC
    for f, ref in enumerate((sol_ref, res_ref)):
        for p in range(ROWS):
            plane, y = p // NY, p % NY
            row = (plane + flip * (1 - 2 * plane)) * NY + y
            j, i = p // per, p % per
            for h in range(NZ // 128):
                tile = None
                for n in range(per):
                    w = in_ref[per * h + n, (f * OUT_TILES + j) * OWN : (f * OUT_TILES + j + 1) * OWN, :]
                    if n != i:
                        w = pltpu.roll(w, (ZC * (n - i)) % 128, 1)
                    tile = w if n == 0 else jnp.where(lane >= ZC * n, w, tile)
                halves[f, h, pl.ds(row, OWN, stride=ROWS), :] = tile * scale
        for h in range(NZ // 128):
            ref[:, 128 * h : 128 * h + 128] = halves[f, h]


def whole(count):
    return [pl.BlockSpec(memory_space=pltpu.VMEM)] * count


def body(load, mean_coeff, kl_ratio, chaos_table):
    params = pltpu.CompilerParams(vmem_limit_bytes=VMEM)
    f32 = jnp.float32
    send = pl.pallas_call(
        pack_kernel,
        out_shape=jax.ShapeDtypeStruct((GROUPS, SEND_ROWS, 128), f32),
        in_specs=whole(4),
        out_specs=pl.BlockSpec(memory_space=pltpu.VMEM),
        scratch_shapes=[pltpu.VMEM((NZ // 128, OWN * ROWS, 128), f32)],
        compiler_params=params,
        name="pack",
    )(load.reshape(OWN * ROWS, NZ), mean_coeff.reshape(ROWS, NZ), kl_ratio.reshape(KL * ROWS, NZ), chaos_table)
    own = lax.all_to_all(send, "mode", 0, 0, tiled=True)
    count = lax.axis_size("space")
    on_chip = [e for i in range(0, count, 2) for e in ((i, i + 1), (i + 1, i))]
    off_chip = [e for i in range(1, count - 1, 2) for e in ((i, i + 1), (i + 1, i))]
    outer = lax.ppermute(own, "space", off_chip)
    inner = lax.ppermute(own, "space", on_chip)
    back = pl.pallas_call(
        step_kernel,
        out_shape=jax.ShapeDtypeStruct((GROUPS, 2 * OUT_TILES * OWN, 128), f32),
        in_specs=whole(4),
        out_specs=pl.BlockSpec(memory_space=pltpu.VMEM),
        scratch_shapes=[pltpu.VMEM((MODES, WIDE), f32)] * 6
        + [pltpu.VMEM((COEF_ROWS, WIDE), f32)] * 2
        + [
            pltpu.VMEM((KL * MODES, 2 * MODES), jnp.bfloat16),
            pltpu.VMEM((MODES, MODES), f32),
            pltpu.VMEM((KL * MODES, 256), f32),
            pltpu.VMEM((2, 8, WIDE), f32),
        ],
        compiler_params=params,
        name="step",
    )(own, inner, outer, chaos_table)
    back = lax.all_to_all(back, "mode", 0, 0, tiled=True)
    flat = jax.ShapeDtypeStruct((OWN * ROWS, NZ), f32)
    sol, res = pl.pallas_call(
        unpack_kernel,
        out_shape=(flat, flat),
        in_specs=whole(2),
        out_specs=tuple(whole(2)),
        scratch_shapes=[pltpu.VMEM((2, NZ // 128, OWN * ROWS, 128), f32)],
        compiler_params=params,
        name="unpack",
    )(back, chaos_table)
    return sol.reshape(load.shape), res.reshape(load.shape)


def solution(mesh):
    in_specs = (
        P("mode", "space", None, None),
        P("space", None, None),
        P(None, "space", None, None),
        P(),
    )
    out_specs = (P("mode", "space", None, None), P("mode", "space", None, None))
    return jax.shard_map(body, mesh=mesh, in_specs=in_specs, out_specs=out_specs, check_vma=False)
```

time: 229 us -> 67.2 us (0.29)
  waiting for transfers between devices: 147 us -> 5.35 us
  other arithmetic: 31.6 us -> 0 us
  blocking collectives: 0 us -> 29.5 us
  Pallas kernels: 0 us -> 22.1 us
  starting transfers between devices: 21.9 us -> 6.7 us
  between operations: 14.5 us -> 0.68 us
  local copies, waits for them, and re-layouts: 8.27 us -> 2.67 us
  matrix products: 4.97 us -> 0 us
    all_gather x2 -> x0, waiting for transfers between devices: 114 us -> none  [body(): shard_piece = lax.all_gather(search, 'mode', axis=0, tiled=True)]
    all_to_all x0 -> x2, blocking collectives: none -> 29.5 us  [the longest x1 15.7 us: body(): own = lax.all_to_all(send, 'mode', 0, 0, tiled=True)]
    ppermute x6 -> x2, waiting for transfers between devices: 33 us -> 5.35 us  [the longest x1 5.35 us: body(): outer = lax.ppermute(own, 'space', off_chip)]
    pallas_call x0 -> x3, Pallas kernels: none -> 22.1 us  [the longest x1 20.4 us: body(): pl.pallas_call(step_kernel, out_shape=jax.ShapeDtypeStruct((GROUPS, 2 * O...]
    ppermute x6 -> x2, starting transfers between devices: 21.9 us -> 6.7 us  [the longest x1 6.61 us: body(): outer = lax.ppermute(own, 'space', off_chip)]
    concatenate x4 -> x0, other arithmetic: 13.2 us -> none  [the longest x3 13.1 us: with_halo(): jnp.concatenate([lax.ppermute(tail, axis, [(i, (i + 1) % count) for i in...]
    mul x10 -> x0, other arithmetic: 11.8 us -> none  [the longest x2 5.4 us: stencil(): face_x * (field_pad[..., 1:, 1:-1, 1:-1] - field_pad[..., :-1, 1:-1, 1:-1])]
    dot_general x2 -> x0, matrix products: 4.97 us -> none  [body(): jnp.dot(rows_flat, shard_piece.reshape(count, -1), precision=lax.Precisio...]
  transfers between devices with their start and end apart: 8 -> 2, of which waited for: 6 -> 1; matrix products, arithmetic and copies ran while one was open for 1% -> 0% of each run, Pallas kernels for 0% -> 0%
where the time goes in v1:
time: 67.2 us; the launch traced here: 66.9 us
  blocking collectives  29.5 us (44%)
  Pallas kernels  22.1 us (33%)
  starting transfers between devices  6.7 us (10%)
  waiting for transfers between devices  5.35 us (8%)
  local copies, waits for them, and re-layouts  2.67 us (4%)
  between operations  0.68 us (1%)
    pallas_call x1, Pallas kernels, body(): pl.pallas_call(step_kernel, out_shape=jax.ShapeDtypeStruct((GROUPS, 2 * O...  20.4 us
    all_to_all x1, blocking collectives, body(): own = lax.all_to_all(send, 'mode', 0, 0, tiled=True)  15.7 us
    all_to_all x1, blocking collectives, body(): back = lax.all_to_all(back, 'mode', 0, 0, tiled=True)  13.7 us
    ppermute x1, starting transfers between devices, body(): outer = lax.ppermute(own, 'space', off_chip)  6.61 us
    ppermute x1, waiting for transfers between devices, body(): outer = lax.ppermute(own, 'space', off_chip)  5.35 us
    unnamed x7, local copies, waits for them, and re-layouts  2.67 us
  transfers between devices with their start and end apart: 2, of which 1 were waited for; matrix products, arithmetic and copies ran while one was open for 0% of the time, Pallas kernels for 0%

profile of v1, /device:TPU:97, one launch (start us, length us, event | category | flops | bytes accessed | tf_op | source)
XLA Modules:
  0.0 66.9 jit_solution(9764430966666964582)
XLA Ops:
  0.6 0.0 copy-start.2
  0.6 0.8 %copy.6.table_ref = s32[128,10]{1,0:T(8,128)S(1)} copy(s32[128,10]{0,1:T(8,128)} %param.7) | data formatting | bytes 10240 | tf_op args[3]
  1.4 0.0 copy-done.2
  1.5 0.0 copy-start
  1.5 0.9 %copy-done = f32[16,2,8,256]{3,2,1,0:T(8,128)S(1)} copy-done((f32[16,2,8,256]{3,2,1,0:T(8,128)S(1)}, f32[16,2,8,256]{3,2,1,0:T(8,128)}, u32[]{:S(2)}) %copy-start) | copy-done | bytes 262168
  2.4 0.0 copy-start.1
  2.4 0.9 %copy-done.1 = f32[10,2,8,256]{3,2,1,0:T(8,128)S(1)} copy-done((f32[10,2,8,256]{3,2,1,0:T(8,128)S(1)}, f32[10,2,8,256]{3,2,1,0:T(8,128)}, u32[]{:S(2)}) %copy-start.1) | copy-done | bytes 163864
  3.3 0.5 pack.1
  3.8 15.7 %all_to_all.10.own_ref = f32[8,96,128]{2,1,0:T(8,128)S(1)} all-to-all(f32[8,96,128]{2,1,0:T(8,128)S(1)} %pack.1), channel_id=1, replica_groups=mesh['space'=32,'mode'=8] {'mode'}, dimensions={0} | all-to-all | bytes 786432 | tf_op jit(solution)/shard_map/all_to_all | solution.py:307
  19.5 6.6 %collective-permute-start.1 = (f32[8,96,128]{2,1,0:T(8,128)S(1)}, f32[8,96,128]{2,1,0:T(8,128)S(1)}, u32[]{:S(2)}, u32[]{:S(2)}) collective-permute-start(f32[8,96,128]{2,1,0:T(8,128)S(1)} %all_to_all.10.own_ref), channel_id=1, source_target_pairs={{8,16},{16,8},{24,32},{32,24},{40,48},{48,40},{56,64},{64,56},{72,... | collective-permute-start | bytes 1179656 | tf_op jit(solution)/shard_map/ppermute | solution.py:311
  26.1 0.1 collective-permute-start
  26.2 5.3 %collective-permute-done.1.outer_ref = f32[8,96,128]{2,1,0:T(8,128)S(1)} collective-permute-done((f32[8,96,128]{2,1,0:T(8,128)S(1)}, f32[8,96,128]{2,1,0:T(8,128)S(1)}, u32[]{:S(2)}, u32[]{:S(2)}) %collective-permute-start.1) | collective-permute-done | bytes 393248 | tf_op jit(solution)/shard_map/ppermute | solution.py:311
  31.6 0.0 collective-permute-done.inner_ref
  31.6 20.4 %step.1 = f32[8,128,128]{2,1,0:T(8,128)S(1)} custom-call(f32[8,96,128]{2,1,0:T(8,128)S(1)} %all_to_all.10.own_ref, f32[8,96,128]{2,1,0:T(8,128)S(1)} %collective-permute-done.inner_ref, f32[8,96,128]{2,1,0:T(8,128)S(1)} %collective-permute-done.1.outer_ref, s32[128,10]{1,0:T(8,128)S(1)} %copy.6.table_ref), custom_call_target="tpu_custom_call" | custom-call | tf_op jit(solution)/shard_map/step/pallas_call | solution.py:313
  52.0 13.7 %all_to_all.11.in_ref = f32[8,128,128]{2,1,0:T(8,128)S(1)} all-to-all(f32[8,128,128]{2,1,0:T(8,128)S(1)} %step.1), channel_id=1, replica_groups=mesh['space'=32,'mode'=8] {'mode'}, dimensions={0} | all-to-all | bytes 1048576 | tf_op jit(solution)/shard_map/all_to_all | solution.py:329
  65.7 1.2 %unpack.1 = (f32[256,256]{1,0:T(8,128)}, f32[256,256]{1,0:T(8,128)}) custom-call(f32[8,128,128]{2,1,0:T(8,128)S(1)} %all_to_all.11.in_ref, s32[128,10]{1,0:T(8,128)S(1)} %copy.6.table_ref), custom_call_target="tpu_custom_call" | custom-call | tf_op jit(solution)/shard_map/unpack/pallas_call | solution.py:331
Async XLA Ops:
  0.6 0.8 %copy-start.2 = (f32[2,8,256]{2,1,0:T(8,128)S(1)}, f32[2,8,256]{2,1,0:T(8,128)}, u32[]{:S(2)}) copy-start(f32[2,8,256]{2,1,0:T(8,128)} %param.5) | copy-start | bytes 49156
  1.5 1.0 %copy-start = (f32[16,2,8,256]{3,2,1,0:T(8,128)S(1)}, f32[16,2,8,256]{3,2,1,0:T(8,128)}, u32[]{:S(2)}) copy-start(f32[16,2,8,256]{3,2,1,0:T(8,128)} %param.4) | copy-start | bytes 786436
  2.4 0.9 %copy-start.1 = (f32[10,2,8,256]{3,2,1,0:T(8,128)S(1)}, f32[10,2,8,256]{3,2,1,0:T(8,128)}, u32[]{:S(2)}) copy-start(f32[10,2,8,256]{3,2,1,0:T(8,128)} %param.6) | copy-start | bytes 491524
  19.5 12.1 %collective-permute-start.1 = (f32[8,96,128]{2,1,0:T(8,128)S(1)}, f32[8,96,128]{2,1,0:T(8,128)S(1)}, u32[]{:S(2)}, u32[]{:S(2)}) collective-permute-start(f32[8,96,128]{2,1,0:T(8,128)S(1)} %all_to_all.10.own_ref), channel_id=1, source_target_pairs={{8,16},{16,8},{24,32},{32,24},{40,48},{48,40},{56,64},{64,56},{72,... | collective-permute-start | bytes 1179656 | tf_op jit(solution)/shard_map/ppermute | solution.py:311
  26.1 5.4 %collective-permute-start = (f32[8,96,128]{2,1,0:T(8,128)S(1)}, f32[8,96,128]{2,1,0:T(8,128)S(1)}, u32[]{:S(2)}, u32[]{:S(2)}) collective-permute-start(f32[8,96,128]{2,1,0:T(8,128)S(1)} %all_to_all.10.own_ref), channel_id=1, source_target_pairs={{0,8},{8,0},{16,24},{24,16},{32,40},{40,32},{48,56},{56,48},{64,72... | collective-permute-start | bytes 1179656 | tf_op jit(solution)/shard_map/ppermute | solution.py:312

commit v2 on v1

v2 whole, which is shorter than its diff:
```python
import functools

import jax
import jax.numpy as jnp
from jax import lax
from jax.experimental import pallas as pl
from jax.experimental.pallas import tpu as pltpu
from jax.sharding import PartitionSpec as P

ITERS = 2
THETA = 24.5
DELTA = 23.5
KL = 10
MODES = 128
GROUPS = 8
OWN = MODES // GROUPS
NX_OWN = 2
NY = 8
NZ = 256
ROWS = NX_OWN * NY
ZC = NZ // GROUPS
HALO = 2
PLANE = NY * ZC
CORE_TILES = NX_OWN * PLANE // 128
RIM = 2 * HALO
RIM_PLANE = NY * RIM
SPARE = NX_OWN * RIM_PLANE
SLOTS = 6
RIMS = SLOTS * PLANE
WIDE = RIMS + 256
NEAR = slice(RIMS, RIMS + 128)
TERMS = KL + 1
COEF_ROWS = 16
SEND_ROWS = (CORE_TILES + 1) * OWN
OUT_TILES = CORE_TILES
SQRT2 = 2.0**0.5
SQRT6 = 6.0**0.5
VMEM = 40 * 1024 * 1024


def lanes(shape):
    return lax.broadcasted_iota(jnp.int32, shape, len(shape) - 1)


def mode_scale(table):
    t = table
    f = jnp.where(t >= 3, SQRT6, jnp.where(t == 2, SQRT2, 1.0)).astype(jnp.float32)
    return jnp.max(f, axis=1, keepdims=True)


def turn(x, by):
    by = by % x.shape[1]
    return pltpu.roll(x, by, 1) if by else x


def rim_of(tiles, d, at, lane):
    out = None
    for side, z in enumerate((ZC * d - HALO, ZC * (d + 1))):
        if not 0 <= z < NZ:
            continue
        lo = at + HALO * side
        w = turn(tiles[z // 128], lo - z % 128)
        w = jnp.where((lane >= lo) & (lane < lo + HALO), w, 0.0)
        out = w if out is None else out + w
    return out


def pack_kernel(load_ref, mean_ref, ratio_ref, table_ref, out_ref, halves):
    me = lax.axis_index("mode")
    flip = 1 - lax.rem(lax.axis_index("space"), 2)
    scale = mode_scale(table_ref[pl.ds(pl.multiple_of(me * OWN, OWN), OWN), :])
    lane = lanes((OWN, 128))
    per = 128 // ZC
    for h in range(NZ // 128):
        halves[h] = load_ref[:, 128 * h : 128 * h + 128]

    def row_of(p):
        plane, y = p // NY, lax.rem(p, NY)
        return (plane + flip * (1 - 2 * plane)) * NY + y

    coefs = []
    for i in range(2):
        row = row_of(2 * me + i)
        mean = mean_ref[pl.ds(row, 1), :]
        terms = [mean * ratio_ref[pl.ds(row + k * ROWS, 1), :] for k in range(KL)] + [mean]
        zero = jnp.zeros_like(mean)
        low = jnp.concatenate(terms + terms[:5], axis=0)
        mid = jnp.concatenate([zero] * 11 + terms[5:10], axis=0)
        top = jnp.concatenate([zero] * 11 + terms[10:] + [zero] * 4, axis=0)
        coefs.append([(c[:, :128], c[:, 128:]) for c in (low, mid, top)])
    sub = lax.broadcasted_iota(jnp.int32, (OWN, 128), 0)
    for d in range(GROUPS):
        total = jnp.zeros((OWN, 128), jnp.float32)
        for i in range(2):
            lo = SPARE + ZC * i
            w = turn(coefs[i][0][d // per], lo - ZC * (d % per))
            total = total + jnp.where((lane >= lo) & (lane < lo + ZC) & (sub < TERMS), w, 0.0)
            for g in range(3):
                w = rim_of(coefs[i][g], d, SPARE + 2 * RIM * g + RIM * i, lane)
                total = total + jnp.where(sub >= TERMS, w, 0.0)
        out_ref[d, CORE_TILES * OWN :, :] = total

    for j in range(CORE_TILES):
        rows = []
        for i in range(per):
            row = row_of(jnp.int32(per * j + i))
            rows.append([halves[h, pl.ds(row, OWN, stride=ROWS), :] * scale for h in range(NZ // 128)])
        for d in range(GROUPS):
            tile = None
            rim = out_ref[d, CORE_TILES * OWN :, :]
            for i in range(per):
                w = turn(rows[i][d // per], ZC * (i - d % per))
                tile = w if i == 0 else jnp.where(lane >= ZC * i, w, tile)
                rim = rim + rim_of(rows[i], d, RIM * (per * j + i), lane)
            out_ref[d, OWN * j : OWN * (j + 1), :] = tile
            out_ref[d, CORE_TILES * OWN :, :] = rim


def build_links(table_ref, links, pad):
    pad[...] = jnp.zeros_like(pad)
    pad[:, :KL] = table_ref[...].astype(jnp.float32)
    rows = pad[...]
    cols = jnp.transpose(rows)
    apart = jnp.zeros((MODES, MODES), jnp.float32)
    for k in range(KL):
        apart = apart + jnp.abs(rows[:, k : k + 1] - cols[k : k + 1, :])
    near = apart == 1.0
    for k in range(KL):
        mine = rows[:, k : k + 1]
        d = mine - cols[k : k + 1, :]
        t = jnp.where(near, jnp.where(d == -1.0, 1.0, jnp.where(d == 1.0, mine + jnp.zeros_like(d), 0.0)), 0.0)
        t = t.astype(jnp.bfloat16)
        links[MODES * k : MODES * (k + 1), :MODES] = t
        links[MODES * k : MODES * (k + 1), MODES:] = t


def core_cell(l):
    return lax.div(l, ZC), lax.rem(l, ZC)


def rim_cell(l):
    zi = lax.rem(l, RIM)
    return lax.rem(lax.div(l, RIM), NY), jnp.where(zi < HALO, zi - HALO, zi + ZC - HALO)


def grid_of(shape, rows_of, cols_of):
    a = rows_of(lax.broadcasted_iota(jnp.int32, shape, 0))
    b = cols_of(lax.broadcasted_iota(jnp.int32, shape, 1))
    return sum(jnp.abs(x - y) for x, y in zip(a, b))


def build_steps(core_step, near_step, far_step):
    def put(ref, at, to, apart):
        ref[at[0] : at[0] + apart.shape[0], to : to + apart.shape[1]] = jnp.where(
            apart == 1, 1.0, 0.0
        ).astype(jnp.bfloat16)

    square = (PLANE, PLANE)
    put(core_step, (0,), 0, grid_of(square, core_cell, core_cell))
    for t in range(4):

        def rim_at(l, t=t):
            y, z = rim_cell(l)
            return y + jnp.where(lax.div(l, RIM_PLANE) == t, 0, 100), z

        put(core_step, (0,), PLANE + 128 * t, grid_of((PLANE, 128), core_cell, rim_at))
        put(near_step, (0,), PLANE * t, grid_of((128, PLANE), rim_at, core_cell))

    def near(l):
        return (lax.div(l, RIM_PLANE) + 1,) + rim_cell(l)

    def far(l):
        t = lax.div(l, RIM_PLANE)
        return (jnp.where(t == 0, 5, jnp.where(t == 1, 0, 100)),) + rim_cell(l)

    put(near_step, (0,), 4 * PLANE, grid_of((128, 128), near, near))
    put(far_step, (0,), 0, grid_of((128, 128), far, near))


def tile_of(ref, j):
    return ref[:, OWN * j : OWN * (j + 1), :].reshape(MODES, 128)


def join(dst, own_ref, inner_ref, outer_ref):
    half = PLANE // 128
    slots = ((inner_ref, 1), (inner_ref, 0), (own_ref, 0), (own_ref, 1), (outer_ref, 1), (outer_ref, 0))
    for t, (ref, plane) in enumerate(slots):
        for h in range(half):
            dst[:, PLANE * t + 128 * h : PLANE * t + 128 * (h + 1)] = tile_of(ref, half * plane + h)
    lane = lanes((MODES, 128))
    inner, own, outer = (tile_of(ref, CORE_TILES) for ref in (inner_ref, own_ref, outer_ref))
    near = jnp.where(lane < RIM_PLANE, inner, turn(own, RIM_PLANE))
    dst[:, NEAR] = jnp.where(lane < 3 * RIM_PLANE, near, turn(outer, 2 * RIM_PLANE))
    far = jnp.where(lane < RIM_PLANE, outer, inner)
    dst[:, RIMS + 128 :] = jnp.where(lane < 2 * RIM_PLANE, far, 0.0)


def slab_coefs(ref):
    lane = lanes((OWN, 128))
    raw = [ref[m, CORE_TILES * OWN :, :] for m in range(GROUPS)]
    core = [jnp.where(lane < SPARE, turn(raw[2 * j], -SPARE), raw[2 * j + 1]) for j in range(CORE_TILES)]
    lane8 = lanes((8, 128))
    parts = []
    for g in range(3):
        total = jnp.zeros((8, 128), jnp.float32)
        for m in range(GROUPS):
            lo = 2 * RIM * m
            w = turn(raw[m][8:, :], lo - SPARE - 2 * RIM * g)
            total = jnp.where((lane8 >= lo) & (lane8 < lo + 2 * RIM), w, total)
        parts.append(total[3:, :])
    rim = jnp.concatenate(parts + [jnp.zeros((1, 128), jnp.float32)], axis=0)
    return core, rim


def join_coefs(dst, own_ref, inner_ref, outer_ref):
    half = PLANE // 128
    own, inner, outer = (slab_coefs(ref) for ref in (own_ref, inner_ref, outer_ref))
    slots = ((inner, 1), (inner, 0), (own, 0), (own, 1), (outer, 1), (outer, 0))
    for t, (slab, plane) in enumerate(slots):
        for h in range(half):
            dst[:, PLANE * t + 128 * h : PLANE * t + 128 * (h + 1)] = slab[0][half * plane + h]
    lane = lanes((COEF_ROWS, 128))
    near = jnp.where(lane < RIM_PLANE, inner[1], turn(own[1], RIM_PLANE))
    dst[:, NEAR] = jnp.where(lane < 3 * RIM_PLANE, near, turn(outer[1], 2 * RIM_PLANE))
    far = jnp.where(lane < RIM_PLANE, outer[1], inner[1])
    dst[:, RIMS + 128 :] = jnp.where(lane < 2 * RIM_PLANE, far, 0.0)


def parts_of(x, count, axis=0):
    out = []
    for _ in range(count - 1):
        h = x.astype(jnp.bfloat16)
        out.append(h)
        x = x - h.astype(jnp.float32)
    return jnp.concatenate(out + [x.astype(jnp.bfloat16)], axis=axis)


def neighbours(src, slots, rims, steps, parts=2):
    core_step, near_step, far_step = steps
    rows = src.shape[0]

    def product(at, matrix):
        out = jnp.dot(parts_of(src[:, at], parts), matrix, preferred_element_type=jnp.float32)
        return sum(out[rows * i : rows * (i + 1)] for i in range(parts))

    plane = lambda t: slice(PLANE * t, PLANE * (t + 1))
    first, last = PLANE * (slots[0] - 1), PLANE * slots[-1]
    if rims:
        rim = product(NEAR, near_step[:, 4 * PLANE :]) + product(slice(RIMS + 128, WIDE), far_step[...])
    edge = product(NEAR, near_step[:, first:last])
    out = {}
    for t in slots:
        x = product(plane(t), core_step[:, :PLANE])
        if rims:
            rim = rim + product(plane(t), core_step[:, PLANE + 128 * (t - 1) : PLANE + 128 * t])
        x = x + edge[:, PLANE * t - PLANE - first : PLANE * t - first]
        out[t] = x + (src[:, plane(t - 1)] + src[:, plane(t + 1)])
    if rims:
        out["rim"] = rim
    return out


def step_kernel(own_ref, inner_ref, outer_ref, table_ref, out_ref, u, v, pc, qc, sol, res, coef, ecoef, links, pad, mixed, core_step, near_step, far_step):
    build_links(table_ref, links, pad)
    steps = (core_step, near_step, far_step)
    build_steps(*steps)
    join(u, own_ref, inner_ref, outer_ref)
    join_coefs(coef, own_ref, inner_ref, outer_ref)
    plane = lambda t: slice(PLANE * t, PLANE * (t + 1))
    for t, x in neighbours(coef, (1, 2, 3, 4), True, steps, 3).items():
        at = NEAR if t == "rim" else plane(t)
        ecoef[:, at] = x + 6.0 * coef[:, at]

    def mix(src, at):
        width = at.stop - at.start
        mixed[:, :width] = jnp.dot(links[...], parts_of(src[:, at], 2), preferred_element_type=jnp.float32)

    def weigh(src, at, weights, r):
        width = at.stop - at.start
        total = src[r : r + 32, at] * weights[KL : KL + 1, at]
        for k in range(KL):
            total = total + mixed[MODES * k + r : MODES * k + r + 32, :width] * weights[k : k + 1, at]
        return total

    def operate(only, both, slots, rims):
        for t, x in neighbours(u, slots, rims, steps).items():
            v[:, NEAR if t == "rim" else plane(t)] = x
        for at, with_q in [(a, False) for a in only] + [(a, True) for a in both]:
            mix(u, at)
            for r in range(0, MODES, 32):
                pc[r : r + 32, at] = weigh(u, at, coef, r)
                if with_q:
                    qc[r : r + 32, at] = weigh(u, at, ecoef, r)
        for at in both:
            mix(v, at)
            for r in range(0, MODES, 32):
                qc[r : r + 32, at] = qc[r : r + 32, at] - weigh(v, at, coef, r)

    sigma = THETA / DELTA
    rho = 1.0 / sigma
    rho_next = 1.0 / (2.0 * sigma - rho)

    operate([plane(0), plane(5), slice(RIMS + 128, WIDE)], [plane(t) for t in (1, 2, 3, 4)] + [NEAR], (1, 2, 3, 4), True)
    for t, around in neighbours(pc, (1, 2, 3, 4), True, steps).items():
        at = NEAR if t == "rim" else plane(t)
        x = u[:, at]
        au = x + 0.5 * (qc[:, at] - around)
        begin = x * (1.0 / THETA)
        r1 = x - au * (1.0 / THETA)
        search = (rho_next * rho) * begin + (2.0 * rho_next / DELTA) * r1
        search = jnp.where(coef[KL : KL + 1, at] > 0.0, search, 0.0)
        if t in (2, 3):
            res[:, plane(t - 2)] = r1
            sol[:, plane(t - 2)] = begin + search
        u[:, at] = search
    operate([plane(1), plane(4), NEAR], [plane(2), plane(3)], (2, 3), False)
    for t, around in neighbours(pc, (2, 3), False, steps).items():
        at = plane(t)
        res[:, plane(t - 2)] = res[:, plane(t - 2)] - (u[:, at] + 0.5 * (qc[:, at] - around))
    for f, field in enumerate((sol, res)):
        for j in range(OUT_TILES):
            n = (f * OUT_TILES + j) * OWN
            out_ref[:, n : n + OWN, :] = field[:, 128 * j : 128 * (j + 1)].reshape(GROUPS, OWN, 128)


def unpack_kernel(in_ref, table_ref, sol_ref, res_ref, halves):
    me = lax.axis_index("mode")
    flip = 1 - lax.rem(lax.axis_index("space"), 2)
    scale = 1.0 / mode_scale(table_ref[pl.ds(pl.multiple_of(me * OWN, OWN), OWN), :])
    lane = lanes((OWN, 128))
    per = 128 // ZC
    for f, ref in enumerate((sol_ref, res_ref)):
        for p in range(ROWS):
            plane, y = p // NY, p % NY
            row = (plane + flip * (1 - 2 * plane)) * NY + y
            j, i = p // per, p % per
            for h in range(NZ // 128):
                tile = None
                for n in range(per):
                    w = in_ref[per * h + n, (f * OUT_TILES + j) * OWN : (f * OUT_TILES + j + 1) * OWN, :]
                    if n != i:
                        w = pltpu.roll(w, (ZC * (n - i)) % 128, 1)
                    tile = w if n == 0 else jnp.where(lane >= ZC * n, w, tile)
                halves[f, h, pl.ds(row, OWN, stride=ROWS), :] = tile * scale
        for h in range(NZ // 128):
            ref[:, 128 * h : 128 * h + 128] = halves[f, h]


def whole(count):
    return [pl.BlockSpec(memory_space=pltpu.VMEM)] * count


def body(load, mean_coeff, kl_ratio, chaos_table):
    params = pltpu.CompilerParams(vmem_limit_bytes=VMEM)
    f32 = jnp.float32
    send = pl.pallas_call(
        pack_kernel,
        out_shape=jax.ShapeDtypeStruct((GROUPS, SEND_ROWS, 128), f32),
        in_specs=whole(4),
        out_specs=pl.BlockSpec(memory_space=pltpu.VMEM),
        scratch_shapes=[pltpu.VMEM((NZ // 128, OWN * ROWS, 128), f32)],
        compiler_params=params,
        name="pack",
    )(load.reshape(OWN * ROWS, NZ), mean_coeff.reshape(ROWS, NZ), kl_ratio.reshape(KL * ROWS, NZ), chaos_table)
    own = lax.all_to_all(send, "mode", 0, 0, tiled=True)
    count = lax.axis_size("space")
    on_chip = [e for i in range(0, count, 2) for e in ((i, i + 1), (i + 1, i))]
    off_chip = [e for i in range(1, count - 1, 2) for e in ((i, i + 1), (i + 1, i))]
    outer = lax.ppermute(own, "space", off_chip)
    inner = lax.ppermute(own, "space", on_chip)
    back = pl.pallas_call(
        step_kernel,
        out_shape=jax.ShapeDtypeStruct((GROUPS, 2 * OUT_TILES * OWN, 128), f32),
        in_specs=whole(4),
        out_specs=pl.BlockSpec(memory_space=pltpu.VMEM),
        scratch_shapes=[pltpu.VMEM((MODES, WIDE), f32)] * 4
        + [pltpu.VMEM((MODES, 2 * PLANE), f32)] * 2
        + [pltpu.VMEM((COEF_ROWS, WIDE), f32)] * 2
        + [
            pltpu.VMEM((KL * MODES, 2 * MODES), jnp.bfloat16),
            pltpu.VMEM((MODES, MODES), f32),
            pltpu.VMEM((KL * MODES, 256), f32),
            pltpu.VMEM((PLANE, PLANE + 4 * 128), jnp.bfloat16),
            pltpu.VMEM((128, 4 * PLANE + 128), jnp.bfloat16),
            pltpu.VMEM((128, 128), jnp.bfloat16),
        ],
        compiler_params=params,
        name="step",
    )(own, inner, outer, chaos_table)
    back = lax.all_to_all(back, "mode", 0, 0, tiled=True)
    flat = jax.ShapeDtypeStruct((OWN * ROWS, NZ), f32)
    sol, res = pl.pallas_call(
        unpack_kernel,
        out_shape=(flat, flat),
        in_specs=whole(2),
        out_specs=tuple(whole(2)),
        scratch_shapes=[pltpu.VMEM((2, NZ // 128, OWN * ROWS, 128), f32)],
        compiler_params=params,
        name="unpack",
    )(back, chaos_table)
    return sol.reshape(load.shape), res.reshape(load.shape)


def solution(mesh):
    in_specs = (
        P("mode", "space", None, None),
        P("space", None, None),
        P(None, "space", None, None),
        P(),
    )
    out_specs = (P("mode", "space", None, None), P("mode", "space", None, None))
    return jax.shard_map(body, mesh=mesh, in_specs=in_specs, out_specs=out_specs, check_vma=False)
```

time: 67.2 us -> 51.9 us (0.77)
  Pallas kernels: 22.1 us -> 8.19 us
  blocking collectives: 29.5 us -> 28.4 us
  waiting for transfers between devices: 5.35 us -> 4.65 us
    pallas_call x1, Pallas kernels: 20.4 us -> 6.3 us  [body(): pl.pallas_call(step_kernel, out_shape=jax.ShapeDtypeStruct((GROUPS, 2 * O...]
    all_to_all x1, blocking collectives: 15.7 us -> 14.7 us  [body(): own = lax.all_to_all(send, 'mode', 0, 0, tiled=True)]
    ppermute x1, waiting for transfers between devices: 5.35 us -> 4.64 us  [body(): outer = lax.ppermute(own, 'space', off_chip)]
where the time goes in v2:
time: 51.9 us; the launch traced here: 51.6 us
  blocking collectives  28.4 us (55%)
  Pallas kernels  8.19 us (16%)
  starting transfers between devices  7 us (13%)
  waiting for transfers between devices  4.65 us (9%)
  local copies, waits for them, and re-layouts  2.67 us (5%)
  between operations  0.68 us (1%)
    all_to_all x1, blocking collectives, body(): own = lax.all_to_all(send, 'mode', 0, 0, tiled=True)  14.7 us
    all_to_all x1, blocking collectives, body(): back = lax.all_to_all(back, 'mode', 0, 0, tiled=True)  13.7 us
    ppermute x1, starting transfers between devices, body(): outer = lax.ppermute(own, 'space', off_chip)  6.91 us
    pallas_call x1, Pallas kernels, body(): pl.pallas_call(step_kernel, out_shape=jax.ShapeDtypeStruct((GROUPS, 2 * O...  6.3 us
    ppermute x1, waiting for transfers between devices, body(): outer = lax.ppermute(own, 'space', off_chip)  4.64 us
    unnamed x7, local copies, waits for them, and re-layouts  2.67 us
    pallas_call x1, Pallas kernels, body(): pl.pallas_call(unpack_kernel, out_shape=(flat, flat), in_specs=whole(2),...  1.23 us
  transfers between devices with their start and end apart: 2, of which 1 were waited for; matrix products, arithmetic and copies ran while one was open for 0% of the time, Pallas kernels for 0%

profile of v2, /device:TPU:97, one launch (start us, length us, event | category | flops | bytes accessed | tf_op | source)
XLA Modules:
  0.0 51.6 jit_solution(11320316641673266409)
XLA Ops:
  0.6 0.0 copy-start.2
  0.6 0.8 %copy.6.table_ref = s32[128,10]{1,0:T(8,128)S(1)} copy(s32[128,10]{0,1:T(8,128)} %param.7) | data formatting | bytes 10240 | tf_op args[3]
  1.4 0.0 copy-done.2
  1.5 0.0 copy-start
  1.5 0.9 %copy-done = f32[16,2,8,256]{3,2,1,0:T(8,128)S(1)} copy-done((f32[16,2,8,256]{3,2,1,0:T(8,128)S(1)}, f32[16,2,8,256]{3,2,1,0:T(8,128)}, u32[]{:S(2)}) %copy-start) | copy-done | bytes 262168
  2.4 0.0 copy-start.1
  2.4 0.9 %copy-done.1 = f32[10,2,8,256]{3,2,1,0:T(8,128)S(1)} copy-done((f32[10,2,8,256]{3,2,1,0:T(8,128)S(1)}, f32[10,2,8,256]{3,2,1,0:T(8,128)}, u32[]{:S(2)}) %copy-start.1) | copy-done | bytes 163864
  3.3 0.7 %pack.1 = f32[8,80,128]{2,1,0:T(8,128)S(1)} custom-call(f32[256,256]{1,0:T(8,128)S(1)} %bitcast.5, f32[16,256]{1,0:T(8,128)S(1)} %bitcast.7, f32[160,256]{1,0:T(8,128)S(1)} %bitcast.6, s32[128,10]{1,0:T(8,128)S(1)} %copy.6.table_ref), custom_call_target="tpu_custom_call" | custom-call | tf_op jit(solution)/shard_map/pack/pallas_call | solution.py:356
  4.0 14.7 %all_to_all.10.own_ref = f32[8,80,128]{2,1,0:T(8,128)S(1)} all-to-all(f32[8,80,128]{2,1,0:T(8,128)S(1)} %pack.1), channel_id=1, replica_groups=mesh['space'=32,'mode'=8] {'mode'}, dimensions={0} | all-to-all | bytes 655360 | tf_op jit(solution)/shard_map/all_to_all | solution.py:365
  18.7 6.9 %collective-permute-start.1 = (f32[8,80,128]{2,1,0:T(8,128)S(1)}, f32[8,80,128]{2,1,0:T(8,128)S(1)}, u32[]{:S(2)}, u32[]{:S(2)}) collective-permute-start(f32[8,80,128]{2,1,0:T(8,128)S(1)} %all_to_all.10.own_ref), channel_id=1, source_target_pairs={{8,16},{16,8},{24,32},{32,24},{40,48},{48,40},{56,64},{64,56},{72,... | collective-permute-start | bytes 983048 | tf_op jit(solution)/shard_map/ppermute | solution.py:369
  25.6 0.1 collective-permute-start
  25.7 4.6 %collective-permute-done.1.outer_ref = f32[8,80,128]{2,1,0:T(8,128)S(1)} collective-permute-done((f32[8,80,128]{2,1,0:T(8,128)S(1)}, f32[8,80,128]{2,1,0:T(8,128)S(1)}, u32[]{:S(2)}, u32[]{:S(2)}) %collective-permute-start.1) | collective-permute-done | bytes 327712 | tf_op jit(solution)/shard_map/ppermute | solution.py:369
  30.4 0.0 collective-permute-done.inner_ref
  30.4 6.3 %step.1 = f32[8,128,128]{2,1,0:T(8,128)S(1)} custom-call(f32[8,80,128]{2,1,0:T(8,128)S(1)} %all_to_all.10.own_ref, f32[8,80,128]{2,1,0:T(8,128)S(1)} %collective-permute-done.inner_ref, f32[8,80,128]{2,1,0:T(8,128)S(1)} %collective-permute-done.1.outer_ref, s32[128,10]{1,0:T(8,128)S(1)} %copy.6.table_ref), custom_call_target="tpu_custom_call" | custom-call | tf_op jit(solution)/shard_map/step/pallas_call | solution.py:371
  36.7 13.7 %all_to_all.11.in_ref = f32[8,128,128]{2,1,0:T(8,128)S(1)} all-to-all(f32[8,128,128]{2,1,0:T(8,128)S(1)} %step.1), channel_id=1, replica_groups=mesh['space'=32,'mode'=8] {'mode'}, dimensions={0} | all-to-all | bytes 1048576 | tf_op jit(solution)/shard_map/all_to_all | solution.py:390
  50.4 1.2 %unpack.1 = (f32[256,256]{1,0:T(8,128)}, f32[256,256]{1,0:T(8,128)}) custom-call(f32[8,128,128]{2,1,0:T(8,128)S(1)} %all_to_all.11.in_ref, s32[128,10]{1,0:T(8,128)S(1)} %copy.6.table_ref), custom_call_target="tpu_custom_call" | custom-call | tf_op jit(solution)/shard_map/unpack/pallas_call | solution.py:392
Async XLA Ops:
  0.6 0.8 %copy-start.2 = (f32[2,8,256]{2,1,0:T(8,128)S(1)}, f32[2,8,256]{2,1,0:T(8,128)}, u32[]{:S(2)}) copy-start(f32[2,8,256]{2,1,0:T(8,128)} %param.5) | copy-start | bytes 49156
  1.5 1.0 %copy-start = (f32[16,2,8,256]{3,2,1,0:T(8,128)S(1)}, f32[16,2,8,256]{3,2,1,0:T(8,128)}, u32[]{:S(2)}) copy-start(f32[16,2,8,256]{3,2,1,0:T(8,128)} %param.4) | copy-start | bytes 786436
  2.4 0.9 %copy-start.1 = (f32[10,2,8,256]{3,2,1,0:T(8,128)S(1)}, f32[10,2,8,256]{3,2,1,0:T(8,128)}, u32[]{:S(2)}) copy-start(f32[10,2,8,256]{3,2,1,0:T(8,128)} %param.6) | copy-start | bytes 491524
  18.7 11.7 %collective-permute-start.1 = (f32[8,80,128]{2,1,0:T(8,128)S(1)}, f32[8,80,128]{2,1,0:T(8,128)S(1)}, u32[]{:S(2)}, u32[]{:S(2)}) collective-permute-start(f32[8,80,128]{2,1,0:T(8,128)S(1)} %all_to_all.10.own_ref), channel_id=1, source_target_pairs={{8,16},{16,8},{24,32},{32,24},{40,48},{48,40},{56,64},{64,56},{72,... | collective-permute-start | bytes 983048 | tf_op jit(solution)/shard_map/ppermute | solution.py:369
  25.6 4.7 %collective-permute-start = (f32[8,80,128]{2,1,0:T(8,128)S(1)}, f32[8,80,128]{2,1,0:T(8,128)S(1)}, u32[]{:S(2)}, u32[]{:S(2)}) collective-permute-start(f32[8,80,128]{2,1,0:T(8,128)S(1)} %all_to_all.10.own_ref), channel_id=1, source_target_pairs={{0,8},{8,0},{16,24},{24,16},{32,40},{40,32},{48,56},{56,48},{64,72... | collective-permute-start | bytes 983048 | tf_op jit(solution)/shard_map/ppermute | solution.py:370

commit v3 on v2

v3 whole, which is shorter than its diff:
```python
import functools

import jax
import jax.numpy as jnp
from jax import lax
from jax.experimental import pallas as pl
from jax.experimental.pallas import tpu as pltpu
from jax.sharding import PartitionSpec as P

ITERS = 2
THETA = 24.5
DELTA = 23.5
KL = 10
MODES = 128
GROUPS = 8
OWN = MODES // GROUPS
NX_OWN = 2
NY = 8
NZ = 256
ROWS = NX_OWN * NY
ZC = NZ // GROUPS
HALO = 2
PLANE = NY * ZC
CORE_TILES = NX_OWN * PLANE // 128
RIM = 2 * HALO
RIM_PLANE = NY * RIM
SPARE = NX_OWN * RIM_PLANE
TERMS = KL + 1
COEF_ROWS = 16
SEND_ROWS = (CORE_TILES + 1) * OWN
OUT_TILES = CORE_TILES
BLOCK = 32
SQRT2 = 2.0**0.5
SQRT6 = 6.0**0.5
VMEM = 40 * 1024 * 1024
PACK_VMEM = 62 * 1024 * 1024


def lanes(shape):
    return lax.broadcasted_iota(jnp.int32, shape, len(shape) - 1)


def mode_scale(t):
    f = jnp.where(t >= 3, SQRT6, jnp.where(t == 2, SQRT2, 1.0)).astype(jnp.float32)
    f = jnp.max(f, axis=0, keepdims=True)
    shape = (OWN, MODES)
    mine = lanes(shape) == lax.broadcasted_iota(jnp.int32, shape, 0) + OWN * lax.axis_index("mode")
    return jnp.sum(jnp.where(mine, f, 0.0), axis=1, keepdims=True)


def turn(x, by):
    by = by % x.shape[1]
    return pltpu.roll(x, by, 1) if by else x


def edges_of(tiles, at, lane):
    out = []
    for e in range(GROUPS + 1):
        z = ZC * e - HALO
        total = None
        for n, tile in enumerate(tiles):
            lo, hi = max(z, 128 * n), min(z + RIM, 128 * (n + 1))
            if lo >= hi:
                continue
            w = turn(tile, at - z)
            w = jnp.where((lane >= at + lo - z) & (lane < at + hi - z), w, 0.0)
            total = w if total is None else total + w
        out.append(total)
    return out


def pack_kernel(load_hbm, mean_hbm, ratio_hbm, table_hbm, out_ref, halves, mean_ref, ratio_ref, table_ref, sems):
    copies = [
        pltpu.make_async_copy(ratio_hbm, ratio_ref, sems.at[0]),
        pltpu.make_async_copy(mean_hbm, mean_ref, sems.at[1]),
        pltpu.make_async_copy(table_hbm, table_ref, sems.at[2]),
    ] + [
        pltpu.make_async_copy(load_hbm.at[:, pl.ds(128 * h, 128)], halves.at[h], sems.at[3 + h])
        for h in range(NZ // 128)
    ]
    for copy in copies:
        copy.start()
    me = lax.axis_index("mode")
    flip = 1 - lax.rem(lax.axis_index("space"), 2)
    lane = lanes((OWN, 128))
    per = 128 // ZC
    for copy in copies:
        copy.wait()
    scale = mode_scale(table_ref[...])

    def row_of(p):
        plane, y = p // NY, lax.rem(p, NY)
        return (plane + flip * (1 - 2 * plane)) * NY + y

    coefs = []
    for i in range(2):
        row = row_of(2 * me + i)
        mean = mean_ref[pl.ds(row, 1), :]
        terms = [mean * ratio_ref[pl.ds(row + k * ROWS, 1), :] for k in range(KL)] + [mean]
        zero = jnp.zeros_like(mean)
        low = jnp.concatenate(terms + terms[:5], axis=0)
        mid = jnp.concatenate([zero] * 11 + terms[5:10], axis=0)
        top = jnp.concatenate([zero] * 11 + terms[10:] + [zero] * 4, axis=0)
        coefs.append([(c[:, :128], c[:, 128:]) for c in (low, mid, top)])
    lane8 = lanes((8, 128))
    sub8 = lax.broadcasted_iota(jnp.int32, (8, 128), 0)
    first = lax.rem(lane8, RIM) < HALO
    borders = [jnp.zeros((8, 128), jnp.float32)] * (GROUPS + 1)
    for i in range(2):
        for g in range(3):
            tiles = [c[8:, :] for c in coefs[i][g]]
            more = edges_of(tiles, SPARE + 2 * RIM * g + RIM * i, lane8)
            borders = [x + y for x, y in zip(borders, more)]
    base = []
    for d in range(GROUPS):
        own_cells = []
        for i in range(2):
            w = turn(coefs[i][0][d // per], SPARE + ZC * i - ZC * (d % per))
            own_cells.append(jnp.where((lane >= SPARE + ZC * i) & (lane < SPARE + ZC * (i + 1)), w, 0.0))
        own_cells = own_cells[0] + own_cells[1]
        low = jnp.where(sub8 < TERMS - 8, own_cells[8:, :], jnp.where(first, borders[d], borders[d + 1]))
        base.append(jnp.concatenate([own_cells[:8, :], low], axis=0))

    first = lax.rem(lane, RIM) < HALO
    borders = [jnp.zeros((OWN, 128), jnp.float32)] * (GROUPS + 1)
    for j in range(CORE_TILES):
        rows = []
        for i in range(per):
            row = row_of(jnp.int32(per * j + i))
            rows.append([halves[h, pl.ds(row, OWN, stride=ROWS), :] * scale for h in range(NZ // 128)])
            more = edges_of(rows[i], RIM * (per * j + i), lane)
            borders = [x + y for x, y in zip(borders, more)]
        for d in range(GROUPS):
            tile = None
            for i in range(per):
                w = turn(rows[i][d // per], ZC * (i - d % per))
                tile = w if i == 0 else jnp.where(lane >= ZC * i, w, tile)
            out_ref[d, OWN * j : OWN * (j + 1), :] = tile
    for d in range(GROUPS):
        out_ref[d, CORE_TILES * OWN :, :] = base[d] + jnp.where(first, borders[d], borders[d + 1])


def build_links(table_ref, links, pad):
    pad[...] = jnp.zeros_like(pad)
    pad[:KL, :] = table_ref[...].astype(jnp.float32)
    cols = pad[...]
    rows = jnp.transpose(cols)
    apart = jnp.zeros((MODES, MODES), jnp.float32)
    for k in range(KL):
        apart = apart + jnp.abs(rows[:, k : k + 1] - cols[k : k + 1, :])
    near = apart == 1.0
    for k in range(KL):
        mine = rows[:, k : k + 1]
        d = mine - cols[k : k + 1, :]
        t = jnp.where(near, jnp.where(d == -1.0, 1.0, jnp.where(d == 1.0, mine + jnp.zeros_like(d), 0.0)), 0.0)
        t = t.astype(jnp.bfloat16)
        for b in range(MODES // BLOCK):
            at = (KL * b + k) * BLOCK
            links[at : at + BLOCK, :MODES] = t[BLOCK * b : BLOCK * (b + 1), :]
            links[at : at + BLOCK, MODES:] = t[BLOCK * b : BLOCK * (b + 1), :]


def core_cell(l):
    return lax.div(l, ZC), lax.rem(l, ZC)


def rim_cell(l):
    zi = lax.rem(l, RIM)
    return lax.rem(lax.div(l, RIM), NY), jnp.where(zi < HALO, zi - HALO, zi + ZC - HALO)


def grid_of(shape, rows_of, cols_of):
    a = rows_of(lax.broadcasted_iota(jnp.int32, shape, 0))
    b = cols_of(lax.broadcasted_iota(jnp.int32, shape, 1))
    return sum(jnp.abs(x - y) for x, y in zip(a, b))


def build_steps(core_step, near_step, far_step):
    def fill(ref, at, to, apart):
        ref[at[0] : at[0] + apart.shape[0], to : to + apart.shape[1]] = jnp.where(
            apart == 1, 1.0, 0.0
        ).astype(jnp.bfloat16)

    square = (PLANE, PLANE)
    fill(core_step, (0,), 0, grid_of(square, core_cell, core_cell))
    for t in range(4):

        def rim_at(l, t=t):
            y, z = rim_cell(l)
            return y + jnp.where(lax.div(l, RIM_PLANE) == t, 0, 100), z

        fill(core_step, (0,), PLANE + 128 * t, grid_of((PLANE, 128), core_cell, rim_at))
        fill(near_step, (0,), PLANE * t, grid_of((128, PLANE), rim_at, core_cell))

    def near(l):
        return (lax.div(l, RIM_PLANE) + 1,) + rim_cell(l)

    def far(l):
        t = lax.div(l, RIM_PLANE)
        return (jnp.where(t == 0, 5, jnp.where(t == 1, 0, 100)),) + rim_cell(l)

    fill(near_step, (0,), 4 * PLANE, grid_of((128, 128), near, near))
    fill(far_step, (0,), 0, grid_of((128, 128), far, near))


def tile_of(ref, j):
    return ref[:, OWN * j : OWN * (j + 1), :].reshape(MODES, 128)


def plane_of(ref, plane):
    half = PLANE // 128
    return jnp.concatenate([tile_of(ref, half * plane + h) for h in range(half)], axis=1)


def near_of(inner, own, outer):
    lane = lanes(own.shape)
    out = jnp.where((lane >= RIM_PLANE) & (lane < 3 * RIM_PLANE), turn(own, RIM_PLANE), 0.0)
    if inner is not None:
        out = jnp.where(lane < RIM_PLANE, inner, out)
    if outer is not None:
        out = jnp.where(lane < 3 * RIM_PLANE, out, turn(outer, 2 * RIM_PLANE))
    return out


def far_of(inner, outer):
    lane = lanes(inner.shape)
    return jnp.where(lane < RIM_PLANE, outer, jnp.where(lane < 2 * RIM_PLANE, inner, 0.0))


def slab_coefs(ref):
    lane = lanes((OWN, 128))
    raw = [ref[m, CORE_TILES * OWN :, :] for m in range(GROUPS)]
    core = [jnp.where(lane < SPARE, turn(raw[2 * j], -SPARE), raw[2 * j + 1]) for j in range(CORE_TILES)]
    lane8 = lanes((8, 128))
    parts = []
    for g in range(3):
        total = jnp.zeros((8, 128), jnp.float32)
        for m in range(GROUPS):
            lo = 2 * RIM * m
            w = turn(raw[m][8:, :], lo - SPARE - 2 * RIM * g)
            total = jnp.where((lane8 >= lo) & (lane8 < lo + 2 * RIM), w, total)
        parts.append(total[3:, :])
    rim = jnp.concatenate(parts + [jnp.zeros((1, 128), jnp.float32)], axis=0)
    return jnp.concatenate(core + [rim], axis=1)


def parts_of(x, count, axis=0):
    out = []
    for _ in range(count - 1):
        h = x.astype(jnp.bfloat16)
        out.append(h)
        x = x - h.astype(jnp.float32)
    return jnp.concatenate(out + [x.astype(jnp.bfloat16)], axis=axis)


def get(field, t):
    part = field[t]
    return part() if callable(part) else part[0][:, part[1]]


def put(field, t, x):
    ref, at = field[t]
    ref[:, at] = x


def product(x, matrix, parts=2):
    out = jnp.dot(parts_of(x, parts), matrix, preferred_element_type=jnp.float32)
    return sum(out[x.shape[0] * i : x.shape[0] * (i + 1)] for i in range(parts))


def neighbours(src, slots, rims, steps, parts=2, along_x=True):
    core_step, near_step, far_step = steps
    out = {}
    for t in slots:
        x = product(get(src, t), core_step[:, :PLANE], parts)
        x = x + product(get(src, "near"), near_step[:, PLANE * (t - 1) : PLANE * t], parts)
        out[t] = x + (get(src, t - 1) + get(src, t + 1)) if along_x else x
    if rims:
        out["near"] = product(get(src, "near"), near_step[:, 4 * PLANE :], parts)
        out["near"] += product(get(src, "far"), far_step[...], parts)
        for t in (1, 2, 3, 4):
            out["near"] += product(get(src, t), core_step[:, PLANE + 128 * (t - 1) : PLANE + 128 * t], parts)
    return out


def mix(links, x, sums):
    width = x.shape[1]
    pair = parts_of(x, 2)
    rows_of = [
        [jnp.broadcast_to(ref[k : k + 1, at], (8, width)) for k in range(TERMS)] for (ref, at), _ in sums
    ]
    split = lambda x: x.reshape(BLOCK // 8, 8, width)
    for b in range(MODES // BLOCK):
        rows = slice(BLOCK * b, BLOCK * (b + 1))
        mixed = jnp.dot(
            links[KL * BLOCK * b : KL * BLOCK * (b + 1), :], pair, preferred_element_type=jnp.float32
        )
        here = split(x[rows, :])
        totals = [here * weights[KL][None] for weights in rows_of]
        for k in range(KL):
            part = split(mixed[BLOCK * k : BLOCK * (k + 1), :])
            totals = [total + part * weights[k][None] for total, weights in zip(totals, rows_of)]
        for total, (_, finish) in zip(totals, sums):
            finish(rows, total.reshape(BLOCK, width))


def into(field, t, sign=0):
    ref, at = field[t]

    def finish(rows, total):
        if sign:
            total = ref[rows, at] + total if sign > 0 else ref[rows, at] - total
        ref[rows, at] = total

    return finish


def prep_kernel(own_ref, table_ref, coef, pc, links, core_step, near_step, far_step, pad):
    build_links(table_ref, links, pad)
    build_steps(core_step, near_step, far_step)
    coef[...] = slab_coefs(own_ref)
    for plane in range(2):
        at = slice(PLANE * plane, PLANE * (plane + 1))
        mix(links, plane_of(own_ref, plane), [((coef, at), into({plane: (pc, at)}, plane))])


def lo(n):
    return slice(PLANE * n, PLANE * (n + 1))


NEAR, FAR = slice(0, 128), slice(128, 256)
TAIL = slice(2 * PLANE, 2 * PLANE + 128)
FAR_TAIL = slice(2 * PLANE + 128, 2 * PLANE + 256)
NEAR_TAIL = slice(4 * PLANE, 4 * PLANE + 128)


def between_kernel(own_ref, inner_ref, coef_own, pc_own, links, core_step, near_step, far_step, coef_inner, ecoef, pc, qc, near):
    steps = (core_step, near_step, far_step)
    uf = {0: functools.partial(plane_of, inner_ref, 1), 1: functools.partial(plane_of, inner_ref, 0)}
    uf.update({2: functools.partial(plane_of, own_ref, 0), 3: functools.partial(plane_of, own_ref, 1)})
    near[...] = near_of(tile_of(inner_ref, CORE_TILES), tile_of(own_ref, CORE_TILES), None)
    uf["near"] = (near, NEAR)
    coef_inner[...] = slab_coefs(inner_ref)
    cf = {0: (coef_inner, lo(1)), 1: (coef_inner, lo(0)), 2: (coef_own, lo(0)), 3: (coef_own, lo(1))}
    cf["near"] = lambda: near_of(coef_inner[:, TAIL], coef_own[:, TAIL], None)
    ef = {t: (ecoef, lo(t - 1)) for t in (1, 2)}
    for t, x in neighbours(cf, (1, 2), False, steps, 3).items():
        put(ef, t, x + 6.0 * get(cf, t))
    pf = {t: (pc, lo(t)) for t in (0, 1)}
    qf = {t: (qc, lo(t - 1)) for t in (1, 2)}
    mix(links, get(uf, 1), [(cf[1], into(pf, 1)), (ef[1], into(qf, 1))])
    mix(links, get(uf, 2), [(ef[2], into(qf, 2))])
    mix(links, get(uf, 0), [(cf[0], into(pf, 0))])
    for t, x in neighbours(uf, (1, 2), False, steps).items():
        mix(links, x, [(cf[t], into(qf, t, -1))])


def step_kernel(own_ref, inner_ref, outer_ref, coef_own, pc_own, links, core_step, near_step, far_step, coef_inner, ecoef_known, pc_known, qc_known, out_ref, rims, coef_outer, coef_rims, ecoef, pc, qc, search, pc2, qc2, sol, res):
    steps = (core_step, near_step, far_step)
    uf = {}
    for t, (ref, plane) in enumerate(((inner_ref, 1), (inner_ref, 0), (own_ref, 0), (own_ref, 1), (outer_ref, 1), (outer_ref, 0))):
        uf[t] = functools.partial(plane_of, ref, plane)
    inner, own, outer = (tile_of(ref, CORE_TILES) for ref in (inner_ref, own_ref, outer_ref))
    rims[:, NEAR] = near_of(inner, own, outer)
    rims[:, FAR] = far_of(inner, outer)
    uf.update(near=(rims, NEAR), far=(rims, FAR))

    coef_outer[...] = slab_coefs(outer_ref)
    coef_rims[:, NEAR] = near_of(coef_inner[:, TAIL], coef_own[:, TAIL], coef_outer[:, TAIL])
    coef_rims[:, FAR] = far_of(coef_inner[:, TAIL], coef_outer[:, TAIL])
    cf = {0: (coef_inner, lo(1)), 1: (coef_inner, lo(0)), 2: (coef_own, lo(0)), 3: (coef_own, lo(1))}
    cf.update({4: (coef_outer, lo(1)), 5: (coef_outer, lo(0)), "near": (coef_rims, NEAR), "far": (coef_rims, FAR)})
    ef = {t: (ecoef_known, lo(t - 1)) for t in (1, 2)}
    ef.update({3: (ecoef, lo(0)), 4: (ecoef, lo(1)), "near": (ecoef, TAIL)})
    for t, x in neighbours(cf, (3, 4), True, steps, 3).items():
        put(ef, t, x + 6.0 * get(cf, t))
    ecoef[:, FAR_TAIL] = jnp.zeros((COEF_ROWS, 128), jnp.float32)

    pf = {0: (pc_known, lo(0)), 1: (pc_known, lo(1)), 2: (pc_own, lo(0)), 3: (pc_own, lo(1)), 4: (pc, lo(0)), 5: (pc, lo(1))}
    pf.update(near=(pc, TAIL), far=(pc, FAR_TAIL))
    qf = {1: (qc_known, lo(0)), 2: (qc_known, lo(1)), 3: (qc, lo(0)), 4: (qc, lo(1)), "near": (qc, TAIL)}
    all_rims = slice(TAIL.start, FAR_TAIL.stop)

    mix(links, get(uf, 3), [(ef[3], into(qf, 3))])
    mix(links, get(uf, 4), [(cf[4], into(pf, 4)), (ef[4], into(qf, 4))])
    mix(links, get(uf, 5), [(cf[5], into(pf, 5))])
    rim_sums = [((coef_rims, slice(0, 256)), pc), ((ecoef, all_rims), qc)]
    mix(links, rims[...], [(weights, into({0: (ref, all_rims)}, 0)) for weights, ref in rim_sums])
    for t, x in neighbours(uf, (3, 4), True, steps).items():
        mix(links, x, [(cf[t], into(qf, t, -1))])

    sigma = THETA / DELTA
    rho = 1.0 / sigma
    rho_next = 1.0 / (2.0 * sigma - rho)
    sf = {t: (search, lo(t - 1)) for t in (1, 2, 3, 4)}
    sf["near"] = (search, NEAR_TAIL)
    for t, x in neighbours(pf, (1, 2, 3, 4), True, steps).items():
        start = get(uf, t)
        au = start + 0.5 * (get(qf, t) - x)
        begin = start * (1.0 / THETA)
        r1 = start - au * (1.0 / THETA)
        new = (rho_next * rho) * begin + (2.0 * rho_next / DELTA) * r1
        new = jnp.where(cf[t][0][KL : KL + 1, cf[t][1]] > 0.0, new, 0.0)
        if t in (2, 3):
            res[:, lo(t - 2)] = r1
            sol[:, lo(t - 2)] = begin + new
        put(sf, t, new)

    pf = {t: (pc2, at) for t, (_, at) in sf.items()}
    qf = {t: (qc2, lo(t - 2)) for t in (2, 3)}
    for t in (2, 3, 1, 4, "near"):
        sums = [(cf[t], into(pf, t))]
        if t in (2, 3):
            sums.append((ef[t], into(qf, t)))
        mix(links, get(sf, t), sums)
    for t, x in neighbours(sf, (2, 3), False, steps).items():
        mix(links, x, [(cf[t], into(qf, t, -1))])
    for t, x in neighbours(pf, (2, 3), False, steps).items():
        res[:, lo(t - 2)] = res[:, lo(t - 2)] - (get(sf, t) + 0.5 * (get(qf, t) - x))
    for f, field in enumerate((sol, res)):
        for j in range(OUT_TILES):
            n = (f * OUT_TILES + j) * OWN
            out_ref[:, n : n + OWN, :] = field[:, 128 * j : 128 * (j + 1)].reshape(GROUPS, OWN, 128)


def unpack_kernel(in_ref, table_ref, sol_hbm, res_hbm, halves, sems):
    flip = 1 - lax.rem(lax.axis_index("space"), 2)
    scale = 1.0 / mode_scale(table_ref[...])
    lane = lanes((OWN, 128))
    per = 128 // ZC
    copies = []
    for f, hbm in enumerate((sol_hbm, res_hbm)):
        for h in range(NZ // 128):
            for p in range(ROWS):
                plane, y = p // NY, p % NY
                row = (plane + flip * (1 - 2 * plane)) * NY + y
                j, i = p // per, p % per
                tile = None
                for n in range(per):
                    w = in_ref[per * h + n, (f * OUT_TILES + j) * OWN : (f * OUT_TILES + j + 1) * OWN, :]
                    w = turn(w, ZC * (n - i))
                    tile = w if n == 0 else jnp.where(lane >= ZC * n, w, tile)
                halves[f, h, pl.ds(row, OWN, stride=ROWS), :] = tile * scale
            copy = pltpu.make_async_copy(halves.at[f, h], hbm.at[:, pl.ds(128 * h, 128)], sems.at[f, h])
            copy.start()
            copies.append(copy)
    for copy in copies:
        copy.wait()


def whole(count):
    return [pl.BlockSpec(memory_space=pltpu.VMEM)] * count


def anywhere(count):
    return [pl.BlockSpec(memory_space=pltpu.HBM)] * count


def body(load, mean_coeff, kl_ratio, chaos_table):
    params = pltpu.CompilerParams(vmem_limit_bytes=VMEM)
    f32, bf16 = jnp.float32, jnp.bfloat16
    vmem = pltpu.VMEM
    halves = NZ // 128
    table = chaos_table.T
    send = pl.pallas_call(
        pack_kernel,
        out_shape=jax.ShapeDtypeStruct((GROUPS, SEND_ROWS, 128), f32),
        in_specs=anywhere(4),
        out_specs=pl.BlockSpec(memory_space=vmem),
        scratch_shapes=[
            vmem((halves, OWN * ROWS, 128), f32),
            vmem((ROWS, NZ), f32),
            vmem((KL * ROWS, NZ), f32),
            vmem((KL, MODES), jnp.int32),
            pltpu.SemaphoreType.DMA((3 + halves,)),
        ],
        compiler_params=pltpu.CompilerParams(vmem_limit_bytes=PACK_VMEM),
        name="pack",
    )(load.reshape(OWN * ROWS, NZ), mean_coeff.reshape(ROWS, NZ), kl_ratio.reshape(KL * ROWS, NZ), table)
    own = lax.all_to_all(send, "mode", 0, 0, tiled=True)
    count = lax.axis_size("space")
    on_chip = [e for i in range(0, count, 2) for e in ((i, i + 1), (i + 1, i))]
    off_chip = [e for i in range(1, count - 1, 2) for e in ((i, i + 1), (i + 1, i))]
    outer = lax.ppermute(own, "space", off_chip)
    inner = lax.ppermute(own, "space", on_chip)
    shapes = [
        ((COEF_ROWS, 2 * PLANE + 128), f32),
        ((MODES, 2 * PLANE), f32),
        ((KL * MODES, 2 * MODES), bf16),
        ((PLANE, PLANE + 4 * 128), bf16),
        ((128, 4 * PLANE + 128), bf16),
        ((128, 128), bf16),
    ]
    state = pl.pallas_call(
        prep_kernel,
        out_shape=[jax.ShapeDtypeStruct(*shape) for shape in shapes],
        in_specs=whole(2),
        out_specs=whole(len(shapes)),
        scratch_shapes=[vmem((MODES, MODES), f32)],
        compiler_params=params,
        cost_estimate=pl.CostEstimate(flops=1 << 34, bytes_accessed=1 << 22, transcendentals=0),
        name="step_prep",
    )(own, table)
    more = [
        ((COEF_ROWS, 2 * PLANE + 128), f32),
        ((COEF_ROWS, 2 * PLANE), f32),
        ((MODES, 2 * PLANE), f32),
        ((MODES, 2 * PLANE), f32),
    ]
    between = pl.pallas_call(
        between_kernel,
        out_shape=[jax.ShapeDtypeStruct(*shape) for shape in more],
        in_specs=whole(2 + len(shapes)),
        out_specs=whole(len(more)),
        scratch_shapes=[vmem((MODES, 128), f32)],
        compiler_params=params,
        cost_estimate=pl.CostEstimate(flops=1 << 10, bytes_accessed=1 << 10, transcendentals=0),
        name="step_between",
    )(own, inner, *state)
    back = pl.pallas_call(
        step_kernel,
        out_shape=jax.ShapeDtypeStruct((GROUPS, 2 * OUT_TILES * OWN, 128), f32),
        in_specs=whole(3 + len(shapes) + len(more)),
        out_specs=pl.BlockSpec(memory_space=vmem),
        scratch_shapes=[
            vmem((MODES, 256), f32),
            vmem((COEF_ROWS, 2 * PLANE + 128), f32),
            vmem((COEF_ROWS, 256), f32),
            vmem((COEF_ROWS, 2 * PLANE + 256), f32),
            vmem((MODES, 2 * PLANE + 256), f32),
            vmem((MODES, 2 * PLANE + 256), f32),
        ]
        + [vmem((MODES, 4 * PLANE + 128), f32)] * 2
        + [vmem((MODES, 2 * PLANE), f32)] * 3,
        compiler_params=params,
        cost_estimate=pl.CostEstimate(flops=2 << 30, bytes_accessed=1 << 22, transcendentals=0),
        name="step",
    )(own, inner, outer, *state, *between)
    back = lax.all_to_all(back, "mode", 0, 0, tiled=True)
    flat = jax.ShapeDtypeStruct((OWN * ROWS, NZ), f32)
    sol, res = pl.pallas_call(
        unpack_kernel,
        out_shape=(flat, flat),
        in_specs=whole(2),
        out_specs=tuple(anywhere(2)),
        scratch_shapes=[vmem((2, halves, OWN * ROWS, 128), f32), pltpu.SemaphoreType.DMA((2, halves))],
        compiler_params=params,
        name="unpack",
    )(back, table)
    return sol.reshape(load.shape), res.reshape(load.shape)


def solution(mesh):
    in_specs = (
        P("mode", "space", None, None),
        P("space", None, None),
        P(None, "space", None, None),
        P(),
    )
    out_specs = (P("mode", "space", None, None), P("mode", "space", None, None))
    return jax.shard_map(body, mesh=mesh, in_specs=in_specs, out_specs=out_specs, check_vma=False)
```

time: 51.9 us -> 49.6 us (0.956)
  Pallas kernels: 8.19 us -> 11 us
  waiting for transfers between devices: 4.65 us -> 1.95 us
  local copies, waits for them, and re-layouts: 2.67 us -> 0.01 us
    ppermute x1, waiting for transfers between devices: 4.64 us -> 1.57 us  [body(): outer = lax.ppermute(own, 'space', off_chip)]
    pallas_call x0 -> x2, Pallas kernels: none -> 2.67 us  [the longest x1 1.45 us: body(): pl.pallas_call(between_kernel, out_shape=[jax.ShapeDtypeStruct(*shape) fo...]
    unnamed x7 -> x2, local copies, waits for them, and re-layouts: 2.67 us -> 0.01 us
    pallas_call x1, Pallas kernels: 0.66 us -> 2.5 us  [body(): pl.pallas_call(pack_kernel, out_shape=jax.ShapeDtypeStruct((GROUPS, SEND_...]
    pallas_call x1, Pallas kernels: 6.3 us -> 4.63 us  [body(): pl.pallas_call(step_kernel, out_shape=jax.ShapeDtypeStruct((GROUPS, 2 * O...]
  transfers between devices with their start and end apart: 2 -> 2, of which waited for: 1 -> 2; matrix products, arithmetic and copies ran while one was open for 0% -> 0% of each run, Pallas kernels for 0% -> 5%
where the time goes in v3:
time: 49.6 us; the launch traced here: 49.3 us
  blocking collectives  28.7 us (58%)
  Pallas kernels  11 us (22%)
  starting transfers between devices  7 us (14%)
  waiting for transfers between devices  1.95 us (4%)
  between operations  0.7 us (1%)
    all_to_all x1, blocking collectives, body(): own = lax.all_to_all(send, 'mode', 0, 0, tiled=True)  14.9 us
    all_to_all x1, blocking collectives, body(): back = lax.all_to_all(back, 'mode', 0, 0, tiled=True)  13.7 us
    ppermute x1, starting transfers between devices, body(): outer = lax.ppermute(own, 'space', off_chip)  6.91 us
    pallas_call x1, Pallas kernels, body(): pl.pallas_call(step_kernel, out_shape=jax.ShapeDtypeStruct((GROUPS, 2 * O...  4.63 us
    pallas_call x1, Pallas kernels, body(): pl.pallas_call(pack_kernel, out_shape=jax.ShapeDtypeStruct((GROUPS, SEND_...  2.5 us
    ppermute x1, waiting for transfers between devices, body(): outer = lax.ppermute(own, 'space', off_chip)  1.57 us
    pallas_call x1, Pallas kernels, body(): pl.pallas_call(between_kernel, out_shape=[jax.ShapeDtypeStruct(*shape) fo...  1.45 us
    pallas_call x1, Pallas kernels, body(): pl.pallas_call(prep_kernel, out_shape=[jax.ShapeDtypeStruct(*shape) for s...  1.22 us
  transfers between devices with their start and end apart: 2, of which 2 were waited for; matrix products, arithmetic and copies ran while one was open for 0% of the time, Pallas kernels for 5%

profile of v3, /device:TPU:97, one launch (start us, length us, event | category | flops | bytes accessed | tf_op | source)
XLA Modules:
  0.0 49.3 jit_solution(6391289422218549549)
XLA Ops:
  0.6 2.5 %pack.1 = f32[8,80,128]{2,1,0:T(8,128)} custom-call(f32[256,256]{1,0:T(8,128)} %bitcast.9, f32[16,256]{1,0:T(8,128)} %bitcast.11, f32[160,256]{1,0:T(8,128)} %bitcast.10, s32[10,128]{1,0:T(8,128)} %bitcast.6), custom_call_target="tpu_custom_call" | custom-call | tf_op jit(solution)/shard_map/pack/pallas_call | solution.py:465
  3.1 0.0 copy-start
  3.1 14.9 %all_to_all.10.own_ref = f32[8,80,128]{2,1,0:T(8,128)S(1)} all-to-all(f32[8,80,128]{2,1,0:T(8,128)} %pack.1), channel_id=1, replica_groups=mesh['space'=32,'mode'=8] {'mode'}, dimensions={0} | all-to-all | bytes 655360 | tf_op jit(solution)/shard_map/all_to_all | solution.py:480
  18.1 6.9 %collective-permute-start.1 = (f32[8,80,128]{2,1,0:T(8,128)S(1)}, f32[8,80,128]{2,1,0:T(8,128)S(1)}, u32[]{:S(2)}, u32[]{:S(2)}) collective-permute-start(f32[8,80,128]{2,1,0:T(8,128)S(1)} %all_to_all.10.own_ref), channel_id=1, source_target_pairs={{8,16},{16,8},{24,32},{32,24},{40,48},{48,40},{56,64},{64,56},{72,... | collective-permute-start | bytes 983048 | tf_op jit(solution)/shard_map/ppermute | solution.py:484
  25.0 0.1 collective-permute-start
  25.1 0.0 copy-done
  25.1 1.2 %step_prep.1 = (f32[16,640]{1,0:T(8,128)S(1)}, f32[128,512]{1,0:T(8,128)S(1)}, bf16[1280,256]{1,0:T(8,128)(2,1)S(1)}, bf16[256,768]{1,0:T(8,128)(2,1)S(1)}, bf16...) custom-call(f32[8,80,128]{2,1,0:T(8,128)S(1)} %all_to_all.10.own_ref, s32[10,128]{1,0:T(8,128)S(1)} %bitcast.7), custom_call_target="tpu_custom_call" | custom-call | flops 17179869184 | bytes 4194304 | tf_op jit(solution)/shard_map/step_prep/pallas_call | solution.py:494
  26.3 0.4 collective-permute-done.inner_ref
  26.7 1.4 %step_between.1 = (f32[16,640]{1,0:T(8,128)S(1)}, f32[16,512]{1,0:T(8,128)S(1)}, f32[128,512]{1,0:T(8,128)S(1)}, f32[128,512]{1,0:T(8,128)S(1)}) custom-call(f32[8,80,128]{2,1,0:T(8,128)S(1)} %all_to_all.10.own_ref, f32[8,80,128]{2,1,0:T(8,128)S(1)} %collective-permute-done.inner_ref, f32[16,640]{1,0:T(8,128)S(1)} %get-tuple-element.14.coef_own, ...), custom_call_target="tpu_custom_call" | custom-call | flops 1024 | bytes 1024 | tf_op jit(solution)/shard_map/step_between/pallas_call | solution.py:510
  28.2 1.6 %collective-permute-done.1.outer_ref = f32[8,80,128]{2,1,0:T(8,128)S(1)} collective-permute-done((f32[8,80,128]{2,1,0:T(8,128)S(1)}, f32[8,80,128]{2,1,0:T(8,128)S(1)}, u32[]{:S(2)}, u32[]{:S(2)}) %collective-permute-start.1) | collective-permute-done | bytes 327712 | tf_op jit(solution)/shard_map/ppermute | solution.py:484
  29.7 4.6 %step.1 = f32[8,128,128]{2,1,0:T(8,128)S(1)} custom-call(f32[8,80,128]{2,1,0:T(8,128)S(1)} %all_to_all.10.own_ref, f32[8,80,128]{2,1,0:T(8,128)S(1)} %collective-permute-done.inner_ref, f32[8,80,128]{2,1,0:T(8,128)S(1)} %collective-permute-done.1.outer_ref, f32[16,640]{1,0:T(8,128)S(1)} %get-tuple-element.14.coef_own, ...), custom_call_target="tpu_custom_call" | custom-call | flops 2147483648 | bytes 4194304 | tf_op jit(solution)/shard_map/step/pallas_call | solution.py:520
  34.4 13.7 %all_to_all.11.in_ref = f32[8,128,128]{2,1,0:T(8,128)S(1)} all-to-all(f32[8,128,128]{2,1,0:T(8,128)S(1)} %step.1), channel_id=1, replica_groups=mesh['space'=32,'mode'=8] {'mode'}, dimensions={0} | all-to-all | bytes 1048576 | tf_op jit(solution)/shard_map/all_to_all | solution.py:539
  48.1 1.2 %unpack.1 = (f32[256,256]{1,0:T(8,128)}, f32[256,256]{1,0:T(8,128)}) custom-call(f32[8,128,128]{2,1,0:T(8,128)S(1)} %all_to_all.11.in_ref, s32[10,128]{1,0:T(8,128)S(1)} %bitcast.8), custom_call_target="tpu_custom_call" | custom-call | tf_op jit(solution)/shard_map/unpack/pallas_call | solution.py:541
Async XLA Ops:
  3.1 22.0 %copy-start = (s32[128,10]{0,1:T(8,128)S(1)}, s32[128,10]{0,1:T(8,128)}, u32[]{:S(2)}) copy-start(s32[128,10]{0,1:T(8,128)} %param.7) | copy-start | bytes 15364
  18.1 11.7 %collective-permute-start.1 = (f32[8,80,128]{2,1,0:T(8,128)S(1)}, f32[8,80,128]{2,1,0:T(8,128)S(1)}, u32[]{:S(2)}, u32[]{:S(2)}) collective-permute-start(f32[8,80,128]{2,1,0:T(8,128)S(1)} %all_to_all.10.own_ref), channel_id=1, source_target_pairs={{8,16},{16,8},{24,32},{32,24},{40,48},{48,40},{56,64},{64,56},{72,... | collective-permute-start | bytes 983048 | tf_op jit(solution)/shard_map/ppermute | solution.py:484
  25.0 1.7 %collective-permute-start = (f32[8,80,128]{2,1,0:T(8,128)S(1)}, f32[8,80,128]{2,1,0:T(8,128)S(1)}, u32[]{:S(2)}, u32[]{:S(2)}) collective-permute-start(f32[8,80,128]{2,1,0:T(8,128)S(1)} %all_to_all.10.own_ref), channel_id=1, source_target_pairs={{0,8},{8,0},{16,24},{24,16},{32,40},{40,32},{48,56},{56,48},{64,72... | collective-permute-start | bytes 983048 | tf_op jit(solution)/shard_map/ppermute | solution.py:485

commit v4 on v3

--- a/solution.py
+++ b/solution.py
@@ -33,7 +33,6 @@
 SQRT2 = 2.0**0.5
 SQRT6 = 6.0**0.5
 VMEM = 40 * 1024 * 1024
-PACK_VMEM = 62 * 1024 * 1024
 
 
 def lanes(shape):
@@ -176,21 +175,21 @@
 
 
 def build_steps(core_step, near_step, far_step):
-    def fill(ref, at, to, apart):
-        ref[at[0] : at[0] + apart.shape[0], to : to + apart.shape[1]] = jnp.where(
-            apart == 1, 1.0, 0.0
-        ).astype(jnp.bfloat16)
-
-    square = (PLANE, PLANE)
-    fill(core_step, (0,), 0, grid_of(square, core_cell, core_cell))
+    def fill(ref, to, apart, times=1):
+        for n in range(times):
+            ref[apart.shape[0] * n : apart.shape[0] * (n + 1), to : to + apart.shape[1]] = jnp.where(
+                apart == 1, 1.0, 0.0
+            ).astype(jnp.bfloat16)
+
+    fill(core_step, 0, grid_of((PLANE, PLANE), core_cell, core_cell))
     for t in range(4):
 
         def rim_at(l, t=t):
             y, z = rim_cell(l)
             return y + jnp.where(lax.div(l, RIM_PLANE) == t, 0, 100), z
 
-        fill(core_step, (0,), PLANE + 128 * t, grid_of((PLANE, 128), core_cell, rim_at))
-        fill(near_step, (0,), PLANE * t, grid_of((128, PLANE), rim_at, core_cell))
+        fill(core_step, PLANE + 128 * t, grid_of((PLANE, 128), core_cell, rim_at))
+        fill(near_step, PLANE * t, grid_of((128, PLANE), rim_at, core_cell), 2)
 
     def near(l):
         return (lax.div(l, RIM_PLANE) + 1,) + rim_cell(l)
@@ -199,8 +198,8 @@
         t = lax.div(l, RIM_PLANE)
         return (jnp.where(t == 0, 5, jnp.where(t == 1, 0, 100)),) + rim_cell(l)
 
-    fill(near_step, (0,), 4 * PLANE, grid_of((128, 128), near, near))
-    fill(far_step, (0,), 0, grid_of((128, 128), far, near))
+    fill(near_step, 4 * PLANE, grid_of((128, 128), near, near), 2)
+    fill(far_step, 0, grid_of((128, 128), far, near), 2)
 
 
 def tile_of(ref, j):
@@ -223,7 +222,9 @@
 
 
 def far_of(inner, outer):
-    lane = lanes(inner.shape)
+    lane = lanes((inner if outer is None else outer).shape)
+    inner = 0.0 if inner is None else inner
+    outer = 0.0 if outer is None else outer
     return jnp.where(lane < RIM_PLANE, outer, jnp.where(lane < 2 * RIM_PLANE, inner, 0.0))
 
 
@@ -268,33 +269,59 @@
     return sum(out[x.shape[0] * i : x.shape[0] * (i + 1)] for i in range(parts))
 
 
-def neighbours(src, slots, rims, steps, parts=2, along_x=True):
+def from_rim(x, matrix):
+    return jnp.dot(parts_of(x, 2, 1), matrix, preferred_element_type=jnp.float32)
+
+
+def to_rim(x, t, core_step, parts=2):
+    return product(x, core_step[:, PLANE + 128 * (t - 1) : PLANE + 128 * t], parts)
+
+
+def neighbours(src, slots, steps, begun={}):
     core_step, near_step, far_step = steps
     out = {}
+    near = get(src, "near")
     for t in slots:
-        x = product(get(src, t), core_step[:, :PLANE], parts)
-        x = x + product(get(src, "near"), near_step[:, PLANE * (t - 1) : PLANE * t], parts)
-        out[t] = x + (get(src, t - 1) + get(src, t + 1)) if along_x else x
+        if t == "near":
+            x = begun[t] + from_rim(near, near_step[:, 4 * PLANE :]) + from_rim(get(src, "far"), far_step[...])
+            out[t] = x + to_rim(get(src, 4), 4, core_step)
+        else:
+            x = begun[t] if t in begun else product(get(src, t), core_step[:, :PLANE])
+            x = x + from_rim(near, near_step[:, PLANE * (t - 1) : PLANE * t])
+            out[t] = x + (get(src, t - 1) + get(src, t + 1))
+    return out
+
+
+def sum_coefs(dst, src, slots, rims, steps):
+    core_step, near_step, far_step = steps
+    near = get(src, "near")
+    for t in slots:
+        x = product(get(src, t), core_step[:, :PLANE], 3)
+        x = x + product(near, near_step[:128, PLANE * (t - 1) : PLANE * t], 3)
+        put(dst, t, x + (get(src, t - 1) + get(src, t + 1)) + 6.0 * get(src, t))
     if rims:
-        out["near"] = product(get(src, "near"), near_step[:, 4 * PLANE :], parts)
-        out["near"] += product(get(src, "far"), far_step[...], parts)
+        x = product(near, near_step[:128, 4 * PLANE :], 3) + product(get(src, "far"), far_step[:128, :], 3)
         for t in (1, 2, 3, 4):
-            out["near"] += product(get(src, t), core_step[:, PLANE + 128 * (t - 1) : PLANE + 128 * t], parts)
-    return out
-
-
-def mix(links, x, sums):
+            x = x + to_rim(get(src, t), t, core_step, 3)
+        put(dst, "near", x + 6.0 * near)
+
+
+def mix(links, x, sums, kept=None, known=None):
     width = x.shape[1]
-    pair = parts_of(x, 2)
+    pair = parts_of(x, 2) if known is None else None
     rows_of = [
         [jnp.broadcast_to(ref[k : k + 1, at], (8, width)) for k in range(TERMS)] for (ref, at), _ in sums
     ]
     split = lambda x: x.reshape(BLOCK // 8, 8, width)
     for b in range(MODES // BLOCK):
         rows = slice(BLOCK * b, BLOCK * (b + 1))
-        mixed = jnp.dot(
-            links[KL * BLOCK * b : KL * BLOCK * (b + 1), :], pair, preferred_element_type=jnp.float32
-        )
+        at = slice(KL * BLOCK * b, KL * BLOCK * (b + 1))
+        if known is None:
+            mixed = jnp.dot(links[at, :], pair, preferred_element_type=jnp.float32)
+        else:
+            mixed = known[at, :]
+        if kept is not None:
+            kept[at, :] = mixed
         here = split(x[rows, :])
         totals = [here * weights[KL][None] for weights in rows_of]
         for k in range(KL):
@@ -315,13 +342,13 @@
     return finish
 
 
-def prep_kernel(own_ref, table_ref, coef, pc, links, core_step, near_step, far_step, pad):
+def prep_kernel(own_ref, table_ref, coef, pc, mix3, links, core_step, near_step, far_step, pad):
     build_links(table_ref, links, pad)
     build_steps(core_step, near_step, far_step)
     coef[...] = slab_coefs(own_ref)
-    for plane in range(2):
+    for plane, kept in ((0, None), (1, mix3)):
         at = slice(PLANE * plane, PLANE * (plane + 1))
-        mix(links, plane_of(own_ref, plane), [((coef, at), into({plane: (pc, at)}, plane))])
+        mix(links, plane_of(own_ref, plane), [((coef, at), into({plane: (pc, at)}, plane))], kept)
 
 
 def lo(n):
@@ -331,37 +358,51 @@
 NEAR, FAR = slice(0, 128), slice(128, 256)
 TAIL = slice(2 * PLANE, 2 * PLANE + 128)
 FAR_TAIL = slice(2 * PLANE + 128, 2 * PLANE + 256)
+BEGUN_U, BEGUN_P = slice(3 * PLANE, 3 * PLANE + 128), slice(3 * PLANE + 128, 3 * PLANE + 256)
 NEAR_TAIL = slice(4 * PLANE, 4 * PLANE + 128)
 
 
-def between_kernel(own_ref, inner_ref, coef_own, pc_own, links, core_step, near_step, far_step, coef_inner, ecoef, pc, qc, near):
+def between_kernel(own_ref, inner_ref, coef_own, pc_own, mix3, links, core_step, near_step, far_step, coef_inner, ecoef, pc, qc, near, begun):
     steps = (core_step, near_step, far_step)
     uf = {0: functools.partial(plane_of, inner_ref, 1), 1: functools.partial(plane_of, inner_ref, 0)}
     uf.update({2: functools.partial(plane_of, own_ref, 0), 3: functools.partial(plane_of, own_ref, 1)})
-    near[...] = near_of(tile_of(inner_ref, CORE_TILES), tile_of(own_ref, CORE_TILES), None)
+    inner = tile_of(inner_ref, CORE_TILES)
+    near[...] = near_of(inner, tile_of(own_ref, CORE_TILES), None)
     uf["near"] = (near, NEAR)
+    uf[4] = lambda: jnp.zeros((MODES, PLANE), jnp.float32)
     coef_inner[...] = slab_coefs(inner_ref)
     cf = {0: (coef_inner, lo(1)), 1: (coef_inner, lo(0)), 2: (coef_own, lo(0)), 3: (coef_own, lo(1))}
     cf["near"] = lambda: near_of(coef_inner[:, TAIL], coef_own[:, TAIL], None)
     ef = {t: (ecoef, lo(t - 1)) for t in (1, 2)}
-    for t, x in neighbours(cf, (1, 2), False, steps, 3).items():
-        put(ef, t, x + 6.0 * get(cf, t))
-    pf = {t: (pc, lo(t)) for t in (0, 1)}
-    qf = {t: (qc, lo(t - 1)) for t in (1, 2)}
+    sum_coefs(ef, cf, (1, 2), False, steps)
+    pf = {0: (pc, lo(0)), 1: (pc, lo(1)), 2: (pc_own, lo(0)), 3: (pc_own, lo(1))}
+    qf = {t: (qc, lo(t - 1)) for t in (1, 2, 3)}
     mix(links, get(uf, 1), [(cf[1], into(pf, 1)), (ef[1], into(qf, 1))])
     mix(links, get(uf, 2), [(ef[2], into(qf, 2))])
     mix(links, get(uf, 0), [(cf[0], into(pf, 0))])
-    for t, x in neighbours(uf, (1, 2), False, steps).items():
+    qc[:, lo(2)] = jnp.zeros((MODES, PLANE), jnp.float32)
+    for t, x in neighbours(uf, (1, 2, 3), steps).items():
         mix(links, x, [(cf[t], into(qf, t, -1))])
-
-
-def step_kernel(own_ref, inner_ref, outer_ref, coef_own, pc_own, links, core_step, near_step, far_step, coef_inner, ecoef_known, pc_known, qc_known, out_ref, rims, coef_outer, coef_rims, ecoef, pc, qc, search, pc2, qc2, sol, res):
+    rim = from_rim(near[...], near_step[:, 4 * PLANE :]) + from_rim(far_of(inner, None), far_step[...])
+    for t in (1, 2, 3):
+        rim = rim + to_rim(get(uf, t), t, core_step)
+    begun[:, BEGUN_U] = rim
+    rim = jnp.zeros((MODES, 128), jnp.float32)
+    for t in (1, 2, 3):
+        x = get(pf, t)
+        begun[:, lo(t - 1)] = product(x, core_step[:, :PLANE])
+        rim = rim + to_rim(x, t, core_step)
+    begun[:, BEGUN_P] = rim
+
+
+def step_kernel(own_ref, inner_ref, outer_ref, coef_own, pc_own, mix3, links, core_step, near_step, far_step, coef_inner, ecoef_known, pc_known, qc_known, near_known, begun, out_ref, rims, coef_outer, coef_rims, ecoef, pc, qc, search, pc2, qc2, sol, res):
     steps = (core_step, near_step, far_step)
     uf = {}
     for t, (ref, plane) in enumerate(((inner_ref, 1), (inner_ref, 0), (own_ref, 0), (own_ref, 1), (outer_ref, 1), (outer_ref, 0))):
         uf[t] = functools.partial(plane_of, ref, plane)
-    inner, own, outer = (tile_of(ref, CORE_TILES) for ref in (inner_ref, own_ref, outer_ref))
-    rims[:, NEAR] = near_of(inner, own, outer)
+    inner, outer = tile_of(inner_ref, CORE_TILES), tile_of(outer_ref, CORE_TILES)
+    near_new = jnp.where(lanes((MODES, 128)) < 3 * RIM_PLANE, 0.0, turn(outer, 2 * RIM_PLANE))
+    rims[:, NEAR] = near_known[...] + near_new
     rims[:, FAR] = far_of(inner, outer)
     uf.update(near=(rims, NEAR), far=(rims, FAR))
 
@@ -372,29 +413,34 @@
     cf.update({4: (coef_outer, lo(1)), 5: (coef_outer, lo(0)), "near": (coef_rims, NEAR), "far": (coef_rims, FAR)})
     ef = {t: (ecoef_known, lo(t - 1)) for t in (1, 2)}
     ef.update({3: (ecoef, lo(0)), 4: (ecoef, lo(1)), "near": (ecoef, TAIL)})
-    for t, x in neighbours(cf, (3, 4), True, steps, 3).items():
-        put(ef, t, x + 6.0 * get(cf, t))
-    ecoef[:, FAR_TAIL] = jnp.zeros((COEF_ROWS, 128), jnp.float32)
 
     pf = {0: (pc_known, lo(0)), 1: (pc_known, lo(1)), 2: (pc_own, lo(0)), 3: (pc_own, lo(1)), 4: (pc, lo(0)), 5: (pc, lo(1))}
     pf.update(near=(pc, TAIL), far=(pc, FAR_TAIL))
     qf = {1: (qc_known, lo(0)), 2: (qc_known, lo(1)), 3: (qc, lo(0)), 4: (qc, lo(1)), "near": (qc, TAIL)}
     all_rims = slice(TAIL.start, FAR_TAIL.stop)
-
-    mix(links, get(uf, 3), [(ef[3], into(qf, 3))])
-    mix(links, get(uf, 4), [(cf[4], into(pf, 4)), (ef[4], into(qf, 4))])
+    qc[:, lo(0)] = qc_known[:, lo(2)]
     mix(links, get(uf, 5), [(cf[5], into(pf, 5))])
+    sum_coefs(ef, cf, (3, 4), True, steps)
+    ecoef[:, FAR_TAIL] = jnp.zeros((COEF_ROWS, 128), jnp.float32)
+    around = neighbours(uf, (4,), steps)[4]
+    x = begun[:, BEGUN_U] + to_rim(get(uf, 4), 4, core_step)
+    around_near = x + from_rim(near_new, near_step[:, 4 * PLANE :]) + from_rim(far_of(None, outer), far_step[...])
     rim_sums = [((coef_rims, slice(0, 256)), pc), ((ecoef, all_rims), qc)]
     mix(links, rims[...], [(weights, into({0: (ref, all_rims)}, 0)) for weights, ref in rim_sums])
-    for t, x in neighbours(uf, (3, 4), True, steps).items():
-        mix(links, x, [(cf[t], into(qf, t, -1))])
+    mix(links, get(uf, 4), [(cf[4], into(pf, 4)), (ef[4], into(qf, 4)), (cf[3], into(qf, 3, -1))])
+    known = {t: begun[:, lo(t - 1)] for t in (1, 2, 3)}
+    known["near"] = begun[:, BEGUN_P]
+    around_p = neighbours(pf, (1, 2, 3, 4, "near"), steps, known)
+    mix(links, around, [(cf[4], into(qf, 4, -1))])
+    mix(links, around_near, [(cf["near"], into(qf, "near", -1))])
+    mix(links, get(uf, 3), [(ef[3], into(qf, 3, 1))], known=mix3)
 
     sigma = THETA / DELTA
     rho = 1.0 / sigma
     rho_next = 1.0 / (2.0 * sigma - rho)
     sf = {t: (search, lo(t - 1)) for t in (1, 2, 3, 4)}
     sf["near"] = (search, NEAR_TAIL)
-    for t, x in neighbours(pf, (1, 2, 3, 4), True, steps).items():
+    for t, x in around_p.items():
         start = get(uf, t)
         au = start + 0.5 * (get(qf, t) - x)
         begin = start * (1.0 / THETA)
@@ -408,14 +454,16 @@
 
     pf = {t: (pc2, at) for t, (_, at) in sf.items()}
     qf = {t: (qc2, lo(t - 2)) for t in (2, 3)}
-    for t in (2, 3, 1, 4, "near"):
+    around = neighbours(sf, (2, 3), steps)
+    for t in (1, 2, 3, 4, "near"):
         sums = [(cf[t], into(pf, t))]
         if t in (2, 3):
             sums.append((ef[t], into(qf, t)))
         mix(links, get(sf, t), sums)
-    for t, x in neighbours(sf, (2, 3), False, steps).items():
+    around_p = neighbours(pf, (2, 3), steps)
+    for t, x in around.items():
         mix(links, x, [(cf[t], into(qf, t, -1))])
-    for t, x in neighbours(pf, (2, 3), False, steps).items():
+    for t, x in around_p.items():
         res[:, lo(t - 2)] = res[:, lo(t - 2)] - (get(sf, t) + 0.5 * (get(qf, t) - x))
     for f, field in enumerate((sol, res)):
         for j in range(OUT_TILES):
@@ -474,9 +522,9 @@
             vmem((KL, MODES), jnp.int32),
             pltpu.SemaphoreType.DMA((3 + halves,)),
         ],
-        compiler_params=pltpu.CompilerParams(vmem_limit_bytes=PACK_VMEM),
+        compiler_params=pltpu.CompilerParams(vmem_limit_bytes=VMEM),
         name="pack",
-    )(load.reshape(OWN * ROWS, NZ), mean_coeff.reshape(ROWS, NZ), kl_ratio.reshape(KL * ROWS, NZ), table)
+    )(*(pltpu.with_memory_space_constraint(x, pltpu.HBM) for x in (load.reshape(OWN * ROWS, NZ), mean_coeff.reshape(ROWS, NZ), kl_ratio.reshape(KL * ROWS, NZ), table)))
     own = lax.all_to_all(send, "mode", 0, 0, tiled=True)
     count = lax.axis_size("space")
     on_chip = [e for i in range(0, count, 2) for e in ((i, i + 1), (i + 1, i))]
@@ -486,10 +534,11 @@
     shapes = [
         ((COEF_ROWS, 2 * PLANE + 128), f32),
         ((MODES, 2 * PLANE), f32),
+        ((KL * MODES, PLANE), f32),
         ((KL * MODES, 2 * MODES), bf16),
         ((PLANE, PLANE + 4 * 128), bf16),
-        ((128, 4 * PLANE + 128), bf16),
-        ((128, 128), bf16),
+        ((256, 4 * PLANE + 128), bf16),
+        ((256, 128), bf16),
     ]
     state = pl.pallas_call(
         prep_kernel,
@@ -505,14 +554,15 @@
         ((COEF_ROWS, 2 * PLANE + 128), f32),
         ((COEF_ROWS, 2 * PLANE), f32),
         ((MODES, 2 * PLANE), f32),
-        ((MODES, 2 * PLANE), f32),
+        ((MODES, 3 * PLANE), f32),
+        ((MODES, 128), f32),
+        ((MODES, 3 * PLANE + 256), f32),
     ]
     between = pl.pallas_call(
         between_kernel,
         out_shape=[jax.ShapeDtypeStruct(*shape) for shape in more],
         in_specs=whole(2 + len(shapes)),
         out_specs=whole(len(more)),
-        scratch_shapes=[vmem((MODES, 128), f32)],
         compiler_params=params,
         cost_estimate=pl.CostEstimate(flops=1 << 10, bytes_accessed=1 << 10, transcendentals=0),
         name="step_between",

time: 49.6 us -> 47.7 us (0.962)
  Pallas kernels: 11 us -> 9.8 us
  waiting for transfers between devices: 1.95 us -> 1.41 us
    pallas_call x1, Pallas kernels: 4.63 us -> 3.63 us  [body(): pl.pallas_call(step_kernel, out_shape=jax.ShapeDtypeStruct((GROUPS, 2 * O...]
    pallas_call x1, Pallas kernels: 2.5 us -> 1.78 us  [body(): pl.pallas_call(pack_kernel, out_shape=jax.ShapeDtypeStruct((GROUPS, SEND_...]
    pallas_call x1, Pallas kernels: 1.45 us -> 2 us  [body(): pl.pallas_call(between_kernel, out_shape=[jax.ShapeDtypeStruct(*shape) fo...]
    ppermute x1, waiting for transfers between devices: 1.57 us -> 1.02 us  [body(): outer = lax.ppermute(own, 'space', off_chip)]
  transfers between devices with their start and end apart: 2 -> 2, of which waited for: 2 -> 2; matrix products, arithmetic and copies ran while one was open for 0% -> 0% of each run, Pallas kernels for 5% -> 7%
where the time goes in v4:
time: 47.7 us; the launch traced here: 47.5 us
  blocking collectives  28.6 us (60%)
  Pallas kernels  9.8 us (21%)
  starting transfers between devices  7 us (15%)
  waiting for transfers between devices  1.41 us (3%)
  between operations  0.69 us (1%)
    all_to_all x1, blocking collectives, body(): own = lax.all_to_all(send, 'mode', 0, 0, tiled=True)  14.7 us
    all_to_all x1, blocking collectives, body(): back = lax.all_to_all(back, 'mode', 0, 0, tiled=True)  13.9 us
    ppermute x1, starting transfers between devices, body(): outer = lax.ppermute(own, 'space', off_chip)  6.91 us
    pallas_call x1, Pallas kernels, body(): pl.pallas_call(step_kernel, out_shape=jax.ShapeDtypeStruct((GROUPS, 2 * O...  3.63 us
    pallas_call x1, Pallas kernels, body(): pl.pallas_call(between_kernel, out_shape=[jax.ShapeDtypeStruct(*shape) fo...  2 us
    pallas_call x1, Pallas kernels, body(): pl.pallas_call(pack_kernel, out_shape=jax.ShapeDtypeStruct((GROUPS, SEND_...  1.78 us
    pallas_call x1, Pallas kernels, body(): pl.pallas_call(prep_kernel, out_shape=[jax.ShapeDtypeStruct(*shape) for s...  1.21 us
    pallas_call x1, Pallas kernels, body(): pl.pallas_call(unpack_kernel, out_shape=(flat, flat), in_specs=whole(2),...  1.18 us
  transfers between devices with their start and end apart: 2, of which 2 were waited for; matrix products, arithmetic and copies ran while one was open for 0% of the time, Pallas kernels for 7%

profile of v4, /device:TPU:97, one launch (start us, length us, event | category | flops | bytes accessed | tf_op | source)
XLA Modules:
  0.0 47.5 jit_solution(12073476395437131894)
XLA Ops:
  0.6 0.0 copy-start
  0.6 1.8 %pack.1 = f32[8,80,128]{2,1,0:T(8,128)S(1)} custom-call(f32[256,256]{1,0:T(8,128)} %bitcast.9, f32[16,256]{1,0:T(8,128)} %bitcast.11, f32[160,256]{1,0:T(8,128)} %bitcast.10, s32[10,128]{1,0:T(8,128)} %bitcast.6), custom_call_target="tpu_custom_call" | custom-call | tf_op jit(solution)/shard_map/pack/pallas_call | solution.py:513
  2.4 14.7 %all_to_all.10.own_ref = f32[8,80,128]{2,1,0:T(8,128)S(1)} all-to-all(f32[8,80,128]{2,1,0:T(8,128)S(1)} %pack.1), channel_id=1, replica_groups=mesh['space'=32,'mode'=8] {'mode'}, dimensions={0} | all-to-all | bytes 655360 | tf_op jit(solution)/shard_map/all_to_all | solution.py:528
  17.2 6.9 %collective-permute-start.1 = (f32[8,80,128]{2,1,0:T(8,128)S(1)}, f32[8,80,128]{2,1,0:T(8,128)S(1)}, u32[]{:S(2)}, u32[]{:S(2)}) collective-permute-start(f32[8,80,128]{2,1,0:T(8,128)S(1)} %all_to_all.10.own_ref), channel_id=1, source_target_pairs={{8,16},{16,8},{24,32},{32,24},{40,48},{48,40},{56,64},{64,56},{72,... | collective-permute-start | bytes 983048 | tf_op jit(solution)/shard_map/ppermute | solution.py:532
  24.1 0.1 collective-permute-start
  24.2 0.0 copy-done
  24.2 1.2 %step_prep.1 = (f32[16,640]{1,0:T(8,128)S(1)}, f32[128,512]{1,0:T(8,128)S(1)}, f32[1280,256]{1,0:T(8,128)S(1)}, bf16[1280,256]{1,0:T(8,128)(2,1)S(1)}, bf16[256,...) custom-call(f32[8,80,128]{2,1,0:T(8,128)S(1)} %all_to_all.10.own_ref, ...), custom_call_target="tpu_custom_call" | custom-call | flops 17179869184 | bytes 4194304 | tf_op jit(solution)/shard_map/step_prep/pallas_call | solution.py:543
  25.4 0.4 collective-permute-done.inner_ref
  25.8 2.0 %step_between.1 = (f32[16,640]{1,0:T(8,128)S(1)}, f32[16,512]{1,0:T(8,128)S(1)}, f32[128,512]{1,0:T(8,128)S(1)}, f32[128,768]{1,0:T(8,128)S(1)}, f32[128,128]{1,0:T(8,128)S(1)}, /*index=5*/f32[128,1024]{1,0:T(8,128)S(1)}) custom-call(f32[8,80,128]{2,1,0:T(8,128)S(1)} %all_to_all.10.own_ref, f32[8,80,128]{2,1,0:T(8,128)S(1)} %collective-permute-done.inner_ref, ...), custom_call_target="tpu_custom_call" | custom-call | flops 1024 | bytes 1024 | tf_op jit(solution)/shard_map/step_between/pallas_call | solution.py:561
  27.8 1.0 %collective-permute-done.1.outer_ref = f32[8,80,128]{2,1,0:T(8,128)S(1)} collective-permute-done((f32[8,80,128]{2,1,0:T(8,128)S(1)}, f32[8,80,128]{2,1,0:T(8,128)S(1)}, u32[]{:S(2)}, u32[]{:S(2)}) %collective-permute-start.1) | collective-permute-done | bytes 327712 | tf_op jit(solution)/shard_map/ppermute | solution.py:532
  28.8 3.6 %step.1 = f32[8,128,128]{2,1,0:T(8,128)S(1)} custom-call(f32[8,80,128]{2,1,0:T(8,128)S(1)} %all_to_all.10.own_ref, f32[8,80,128]{2,1,0:T(8,128)S(1)} %collective-permute-done.inner_ref, f32[8,80,128]{2,1,0:T(8,128)S(1)} %collective-permute-done.1.outer_ref, f32[16,640]{1,0:T(8,128)S(1)} %get-tuple-element.17.coef_own, ...), custom_call_target="tpu_custom_call" | custom-call | flops 2147483648 | bytes 4194304 | tf_op jit(solution)/shard_map/step/pallas_call | solution.py:570
  32.4 13.9 %all_to_all.11.in_ref = f32[8,128,128]{2,1,0:T(8,128)S(1)} all-to-all(f32[8,128,128]{2,1,0:T(8,128)S(1)} %step.1), channel_id=1, replica_groups=mesh['space'=32,'mode'=8] {'mode'}, dimensions={0} | all-to-all | bytes 1048576 | tf_op jit(solution)/shard_map/all_to_all | solution.py:589
  46.3 1.2 %unpack.1 = (f32[256,256]{1,0:T(8,128)}, f32[256,256]{1,0:T(8,128)}) custom-call(f32[8,128,128]{2,1,0:T(8,128)S(1)} %all_to_all.11.in_ref, s32[10,128]{1,0:T(8,128)S(1)} %bitcast.8), custom_call_target="tpu_custom_call" | custom-call | tf_op jit(solution)/shard_map/unpack/pallas_call | solution.py:591
Async XLA Ops:
  0.6 23.5 %copy-start = (s32[128,10]{0,1:T(8,128)S(1)}, s32[128,10]{0,1:T(8,128)}, u32[]{:S(2)}) copy-start(s32[128,10]{0,1:T(8,128)} %param.7) | copy-start | bytes 15364
  17.2 11.7 %collective-permute-start.1 = (f32[8,80,128]{2,1,0:T(8,128)S(1)}, f32[8,80,128]{2,1,0:T(8,128)S(1)}, u32[]{:S(2)}, u32[]{:S(2)}) collective-permute-start(f32[8,80,128]{2,1,0:T(8,128)S(1)} %all_to_all.10.own_ref), channel_id=1, source_target_pairs={{8,16},{16,8},{24,32},{32,24},{40,48},{48,40},{56,64},{64,56},{72,... | collective-permute-start | bytes 983048 | tf_op jit(solution)/shard_map/ppermute | solution.py:532
  24.1 1.7 %collective-permute-start = (f32[8,80,128]{2,1,0:T(8,128)S(1)}, f32[8,80,128]{2,1,0:T(8,128)S(1)}, u32[]{:S(2)}, u32[]{:S(2)}) collective-permute-start(f32[8,80,128]{2,1,0:T(8,128)S(1)} %all_to_all.10.own_ref), channel_id=1, source_target_pairs={{0,8},{8,0},{16,24},{24,16},{32,40},{40,32},{48,56},{56,48},{64,72... | collective-permute-start | bytes 983048 | tf_op jit(solution)/shard_map/ppermute | solution.py:533

commit v5 on v4

--- a/solution.py
+++ b/solution.py
@@ -83,9 +83,8 @@
     flip = 1 - lax.rem(lax.axis_index("space"), 2)
     lane = lanes((OWN, 128))
     per = 128 // ZC
-    for copy in copies:
+    for copy in copies[:2]:
         copy.wait()
-    scale = mode_scale(table_ref[...])
 
     def row_of(p):
         plane, y = p // NY, lax.rem(p, NY)
@@ -103,7 +102,7 @@
         coefs.append([(c[:, :128], c[:, 128:]) for c in (low, mid, top)])
     lane8 = lanes((8, 128))
     sub8 = lax.broadcasted_iota(jnp.int32, (8, 128), 0)
-    first = lax.rem(lane8, RIM) < HALO
+    first = (lane8 & (RIM - 1)) < HALO
     borders = [jnp.zeros((8, 128), jnp.float32)] * (GROUPS + 1)
     for i in range(2):
         for g in range(3):
@@ -120,7 +119,10 @@
         low = jnp.where(sub8 < TERMS - 8, own_cells[8:, :], jnp.where(first, borders[d], borders[d + 1]))
         base.append(jnp.concatenate([own_cells[:8, :], low], axis=0))
 
-    first = lax.rem(lane, RIM) < HALO
+    for copy in copies[2:]:
+        copy.wait()
+    scale = mode_scale(table_ref[...])
+    first = (lane & (RIM - 1)) < HALO
     borders = [jnp.zeros((OWN, 128), jnp.float32)] * (GROUPS + 1)
     for j in range(CORE_TILES):
         rows = []
@@ -160,12 +162,12 @@
 
 
 def core_cell(l):
-    return lax.div(l, ZC), lax.rem(l, ZC)
+    return l >> 5, l & (ZC - 1)
 
 
 def rim_cell(l):
-    zi = lax.rem(l, RIM)
-    return lax.rem(lax.div(l, RIM), NY), jnp.where(zi < HALO, zi - HALO, zi + ZC - HALO)
+    zi = l & (RIM - 1)
+    return (l >> 2) & (NY - 1), jnp.where(zi < HALO, zi - HALO, zi + ZC - HALO)
 
 
 def grid_of(shape, rows_of, cols_of):
@@ -174,7 +176,7 @@
     return sum(jnp.abs(x - y) for x, y in zip(a, b))
 
 
-def build_steps(core_step, near_step, far_step):
+def build_steps(core_step, near_step):
     def fill(ref, to, apart, times=1):
         for n in range(times):
             ref[apart.shape[0] * n : apart.shape[0] * (n + 1), to : to + apart.shape[1]] = jnp.where(
@@ -182,24 +184,20 @@
             ).astype(jnp.bfloat16)
 
     fill(core_step, 0, grid_of((PLANE, PLANE), core_cell, core_cell))
-    for t in range(4):
+    for t in (1, 2, 3, 4):
 
         def rim_at(l, t=t):
             y, z = rim_cell(l)
-            return y + jnp.where(lax.div(l, RIM_PLANE) == t, 0, 100), z
-
-        fill(core_step, PLANE + 128 * t, grid_of((PLANE, 128), core_cell, rim_at))
-        fill(near_step, PLANE * t, grid_of((128, PLANE), rim_at, core_cell), 2)
+            return y + jnp.where((l >> 5) == t - 1, 0, 100), z
+
+        if t in (2, 3):
+            fill(core_step, PLANE + 128 * (t - 2), grid_of((PLANE, 128), core_cell, rim_at))
+        fill(near_step, PLANE * (t - 1), grid_of((128, PLANE), rim_at, core_cell), 2)
 
     def near(l):
-        return (lax.div(l, RIM_PLANE) + 1,) + rim_cell(l)
-
-    def far(l):
-        t = lax.div(l, RIM_PLANE)
-        return (jnp.where(t == 0, 5, jnp.where(t == 1, 0, 100)),) + rim_cell(l)
+        return ((l >> 5),) + rim_cell(l)
 
     fill(near_step, 4 * PLANE, grid_of((128, 128), near, near), 2)
-    fill(far_step, 0, grid_of((128, 128), far, near), 2)
 
 
 def tile_of(ref, j):
@@ -219,13 +217,6 @@
     if outer is not None:
         out = jnp.where(lane < 3 * RIM_PLANE, out, turn(outer, 2 * RIM_PLANE))
     return out
-
-
-def far_of(inner, outer):
-    lane = lanes((inner if outer is None else outer).shape)
-    inner = 0.0 if inner is None else inner
-    outer = 0.0 if outer is None else outer
-    return jnp.where(lane < RIM_PLANE, outer, jnp.where(lane < 2 * RIM_PLANE, inner, 0.0))
 
 
 def slab_coefs(ref):
@@ -274,17 +265,16 @@
 
 
 def to_rim(x, t, core_step, parts=2):
-    return product(x, core_step[:, PLANE + 128 * (t - 1) : PLANE + 128 * t], parts)
+    return product(x, core_step[:, PLANE + 128 * (t - 2) : PLANE + 128 * (t - 1)], parts)
 
 
 def neighbours(src, slots, steps, begun={}):
-    core_step, near_step, far_step = steps
+    core_step, near_step = steps
     out = {}
     near = get(src, "near")
     for t in slots:
         if t == "near":
-            x = begun[t] + from_rim(near, near_step[:, 4 * PLANE :]) + from_rim(get(src, "far"), far_step[...])
-            out[t] = x + to_rim(get(src, 4), 4, core_step)
+            out[t] = begun[t] + from_rim(near, near_step[:, 4 * PLANE :])
         else:
             x = begun[t] if t in begun else product(get(src, t), core_step[:, :PLANE])
             x = x + from_rim(near, near_step[:, PLANE * (t - 1) : PLANE * t])
@@ -292,18 +282,13 @@
     return out
 
 
-def sum_coefs(dst, src, slots, rims, steps):
-    core_step, near_step, far_step = steps
+def sum_coefs(dst, src, slots, steps):
+    core_step, near_step = steps
     near = get(src, "near")
     for t in slots:
         x = product(get(src, t), core_step[:, :PLANE], 3)
         x = x + product(near, near_step[:128, PLANE * (t - 1) : PLANE * t], 3)
         put(dst, t, x + (get(src, t - 1) + get(src, t + 1)) + 6.0 * get(src, t))
-    if rims:
-        x = product(near, near_step[:128, 4 * PLANE :], 3) + product(get(src, "far"), far_step[:128, :], 3)
-        for t in (1, 2, 3, 4):
-            x = x + to_rim(get(src, t), t, core_step, 3)
-        put(dst, "near", x + 6.0 * near)
 
 
 def mix(links, x, sums, kept=None, known=None):
@@ -342,9 +327,9 @@
     return finish
 
 
-def prep_kernel(own_ref, table_ref, coef, pc, mix3, links, core_step, near_step, far_step, pad):
+def prep_kernel(own_ref, table_ref, coef, pc, mix3, links, core_step, near_step, pad):
     build_links(table_ref, links, pad)
-    build_steps(core_step, near_step, far_step)
+    build_steps(core_step, near_step)
     coef[...] = slab_coefs(own_ref)
     for plane, kept in ((0, None), (1, mix3)):
         at = slice(PLANE * plane, PLANE * (plane + 1))
@@ -362,8 +347,8 @@
 NEAR_TAIL = slice(4 * PLANE, 4 * PLANE + 128)
 
 
-def between_kernel(own_ref, inner_ref, coef_own, pc_own, mix3, links, core_step, near_step, far_step, coef_inner, ecoef, pc, qc, near, begun):
-    steps = (core_step, near_step, far_step)
+def between_kernel(own_ref, inner_ref, coef_own, pc_own, mix3, links, core_step, near_step, coef_inner, ecoef, pc, qc, near, begun):
+    steps = (core_step, near_step)
     uf = {0: functools.partial(plane_of, inner_ref, 1), 1: functools.partial(plane_of, inner_ref, 0)}
     uf.update({2: functools.partial(plane_of, own_ref, 0), 3: functools.partial(plane_of, own_ref, 1)})
     inner = tile_of(inner_ref, CORE_TILES)
@@ -374,7 +359,8 @@
     cf = {0: (coef_inner, lo(1)), 1: (coef_inner, lo(0)), 2: (coef_own, lo(0)), 3: (coef_own, lo(1))}
     cf["near"] = lambda: near_of(coef_inner[:, TAIL], coef_own[:, TAIL], None)
     ef = {t: (ecoef, lo(t - 1)) for t in (1, 2)}
-    sum_coefs(ef, cf, (1, 2), False, steps)
+    sum_coefs(ef, cf, (1, 2), steps)
+    ecoef[:, TAIL] = to_rim(get(cf, 2), 2, core_step, 3) + to_rim(get(cf, 3), 3, core_step, 3)
     pf = {0: (pc, lo(0)), 1: (pc, lo(1)), 2: (pc_own, lo(0)), 3: (pc_own, lo(1))}
     qf = {t: (qc, lo(t - 1)) for t in (1, 2, 3)}
     mix(links, get(uf, 1), [(cf[1], into(pf, 1)), (ef[1], into(qf, 1))])
@@ -383,48 +369,43 @@
     qc[:, lo(2)] = jnp.zeros((MODES, PLANE), jnp.float32)
     for t, x in neighbours(uf, (1, 2, 3), steps).items():
         mix(links, x, [(cf[t], into(qf, t, -1))])
-    rim = from_rim(near[...], near_step[:, 4 * PLANE :]) + from_rim(far_of(inner, None), far_step[...])
+    rim = from_rim(near[...], near_step[:, 4 * PLANE :])
+    begun[:, BEGUN_U] = rim + to_rim(get(uf, 2), 2, core_step) + to_rim(get(uf, 3), 3, core_step)
     for t in (1, 2, 3):
-        rim = rim + to_rim(get(uf, t), t, core_step)
-    begun[:, BEGUN_U] = rim
-    rim = jnp.zeros((MODES, 128), jnp.float32)
-    for t in (1, 2, 3):
-        x = get(pf, t)
-        begun[:, lo(t - 1)] = product(x, core_step[:, :PLANE])
-        rim = rim + to_rim(x, t, core_step)
-    begun[:, BEGUN_P] = rim
-
-
-def step_kernel(own_ref, inner_ref, outer_ref, coef_own, pc_own, mix3, links, core_step, near_step, far_step, coef_inner, ecoef_known, pc_known, qc_known, near_known, begun, out_ref, rims, coef_outer, coef_rims, ecoef, pc, qc, search, pc2, qc2, sol, res):
-    steps = (core_step, near_step, far_step)
+        begun[:, lo(t - 1)] = product(get(pf, t), core_step[:, :PLANE])
+    begun[:, BEGUN_P] = to_rim(get(pf, 2), 2, core_step) + to_rim(get(pf, 3), 3, core_step)
+
+
+def step_kernel(own_ref, inner_ref, outer_ref, coef_own, pc_own, mix3, links, core_step, near_step, coef_inner, ecoef_known, pc_known, qc_known, near_known, begun, out_ref, rims, coef_outer, coef_rims, ecoef, pc, qc, search, pc2, qc2, sol, res):
+    steps = (core_step, near_step)
     uf = {}
     for t, (ref, plane) in enumerate(((inner_ref, 1), (inner_ref, 0), (own_ref, 0), (own_ref, 1), (outer_ref, 1), (outer_ref, 0))):
         uf[t] = functools.partial(plane_of, ref, plane)
-    inner, outer = tile_of(inner_ref, CORE_TILES), tile_of(outer_ref, CORE_TILES)
-    near_new = jnp.where(lanes((MODES, 128)) < 3 * RIM_PLANE, 0.0, turn(outer, 2 * RIM_PLANE))
+    near_new = turn(tile_of(outer_ref, CORE_TILES), 2 * RIM_PLANE)
+    near_new = jnp.where(lanes((MODES, 128)) < 3 * RIM_PLANE, 0.0, near_new)
     rims[:, NEAR] = near_known[...] + near_new
-    rims[:, FAR] = far_of(inner, outer)
-    uf.update(near=(rims, NEAR), far=(rims, FAR))
+    uf["near"] = (rims, NEAR)
 
     coef_outer[...] = slab_coefs(outer_ref)
-    coef_rims[:, NEAR] = near_of(coef_inner[:, TAIL], coef_own[:, TAIL], coef_outer[:, TAIL])
-    coef_rims[:, FAR] = far_of(coef_inner[:, TAIL], coef_outer[:, TAIL])
+    near = near_of(coef_inner[:, TAIL], coef_own[:, TAIL], coef_outer[:, TAIL])
+    coef_rims[:, NEAR] = near
+    coef_rims[:, FAR] = near
     cf = {0: (coef_inner, lo(1)), 1: (coef_inner, lo(0)), 2: (coef_own, lo(0)), 3: (coef_own, lo(1))}
-    cf.update({4: (coef_outer, lo(1)), 5: (coef_outer, lo(0)), "near": (coef_rims, NEAR), "far": (coef_rims, FAR)})
+    cf.update({4: (coef_outer, lo(1)), 5: (coef_outer, lo(0)), "near": (coef_rims, NEAR)})
     ef = {t: (ecoef_known, lo(t - 1)) for t in (1, 2)}
     ef.update({3: (ecoef, lo(0)), 4: (ecoef, lo(1)), "near": (ecoef, TAIL)})
 
     pf = {0: (pc_known, lo(0)), 1: (pc_known, lo(1)), 2: (pc_own, lo(0)), 3: (pc_own, lo(1)), 4: (pc, lo(0)), 5: (pc, lo(1))}
-    pf.update(near=(pc, TAIL), far=(pc, FAR_TAIL))
+    pf["near"] = (pc, TAIL)
     qf = {1: (qc_known, lo(0)), 2: (qc_known, lo(1)), 3: (qc, lo(0)), 4: (qc, lo(1)), "near": (qc, TAIL)}
     all_rims = slice(TAIL.start, FAR_TAIL.stop)
     qc[:, lo(0)] = qc_known[:, lo(2)]
     mix(links, get(uf, 5), [(cf[5], into(pf, 5))])
-    sum_coefs(ef, cf, (3, 4), True, steps)
+    sum_coefs(ef, cf, (3, 4), steps)
+    ecoef[:, TAIL] = ecoef_known[:, TAIL] + product(near, near_step[:128, 4 * PLANE :], 3) + 6.0 * near
     ecoef[:, FAR_TAIL] = jnp.zeros((COEF_ROWS, 128), jnp.float32)
     around = neighbours(uf, (4,), steps)[4]
-    x = begun[:, BEGUN_U] + to_rim(get(uf, 4), 4, core_step)
-    around_near = x + from_rim(near_new, near_step[:, 4 * PLANE :]) + from_rim(far_of(None, outer), far_step[...])
+    rims[:, FAR] = begun[:, BEGUN_U] + from_rim(near_new, near_step[:, 4 * PLANE :])
     rim_sums = [((coef_rims, slice(0, 256)), pc), ((ecoef, all_rims), qc)]
     mix(links, rims[...], [(weights, into({0: (ref, all_rims)}, 0)) for weights, ref in rim_sums])
     mix(links, get(uf, 4), [(cf[4], into(pf, 4)), (ef[4], into(qf, 4)), (cf[3], into(qf, 3, -1))])
@@ -432,7 +413,6 @@
     known["near"] = begun[:, BEGUN_P]
     around_p = neighbours(pf, (1, 2, 3, 4, "near"), steps, known)
     mix(links, around, [(cf[4], into(qf, 4, -1))])
-    mix(links, around_near, [(cf["near"], into(qf, "near", -1))])
     mix(links, get(uf, 3), [(ef[3], into(qf, 3, 1))], known=mix3)
 
     sigma = THETA / DELTA
@@ -442,7 +422,8 @@
     sf["near"] = (search, NEAR_TAIL)
     for t, x in around_p.items():
         start = get(uf, t)
-        au = start + 0.5 * (get(qf, t) - x)
+        q = get(qf, t) - (pc[:, FAR_TAIL] if t == "near" else 0.0)
+        au = start + 0.5 * (q - x)
         begin = start * (1.0 / THETA)
         r1 = start - au * (1.0 / THETA)
         new = (rho_next * rho) * begin + (2.0 * rho_next / DELTA) * r1
@@ -536,9 +517,8 @@
         ((MODES, 2 * PLANE), f32),
         ((KL * MODES, PLANE), f32),
         ((KL * MODES, 2 * MODES), bf16),
-        ((PLANE, PLANE + 4 * 128), bf16),
+        ((PLANE, PLANE + 2 * 128), bf16),
         ((256, 4 * PLANE + 128), bf16),
-        ((256, 128), bf16),
     ]
     state = pl.pallas_call(
         prep_kernel,
@@ -552,7 +532,7 @@
     )(own, table)
     more = [
         ((COEF_ROWS, 2 * PLANE + 128), f32),
-        ((COEF_ROWS, 2 * PLANE), f32),
+        ((COEF_ROWS, 2 * PLANE + 128), f32),
         ((MODES, 2 * PLANE), f32),
         ((MODES, 3 * PLANE), f32),
         ((MODES, 128), f32),

time: 47.7 us -> 47.5 us (level)
  no operation moved by 1% of the time
where the time goes in v5:
time: 47.5 us; the launch traced here: 47.3 us
  blocking collectives  28.5 us (60%)
  Pallas kernels  9.62 us (20%)
  starting transfers between devices  7 us (15%)
  waiting for transfers between devices  1.5 us (3%)
  between operations  0.69 us (1%)
    all_to_all x1, blocking collectives, body(): own = lax.all_to_all(send, 'mode', 0, 0, tiled=True)  14.7 us
    all_to_all x1, blocking collectives, body(): back = lax.all_to_all(back, 'mode', 0, 0, tiled=True)  13.8 us
    ppermute x1, starting transfers between devices, body(): outer = lax.ppermute(own, 'space', off_chip)  6.91 us
    pallas_call x1, Pallas kernels, body(): pl.pallas_call(step_kernel, out_shape=jax.ShapeDtypeStruct((GROUPS, 2 * O...  3.56 us
    pallas_call x1, Pallas kernels, body(): pl.pallas_call(between_kernel, out_shape=[jax.ShapeDtypeStruct(*shape) fo...  1.92 us
    pallas_call x1, Pallas kernels, body(): pl.pallas_call(pack_kernel, out_shape=jax.ShapeDtypeStruct((GROUPS, SEND_...  1.77 us
    pallas_call x1, Pallas kernels, body(): pl.pallas_call(prep_kernel, out_shape=[jax.ShapeDtypeStruct(*shape) for s...  1.2 us
    pallas_call x1, Pallas kernels, body(): pl.pallas_call(unpack_kernel, out_shape=(flat, flat), in_specs=whole(2),...  1.18 us
  transfers between devices with their start and end apart: 2, of which 2 were waited for; matrix products, arithmetic and copies ran while one was open for 0% of the time, Pallas kernels for 7%

profile of v5, /device:TPU:97, one launch (start us, length us, event | category | flops | bytes accessed | tf_op | source)
XLA Modules:
  0.0 47.3 jit_solution(8481126284635938059)
XLA Ops:
  0.6 0.0 copy-start
  0.6 1.8 %pack.1 = f32[8,80,128]{2,1,0:T(8,128)S(1)} custom-call(f32[256,256]{1,0:T(8,128)} %bitcast.9, f32[16,256]{1,0:T(8,128)} %bitcast.11, f32[160,256]{1,0:T(8,128)} %bitcast.10, s32[10,128]{1,0:T(8,128)} %bitcast.6), custom_call_target="tpu_custom_call" | custom-call | tf_op jit(solution)/shard_map/pack/pallas_call | solution.py:494
  2.4 14.7 %all_to_all.10.own_ref = f32[8,80,128]{2,1,0:T(8,128)S(1)} all-to-all(f32[8,80,128]{2,1,0:T(8,128)S(1)} %pack.1), channel_id=1, replica_groups=mesh['space'=32,'mode'=8] {'mode'}, dimensions={0} | all-to-all | bytes 655360 | tf_op jit(solution)/shard_map/all_to_all | solution.py:509
  17.1 6.9 %collective-permute-start.1 = (f32[8,80,128]{2,1,0:T(8,128)S(1)}, f32[8,80,128]{2,1,0:T(8,128)S(1)}, u32[]{:S(2)}, u32[]{:S(2)}) collective-permute-start(f32[8,80,128]{2,1,0:T(8,128)S(1)} %all_to_all.10.own_ref), channel_id=1, source_target_pairs={{8,16},{16,8},{24,32},{32,24},{40,48},{48,40},{56,64},{64,56},{72,... | collective-permute-start | bytes 983048 | tf_op jit(solution)/shard_map/ppermute | solution.py:513
  24.1 0.1 collective-permute-start
  24.2 0.0 copy-done
  24.2 1.2 %step_prep.1 = (f32[16,640]{1,0:T(8,128)S(1)}, f32[128,512]{1,0:T(8,128)S(1)}, f32[1280,256]{1,0:T(8,128)S(1)}, bf16[1280,256]{1,0:T(8,128)(2,1)S(1)}, bf16[256,...) custom-call(f32[8,80,128]{2,1,0:T(8,128)S(1)} %all_to_all.10.own_ref, s32[10,128]{1,0:T(8,128)S(1)} %bitcast.7), custom_call_target="tpu_custom_call" | custom-call | flops 17179869184 | bytes 4194304 | tf_op jit(solution)/shard_map/step_prep/pallas_call | solution.py:523
  25.4 0.4 collective-permute-done.inner_ref
  25.8 1.9 %step_between.1 = (f32[16,640]{1,0:T(8,128)S(1)}, f32[16,640]{1,0:T(8,128)S(1)}, f32[128,512]{1,0:T(8,128)S(1)}, f32[128,768]{1,0:T(8,128)S(1)}, f32[128,128]{1,0:T(8,128)S(1)}, /*index=5*/f32[128,1024]{1,0:T(8,128)S(1)}) custom-call(f32[8,80,128]{2,1,0:T(8,128)S(1)} %all_to_all.10.own_ref, f32[8,80,128]{2,1,0:T(8,128)S(1)} %collective-permute-done.inner_ref, ...), custom_call_target="tpu_custom_call" | custom-call | flops 1024 | bytes 1024 | tf_op jit(solution)/shard_map/step_between/pallas_call | solution.py:541
  27.7 1.1 %collective-permute-done.1.outer_ref = f32[8,80,128]{2,1,0:T(8,128)S(1)} collective-permute-done((f32[8,80,128]{2,1,0:T(8,128)S(1)}, f32[8,80,128]{2,1,0:T(8,128)S(1)}, u32[]{:S(2)}, u32[]{:S(2)}) %collective-permute-start.1) | collective-permute-done | bytes 327712 | tf_op jit(solution)/shard_map/ppermute | solution.py:513
  28.8 3.6 %step.1 = f32[8,128,128]{2,1,0:T(8,128)S(1)} custom-call(f32[8,80,128]{2,1,0:T(8,128)S(1)} %all_to_all.10.own_ref, f32[8,80,128]{2,1,0:T(8,128)S(1)} %collective-permute-done.inner_ref, f32[8,80,128]{2,1,0:T(8,128)S(1)} %collective-permute-done.1.outer_ref, f32[16,640]{1,0:T(8,128)S(1)} %get-tuple-element.16.coef_own, ...), custom_call_target="tpu_custom_call" | custom-call | flops 2147483648 | bytes 4194304 | tf_op jit(solution)/shard_map/step/pallas_call | solution.py:550
  32.4 13.8 %all_to_all.11.in_ref = f32[8,128,128]{2,1,0:T(8,128)S(1)} all-to-all(f32[8,128,128]{2,1,0:T(8,128)S(1)} %step.1), channel_id=1, replica_groups=mesh['space'=32,'mode'=8] {'mode'}, dimensions={0} | all-to-all | bytes 1048576 | tf_op jit(solution)/shard_map/all_to_all | solution.py:569
  46.1 1.2 %unpack.1 = (f32[256,256]{1,0:T(8,128)}, f32[256,256]{1,0:T(8,128)}) custom-call(f32[8,128,128]{2,1,0:T(8,128)S(1)} %all_to_all.11.in_ref, s32[10,128]{1,0:T(8,128)S(1)} %bitcast.8), custom_call_target="tpu_custom_call" | custom-call | tf_op jit(solution)/shard_map/unpack/pallas_call | solution.py:571
Async XLA Ops:
  0.6 23.5 %copy-start = (s32[128,10]{0,1:T(8,128)S(1)}, s32[128,10]{0,1:T(8,128)}, u32[]{:S(2)}) copy-start(s32[128,10]{0,1:T(8,128)} %param.7) | copy-start | bytes 15364
  17.1 11.7 %collective-permute-start.1 = (f32[8,80,128]{2,1,0:T(8,128)S(1)}, f32[8,80,128]{2,1,0:T(8,128)S(1)}, u32[]{:S(2)}, u32[]{:S(2)}) collective-permute-start(f32[8,80,128]{2,1,0:T(8,128)S(1)} %all_to_all.10.own_ref), channel_id=1, source_target_pairs={{8,16},{16,8},{24,32},{32,24},{40,48},{48,40},{56,64},{64,56},{72,... | collective-permute-start | bytes 983048 | tf_op jit(solution)/shard_map/ppermute | solution.py:513
  24.1 1.7 %collective-permute-start = (f32[8,80,128]{2,1,0:T(8,128)S(1)}, f32[8,80,128]{2,1,0:T(8,128)S(1)}, u32[]{:S(2)}, u32[]{:S(2)}) collective-permute-start(f32[8,80,128]{2,1,0:T(8,128)S(1)} %all_to_all.10.own_ref), channel_id=1, source_target_pairs={{0,8},{8,0},{16,24},{24,16},{32,40},{40,32},{48,56},{56,48},{64,72... | collective-permute-start | bytes 983048 | tf_op jit(solution)/shard_map/ppermute | solution.py:514

commit v6 on v5

--- a/solution.py
+++ b/solution.py
@@ -376,7 +376,7 @@
     begun[:, BEGUN_P] = to_rim(get(pf, 2), 2, core_step) + to_rim(get(pf, 3), 3, core_step)
 
 
-def step_kernel(own_ref, inner_ref, outer_ref, coef_own, pc_own, mix3, links, core_step, near_step, coef_inner, ecoef_known, pc_known, qc_known, near_known, begun, out_ref, rims, coef_outer, coef_rims, ecoef, pc, qc, search, pc2, qc2, sol, res):
+def step_kernel(own_ref, inner_ref, outer_ref, coef_own, pc_own, mix3, links, core_step, near_step, coef_inner, ecoef_known, pc_known, qc_known, near_known, begun, out_ref, rims, coef_outer, coef_rims, ecoef, pc, qc, search, pc2, qc2, sol, res, mix4):
     steps = (core_step, near_step)
     uf = {}
     for t, (ref, plane) in enumerate(((inner_ref, 1), (inner_ref, 0), (own_ref, 0), (own_ref, 1), (outer_ref, 1), (outer_ref, 0))):
@@ -401,19 +401,21 @@
     all_rims = slice(TAIL.start, FAR_TAIL.stop)
     qc[:, lo(0)] = qc_known[:, lo(2)]
     mix(links, get(uf, 5), [(cf[5], into(pf, 5))])
+    around = neighbours(uf, (4,), steps)[4]
+    rims[:, FAR] = begun[:, BEGUN_U] + from_rim(near_new, near_step[:, 4 * PLANE :])
+    rim_sums = [((coef_rims, slice(0, 256)), pc), ((ecoef, all_rims), qc)]
+    mix(links, get(uf, 4), [(cf[4], into(pf, 4)), (cf[3], into(qf, 3, -1))], mix4)
     sum_coefs(ef, cf, (3, 4), steps)
     ecoef[:, TAIL] = ecoef_known[:, TAIL] + product(near, near_step[:128, 4 * PLANE :], 3) + 6.0 * near
     ecoef[:, FAR_TAIL] = jnp.zeros((COEF_ROWS, 128), jnp.float32)
-    around = neighbours(uf, (4,), steps)[4]
-    rims[:, FAR] = begun[:, BEGUN_U] + from_rim(near_new, near_step[:, 4 * PLANE :])
-    rim_sums = [((coef_rims, slice(0, 256)), pc), ((ecoef, all_rims), qc)]
     mix(links, rims[...], [(weights, into({0: (ref, all_rims)}, 0)) for weights, ref in rim_sums])
-    mix(links, get(uf, 4), [(cf[4], into(pf, 4)), (ef[4], into(qf, 4)), (cf[3], into(qf, 3, -1))])
     known = {t: begun[:, lo(t - 1)] for t in (1, 2, 3)}
     known["near"] = begun[:, BEGUN_P]
     around_p = neighbours(pf, (1, 2, 3, 4, "near"), steps, known)
+    qc[:, lo(1)] = jnp.zeros((MODES, PLANE), jnp.float32)
     mix(links, around, [(cf[4], into(qf, 4, -1))])
     mix(links, get(uf, 3), [(ef[3], into(qf, 3, 1))], known=mix3)
+    mix(links, get(uf, 4), [(ef[4], into(qf, 4, 1))], known=mix4)
 
     sigma = THETA / DELTA
     rho = 1.0 / sigma
@@ -561,7 +563,8 @@
             vmem((MODES, 2 * PLANE + 256), f32),
         ]
         + [vmem((MODES, 4 * PLANE + 128), f32)] * 2
-        + [vmem((MODES, 2 * PLANE), f32)] * 3,
+        + [vmem((MODES, 2 * PLANE), f32)] * 3
+        + [vmem((KL * MODES, PLANE), f32)],
         compiler_params=params,
         cost_estimate=pl.CostEstimate(flops=2 << 30, bytes_accessed=1 << 22, transcendentals=0),
         name="step",

time: 47.5 us -> 47.5 us (level)
  no operation moved by 1% of the time
where the time goes in v6:
time: 47.5 us; the launch traced here: 47.3 us
  blocking collectives  28.5 us (60%)
  Pallas kernels  9.58 us (20%)
  starting transfers between devices  7 us (15%)
  waiting for transfers between devices  1.5 us (3%)
  between operations  0.69 us (1%)
    all_to_all x1, blocking collectives, body(): own = lax.all_to_all(send, 'mode', 0, 0, tiled=True)  14.7 us
    all_to_all x1, blocking collectives, body(): back = lax.all_to_all(back, 'mode', 0, 0, tiled=True)  13.8 us
    ppermute x1, starting transfers between devices, body(): outer = lax.ppermute(own, 'space', off_chip)  6.91 us
    pallas_call x1, Pallas kernels, body(): pl.pallas_call(step_kernel, out_shape=jax.ShapeDtypeStruct((GROUPS, 2 * O...  3.52 us
    pallas_call x1, Pallas kernels, body(): pl.pallas_call(between_kernel, out_shape=[jax.ShapeDtypeStruct(*shape) fo...  1.92 us
    pallas_call x1, Pallas kernels, body(): pl.pallas_call(pack_kernel, out_shape=jax.ShapeDtypeStruct((GROUPS, SEND_...  1.77 us
    pallas_call x1, Pallas kernels, body(): pl.pallas_call(prep_kernel, out_shape=[jax.ShapeDtypeStruct(*shape) for s...  1.2 us
    pallas_call x1, Pallas kernels, body(): pl.pallas_call(unpack_kernel, out_shape=(flat, flat), in_specs=whole(2),...  1.18 us
  transfers between devices with their start and end apart: 2, of which 2 were waited for; matrix products, arithmetic and copies ran while one was open for 0% of the time, Pallas kernels for 7%

profile of v6, /device:TPU:97, one launch (start us, length us, event | category | flops | bytes accessed | tf_op | source)
XLA Modules:
  0.0 47.3 jit_solution(10288322516109605101)
XLA Ops:
  0.6 0.0 copy-start
  0.6 1.8 %pack.1 = f32[8,80,128]{2,1,0:T(8,128)S(1)} custom-call(f32[256,256]{1,0:T(8,128)} %bitcast.9, f32[16,256]{1,0:T(8,128)} %bitcast.11, f32[160,256]{1,0:T(8,128)} %bitcast.10, s32[10,128]{1,0:T(8,128)} %bitcast.6), custom_call_target="tpu_custom_call" | custom-call | tf_op jit(solution)/shard_map/pack/pallas_call | solution.py:496
  2.4 14.7 %all_to_all.10.own_ref = f32[8,80,128]{2,1,0:T(8,128)S(1)} all-to-all(f32[8,80,128]{2,1,0:T(8,128)S(1)} %pack.1), channel_id=1, replica_groups=mesh['space'=32,'mode'=8] {'mode'}, dimensions={0} | all-to-all | bytes 655360 | tf_op jit(solution)/shard_map/all_to_all | solution.py:511
  17.1 6.9 %collective-permute-start.1 = (f32[8,80,128]{2,1,0:T(8,128)S(1)}, f32[8,80,128]{2,1,0:T(8,128)S(1)}, u32[]{:S(2)}, u32[]{:S(2)}) collective-permute-start(f32[8,80,128]{2,1,0:T(8,128)S(1)} %all_to_all.10.own_ref), channel_id=1, source_target_pairs={{8,16},{16,8},{24,32},{32,24},{40,48},{48,40},{56,64},{64,56},{72,... | collective-permute-start | bytes 983048 | tf_op jit(solution)/shard_map/ppermute | solution.py:515
  24.1 0.1 collective-permute-start
  24.2 0.0 copy-done
  24.2 1.2 %step_prep.1 = (f32[16,640]{1,0:T(8,128)S(1)}, f32[128,512]{1,0:T(8,128)S(1)}, f32[1280,256]{1,0:T(8,128)S(1)}, bf16[1280,256]{1,0:T(8,128)(2,1)S(1)}, bf16[256,...) custom-call(f32[8,80,128]{2,1,0:T(8,128)S(1)} %all_to_all.10.own_ref, s32[10,128]{1,0:T(8,128)S(1)} %bitcast.7), custom_call_target="tpu_custom_call" | custom-call | flops 17179869184 | bytes 4194304 | tf_op jit(solution)/shard_map/step_prep/pallas_call | solution.py:525
  25.4 0.4 collective-permute-done.inner_ref
  25.8 1.9 %step_between.1 = (f32[16,640]{1,0:T(8,128)S(1)}, f32[16,640]{1,0:T(8,128)S(1)}, f32[128,512]{1,0:T(8,128)S(1)}, f32[128,768]{1,0:T(8,128)S(1)}, f32[128,128]{1,0:T(8,128)S(1)}, /*index=5*/f32[128,1024]{1,0:T(8,128)S(1)}) custom-call(f32[8,80,128]{2,1,0:T(8,128)S(1)} %all_to_all.10.own_ref, f32[8,80,128]{2,1,0:T(8,128)S(1)} %collective-permute-done.inner_ref, ...), custom_call_target="tpu_custom_call" | custom-call | flops 1024 | bytes 1024 | tf_op jit(solution)/shard_map/step_between/pallas_call | solution.py:543
  27.7 1.1 %collective-permute-done.1.outer_ref = f32[8,80,128]{2,1,0:T(8,128)S(1)} collective-permute-done((f32[8,80,128]{2,1,0:T(8,128)S(1)}, f32[8,80,128]{2,1,0:T(8,128)S(1)}, u32[]{:S(2)}, u32[]{:S(2)}) %collective-permute-start.1) | collective-permute-done | bytes 327712 | tf_op jit(solution)/shard_map/ppermute | solution.py:515
  28.8 3.5 %step.1 = f32[8,128,128]{2,1,0:T(8,128)S(1)} custom-call(f32[8,80,128]{2,1,0:T(8,128)S(1)} %all_to_all.10.own_ref, f32[8,80,128]{2,1,0:T(8,128)S(1)} %collective-permute-done.inner_ref, f32[8,80,128]{2,1,0:T(8,128)S(1)} %collective-permute-done.1.outer_ref, f32[16,640]{1,0:T(8,128)S(1)} %get-tuple-element.16.coef_own, ...), custom_call_target="tpu_custom_call" | custom-call | flops 2147483648 | bytes 4194304 | tf_op jit(solution)/shard_map/step/pallas_call | solution.py:552
  32.3 13.8 %all_to_all.11.in_ref = f32[8,128,128]{2,1,0:T(8,128)S(1)} all-to-all(f32[8,128,128]{2,1,0:T(8,128)S(1)} %step.1), channel_id=1, replica_groups=mesh['space'=32,'mode'=8] {'mode'}, dimensions={0} | all-to-all | bytes 1048576 | tf_op jit(solution)/shard_map/all_to_all | solution.py:572
  46.1 1.2 %unpack.1 = (f32[256,256]{1,0:T(8,128)}, f32[256,256]{1,0:T(8,128)}) custom-call(f32[8,128,128]{2,1,0:T(8,128)S(1)} %all_to_all.11.in_ref, s32[10,128]{1,0:T(8,128)S(1)} %bitcast.8), custom_call_target="tpu_custom_call" | custom-call | tf_op jit(solution)/shard_map/unpack/pallas_call | solution.py:574
Async XLA Ops:
  0.6 23.5 %copy-start = (s32[128,10]{0,1:T(8,128)S(1)}, s32[128,10]{0,1:T(8,128)}, u32[]{:S(2)}) copy-start(s32[128,10]{0,1:T(8,128)} %param.7) | copy-start | bytes 15364
  17.1 11.7 %collective-permute-start.1 = (f32[8,80,128]{2,1,0:T(8,128)S(1)}, f32[8,80,128]{2,1,0:T(8,128)S(1)}, u32[]{:S(2)}, u32[]{:S(2)}) collective-permute-start(f32[8,80,128]{2,1,0:T(8,128)S(1)} %all_to_all.10.own_ref), channel_id=1, source_target_pairs={{8,16},{16,8},{24,32},{32,24},{40,48},{48,40},{56,64},{64,56},{72,... | collective-permute-start | bytes 983048 | tf_op jit(solution)/shard_map/ppermute | solution.py:515
  24.1 1.7 %collective-permute-start = (f32[8,80,128]{2,1,0:T(8,128)S(1)}, f32[8,80,128]{2,1,0:T(8,128)S(1)}, u32[]{:S(2)}, u32[]{:S(2)}) collective-permute-start(f32[8,80,128]{2,1,0:T(8,128)S(1)} %all_to_all.10.own_ref), channel_id=1, source_target_pairs={{0,8},{8,0},{16,24},{24,16},{32,40},{40,32},{48,56},{56,48},{64,72... | collective-permute-start | bytes 983048 | tf_op jit(solution)/shard_map/ppermute | solution.py:516

commit v7 on v6

--- a/solution.py
+++ b/solution.py
@@ -359,15 +359,16 @@
     cf = {0: (coef_inner, lo(1)), 1: (coef_inner, lo(0)), 2: (coef_own, lo(0)), 3: (coef_own, lo(1))}
     cf["near"] = lambda: near_of(coef_inner[:, TAIL], coef_own[:, TAIL], None)
     ef = {t: (ecoef, lo(t - 1)) for t in (1, 2)}
+    pf = {0: (pc, lo(0)), 1: (pc, lo(1)), 2: (pc_own, lo(0)), 3: (pc_own, lo(1))}
+    qf = {t: (qc, lo(t - 1)) for t in (1, 2, 3)}
+    mix(links, get(uf, 0), [(cf[0], into(pf, 0))])
+    around = neighbours(uf, (1, 2, 3), steps)
     sum_coefs(ef, cf, (1, 2), steps)
     ecoef[:, TAIL] = to_rim(get(cf, 2), 2, core_step, 3) + to_rim(get(cf, 3), 3, core_step, 3)
-    pf = {0: (pc, lo(0)), 1: (pc, lo(1)), 2: (pc_own, lo(0)), 3: (pc_own, lo(1))}
-    qf = {t: (qc, lo(t - 1)) for t in (1, 2, 3)}
     mix(links, get(uf, 1), [(cf[1], into(pf, 1)), (ef[1], into(qf, 1))])
     mix(links, get(uf, 2), [(ef[2], into(qf, 2))])
-    mix(links, get(uf, 0), [(cf[0], into(pf, 0))])
     qc[:, lo(2)] = jnp.zeros((MODES, PLANE), jnp.float32)
-    for t, x in neighbours(uf, (1, 2, 3), steps).items():
+    for t, x in around.items():
         mix(links, x, [(cf[t], into(qf, t, -1))])
     rim = from_rim(near[...], near_step[:, 4 * PLANE :])
     begun[:, BEGUN_U] = rim + to_rim(get(uf, 2), 2, core_step) + to_rim(get(uf, 3), 3, core_step)

time: 47.5 us -> 47.4 us (level)
  transfers between devices with their start and end apart: 2 -> 2, of which waited for: 2 -> 2; matrix products, arithmetic and copies ran while one was open for 0% -> 0% of each run, Pallas kernels for 7% -> 6%
where the time goes in v7:
time: 47.4 us; the launch traced here: 47.2 us
  blocking collectives  28.4 us (60%)
  Pallas kernels  9.52 us (20%)
  starting transfers between devices  7 us (15%)
  waiting for transfers between devices  1.56 us (3%)
  between operations  0.7 us (1%)
    all_to_all x1, blocking collectives, body(): own = lax.all_to_all(send, 'mode', 0, 0, tiled=True)  14.7 us
    all_to_all x1, blocking collectives, body(): back = lax.all_to_all(back, 'mode', 0, 0, tiled=True)  13.7 us
    ppermute x1, starting transfers between devices, body(): outer = lax.ppermute(own, 'space', off_chip)  6.91 us
    pallas_call x1, Pallas kernels, body(): pl.pallas_call(step_kernel, out_shape=jax.ShapeDtypeStruct((GROUPS, 2 * O...  3.52 us
    pallas_call x1, Pallas kernels, body(): pl.pallas_call(between_kernel, out_shape=[jax.ShapeDtypeStruct(*shape) fo...  1.86 us
    pallas_call x1, Pallas kernels, body(): pl.pallas_call(pack_kernel, out_shape=jax.ShapeDtypeStruct((GROUPS, SEND_...  1.77 us
    pallas_call x1, Pallas kernels, body(): pl.pallas_call(prep_kernel, out_shape=[jax.ShapeDtypeStruct(*shape) for s...  1.2 us
    pallas_call x1, Pallas kernels, body(): pl.pallas_call(unpack_kernel, out_shape=(flat, flat), in_specs=whole(2),...  1.18 us
  transfers between devices with their start and end apart: 2, of which 2 were waited for; matrix products, arithmetic and copies ran while one was open for 0% of the time, Pallas kernels for 6%

profile of v7, /device:TPU:97, one launch (start us, length us, event | category | flops | bytes accessed | tf_op | source)
XLA Modules:
  0.0 47.2 jit_solution(7493726762950301385)
XLA Ops:
  0.6 0.0 copy-start
  0.6 1.8 %pack.1 = f32[8,80,128]{2,1,0:T(8,128)S(1)} custom-call(f32[256,256]{1,0:T(8,128)} %bitcast.9, f32[16,256]{1,0:T(8,128)} %bitcast.11, f32[160,256]{1,0:T(8,128)} %bitcast.10, s32[10,128]{1,0:T(8,128)} %bitcast.6), custom_call_target="tpu_custom_call" | custom-call | tf_op jit(solution)/shard_map/pack/pallas_call | solution.py:497
  2.4 14.7 %all_to_all.10.own_ref = f32[8,80,128]{2,1,0:T(8,128)S(1)} all-to-all(f32[8,80,128]{2,1,0:T(8,128)S(1)} %pack.1), channel_id=1, replica_groups=mesh['space'=32,'mode'=8] {'mode'}, dimensions={0} | all-to-all | bytes 655360 | tf_op jit(solution)/shard_map/all_to_all | solution.py:512
  17.1 6.9 %collective-permute-start.1 = (f32[8,80,128]{2,1,0:T(8,128)S(1)}, f32[8,80,128]{2,1,0:T(8,128)S(1)}, u32[]{:S(2)}, u32[]{:S(2)}) collective-permute-start(f32[8,80,128]{2,1,0:T(8,128)S(1)} %all_to_all.10.own_ref), channel_id=1, source_target_pairs={{8,16},{16,8},{24,32},{32,24},{40,48},{48,40},{56,64},{64,56},{72,... | collective-permute-start | bytes 983048 | tf_op jit(solution)/shard_map/ppermute | solution.py:516
  24.1 0.1 collective-permute-start
  24.2 0.0 copy-done
  24.2 1.2 %step_prep.1 = (f32[16,640]{1,0:T(8,128)S(1)}, f32[128,512]{1,0:T(8,128)S(1)}, f32[1280,256]{1,0:T(8,128)S(1)}, bf16[1280,256]{1,0:T(8,128)(2,1)S(1)}, bf16[256,...) custom-call(f32[8,80,128]{2,1,0:T(8,128)S(1)} %all_to_all.10.own_ref, s32[10,128]{1,0:T(8,128)S(1)} %bitcast.7), custom_call_target="tpu_custom_call" | custom-call | flops 17179869184 | bytes 4194304 | tf_op jit(solution)/shard_map/step_prep/pallas_call | solution.py:526
  25.4 0.4 collective-permute-done.inner_ref
  25.8 1.9 %step_between.1 = (f32[16,640]{1,0:T(8,128)S(1)}, f32[16,640]{1,0:T(8,128)S(1)}, f32[128,512]{1,0:T(8,128)S(1)}, f32[128,768]{1,0:T(8,128)S(1)}, f32[128,128]{1,0:T(8,128)S(1)}, /*index=5*/f32[128,1024]{1,0:T(8,128)S(1)}) custom-call(f32[8,80,128]{2,1,0:T(8,128)S(1)} %all_to_all.10.own_ref, f32[8,80,128]{2,1,0:T(8,128)S(1)} %collective-permute-done.inner_ref, ...), custom_call_target="tpu_custom_call" | custom-call | flops 1024 | bytes 1024 | tf_op jit(solution)/shard_map/step_between/pallas_call | solution.py:544
  27.6 1.2 %collective-permute-done.1.outer_ref = f32[8,80,128]{2,1,0:T(8,128)S(1)} collective-permute-done((f32[8,80,128]{2,1,0:T(8,128)S(1)}, f32[8,80,128]{2,1,0:T(8,128)S(1)}, u32[]{:S(2)}, u32[]{:S(2)}) %collective-permute-start.1) | collective-permute-done | bytes 327712 | tf_op jit(solution)/shard_map/ppermute | solution.py:516
  28.8 3.5 %step.1 = f32[8,128,128]{2,1,0:T(8,128)S(1)} custom-call(f32[8,80,128]{2,1,0:T(8,128)S(1)} %all_to_all.10.own_ref, f32[8,80,128]{2,1,0:T(8,128)S(1)} %collective-permute-done.inner_ref, f32[8,80,128]{2,1,0:T(8,128)S(1)} %collective-permute-done.1.outer_ref, f32[16,640]{1,0:T(8,128)S(1)} %get-tuple-element.16.coef_own, ...), custom_call_target="tpu_custom_call" | custom-call | flops 2147483648 | bytes 4194304 | tf_op jit(solution)/shard_map/step/pallas_call | solution.py:553
  32.3 13.7 %all_to_all.11.in_ref = f32[8,128,128]{2,1,0:T(8,128)S(1)} all-to-all(f32[8,128,128]{2,1,0:T(8,128)S(1)} %step.1), channel_id=1, replica_groups=mesh['space'=32,'mode'=8] {'mode'}, dimensions={0} | all-to-all | bytes 1048576 | tf_op jit(solution)/shard_map/all_to_all | solution.py:573
  46.0 1.2 %unpack.1 = (f32[256,256]{1,0:T(8,128)}, f32[256,256]{1,0:T(8,128)}) custom-call(f32[8,128,128]{2,1,0:T(8,128)S(1)} %all_to_all.11.in_ref, s32[10,128]{1,0:T(8,128)S(1)} %bitcast.8), custom_call_target="tpu_custom_call" | custom-call | tf_op jit(solution)/shard_map/unpack/pallas_call | solution.py:575
Async XLA Ops:
  0.6 23.5 %copy-start = (s32[128,10]{0,1:T(8,128)S(1)}, s32[128,10]{0,1:T(8,128)}, u32[]{:S(2)}) copy-start(s32[128,10]{0,1:T(8,128)} %param.7) | copy-start | bytes 15364
  17.1 11.7 %collective-permute-start.1 = (f32[8,80,128]{2,1,0:T(8,128)S(1)}, f32[8,80,128]{2,1,0:T(8,128)S(1)}, u32[]{:S(2)}, u32[]{:S(2)}) collective-permute-start(f32[8,80,128]{2,1,0:T(8,128)S(1)} %all_to_all.10.own_ref), channel_id=1, source_target_pairs={{8,16},{16,8},{24,32},{32,24},{40,48},{48,40},{56,64},{64,56},{72,... | collective-permute-start | bytes 983048 | tf_op jit(solution)/shard_map/ppermute | solution.py:516
  24.1 1.7 %collective-permute-start = (f32[8,80,128]{2,1,0:T(8,128)S(1)}, f32[8,80,128]{2,1,0:T(8,128)S(1)}, u32[]{:S(2)}, u32[]{:S(2)}) collective-permute-start(f32[8,80,128]{2,1,0:T(8,128)S(1)} %all_to_all.10.own_ref), channel_id=1, source_target_pairs={{0,8},{8,0},{16,24},{24,16},{32,40},{40,32},{48,56},{56,48},{64,72... | collective-permute-start | bytes 983048 | tf_op jit(solution)/shard_map/ppermute | solution.py:517

commit v8 on v7

--- a/solution.py
+++ b/solution.py
@@ -329,11 +329,11 @@
 
 def prep_kernel(own_ref, table_ref, coef, pc, mix3, links, core_step, near_step, pad):
     build_links(table_ref, links, pad)
-    build_steps(core_step, near_step)
     coef[...] = slab_coefs(own_ref)
     for plane, kept in ((0, None), (1, mix3)):
         at = slice(PLANE * plane, PLANE * (plane + 1))
         mix(links, plane_of(own_ref, plane), [((coef, at), into({plane: (pc, at)}, plane))], kept)
+    build_steps(core_step, near_step)
 
 
 def lo(n):

time: 47.4 us -> 47.4 us (level)
  no operation moved by 1% of the time
where the time goes in v8:
time: 47.4 us; the launch traced here: 47.2 us
  blocking collectives  28.4 us (60%)
  Pallas kernels  9.53 us (20%)
  starting transfers between devices  7 us (15%)
  waiting for transfers between devices  1.55 us (3%)
  between operations  0.7 us (1%)
    all_to_all x1, blocking collectives, body(): own = lax.all_to_all(send, 'mode', 0, 0, tiled=True)  14.7 us
    all_to_all x1, blocking collectives, body(): back = lax.all_to_all(back, 'mode', 0, 0, tiled=True)  13.7 us
    ppermute x1, starting transfers between devices, body(): outer = lax.ppermute(own, 'space', off_chip)  6.91 us
    pallas_call x1, Pallas kernels, body(): pl.pallas_call(step_kernel, out_shape=jax.ShapeDtypeStruct((GROUPS, 2 * O...  3.52 us
    pallas_call x1, Pallas kernels, body(): pl.pallas_call(between_kernel, out_shape=[jax.ShapeDtypeStruct(*shape) fo...  1.86 us
    pallas_call x1, Pallas kernels, body(): pl.pallas_call(pack_kernel, out_shape=jax.ShapeDtypeStruct((GROUPS, SEND_...  1.77 us
    pallas_call x1, Pallas kernels, body(): pl.pallas_call(prep_kernel, out_shape=[jax.ShapeDtypeStruct(*shape) for s...  1.21 us
    pallas_call x1, Pallas kernels, body(): pl.pallas_call(unpack_kernel, out_shape=(flat, flat), in_specs=whole(2),...  1.18 us
  transfers between devices with their start and end apart: 2, of which 2 were waited for; matrix products, arithmetic and copies ran while one was open for 0% of the time, Pallas kernels for 6%

profile of v8, /device:TPU:97, one launch (start us, length us, event | category | flops | bytes accessed | tf_op | source)
XLA Modules:
  0.0 47.2 jit_solution(10668302000684726034)
XLA Ops:
  0.6 0.0 copy-start
  0.6 1.8 %pack.1 = f32[8,80,128]{2,1,0:T(8,128)S(1)} custom-call(f32[256,256]{1,0:T(8,128)} %bitcast.9, f32[16,256]{1,0:T(8,128)} %bitcast.11, f32[160,256]{1,0:T(8,128)} %bitcast.10, s32[10,128]{1,0:T(8,128)} %bitcast.6), custom_call_target="tpu_custom_call" | custom-call | tf_op jit(solution)/shard_map/pack/pallas_call | solution.py:497
  2.4 14.7 %all_to_all.10.own_ref = f32[8,80,128]{2,1,0:T(8,128)S(1)} all-to-all(f32[8,80,128]{2,1,0:T(8,128)S(1)} %pack.1), channel_id=1, replica_groups=mesh['space'=32,'mode'=8] {'mode'}, dimensions={0} | all-to-all | bytes 655360 | tf_op jit(solution)/shard_map/all_to_all | solution.py:512
  17.1 6.9 %collective-permute-start.1 = (f32[8,80,128]{2,1,0:T(8,128)S(1)}, f32[8,80,128]{2,1,0:T(8,128)S(1)}, u32[]{:S(2)}, u32[]{:S(2)}) collective-permute-start(f32[8,80,128]{2,1,0:T(8,128)S(1)} %all_to_all.10.own_ref), channel_id=1, source_target_pairs={{8,16},{16,8},{24,32},{32,24},{40,48},{48,40},{56,64},{64,56},{72,... | collective-permute-start | bytes 983048 | tf_op jit(solution)/shard_map/ppermute | solution.py:516
  24.1 0.1 collective-permute-start
  24.2 0.0 copy-done
  24.2 1.2 %step_prep.1 = (f32[16,640]{1,0:T(8,128)S(1)}, f32[128,512]{1,0:T(8,128)S(1)}, f32[1280,256]{1,0:T(8,128)S(1)}, bf16[1280,256]{1,0:T(8,128)(2,1)S(1)}, bf16[256,...) custom-call(f32[8,80,128]{2,1,0:T(8,128)S(1)} %all_to_all.10.own_ref, s32[10,128]{1,0:T(8,128)S(1)} %bitcast.7), custom_call_target="tpu_custom_call" | custom-call | flops 17179869184 | bytes 4194304 | tf_op jit(solution)/shard_map/step_prep/pallas_call | solution.py:526
  25.4 0.4 collective-permute-done.inner_ref
  25.8 1.9 %step_between.1 = (f32[16,640]{1,0:T(8,128)S(1)}, f32[16,640]{1,0:T(8,128)S(1)}, f32[128,512]{1,0:T(8,128)S(1)}, f32[128,768]{1,0:T(8,128)S(1)}, f32[128,128]{1,0:T(8,128)S(1)}, /*index=5*/f32[128,1024]{1,0:T(8,128)S(1)}) custom-call(f32[8,80,128]{2,1,0:T(8,128)S(1)} %all_to_all.10.own_ref, f32[8,80,128]{2,1,0:T(8,128)S(1)} %collective-permute-done.inner_ref, ...), custom_call_target="tpu_custom_call" | custom-call | flops 1024 | bytes 1024 | tf_op jit(solution)/shard_map/step_between/pallas_call | solution.py:544
  27.6 1.2 %collective-permute-done.1.outer_ref = f32[8,80,128]{2,1,0:T(8,128)S(1)} collective-permute-done((f32[8,80,128]{2,1,0:T(8,128)S(1)}, f32[8,80,128]{2,1,0:T(8,128)S(1)}, u32[]{:S(2)}, u32[]{:S(2)}) %collective-permute-start.1) | collective-permute-done | bytes 327712 | tf_op jit(solution)/shard_map/ppermute | solution.py:516
  28.8 3.5 %step.1 = f32[8,128,128]{2,1,0:T(8,128)S(1)} custom-call(f32[8,80,128]{2,1,0:T(8,128)S(1)} %all_to_all.10.own_ref, f32[8,80,128]{2,1,0:T(8,128)S(1)} %collective-permute-done.inner_ref, f32[8,80,128]{2,1,0:T(8,128)S(1)} %collective-permute-done.1.outer_ref, f32[16,640]{1,0:T(8,128)S(1)} %get-tuple-element.16.coef_own, ...), custom_call_target="tpu_custom_call" | custom-call | flops 2147483648 | bytes 4194304 | tf_op jit(solution)/shard_map/step/pallas_call | solution.py:553
  32.3 13.7 %all_to_all.11.in_ref = f32[8,128,128]{2,1,0:T(8,128)S(1)} all-to-all(f32[8,128,128]{2,1,0:T(8,128)S(1)} %step.1), channel_id=1, replica_groups=mesh['space'=32,'mode'=8] {'mode'}, dimensions={0} | all-to-all | bytes 1048576 | tf_op jit(solution)/shard_map/all_to_all | solution.py:573
  46.0 1.2 %unpack.1 = (f32[256,256]{1,0:T(8,128)}, f32[256,256]{1,0:T(8,128)}) custom-call(f32[8,128,128]{2,1,0:T(8,128)S(1)} %all_to_all.11.in_ref, s32[10,128]{1,0:T(8,128)S(1)} %bitcast.8), custom_call_target="tpu_custom_call" | custom-call | tf_op jit(solution)/shard_map/unpack/pallas_call | solution.py:575
Async XLA Ops:
  0.6 23.5 %copy-start = (s32[128,10]{0,1:T(8,128)S(1)}, s32[128,10]{0,1:T(8,128)}, u32[]{:S(2)}) copy-start(s32[128,10]{0,1:T(8,128)} %param.7) | copy-start | bytes 15364
  17.1 11.7 %collective-permute-start.1 = (f32[8,80,128]{2,1,0:T(8,128)S(1)}, f32[8,80,128]{2,1,0:T(8,128)S(1)}, u32[]{:S(2)}, u32[]{:S(2)}) collective-permute-start(f32[8,80,128]{2,1,0:T(8,128)S(1)} %all_to_all.10.own_ref), channel_id=1, source_target_pairs={{8,16},{16,8},{24,32},{32,24},{40,48},{48,40},{56,64},{64,56},{72,... | collective-permute-start | bytes 983048 | tf_op jit(solution)/shard_map/ppermute | solution.py:516
  24.1 1.7 %collective-permute-start = (f32[8,80,128]{2,1,0:T(8,128)S(1)}, f32[8,80,128]{2,1,0:T(8,128)S(1)}, u32[]{:S(2)}, u32[]{:S(2)}) collective-permute-start(f32[8,80,128]{2,1,0:T(8,128)S(1)} %all_to_all.10.own_ref), channel_id=1, source_target_pairs={{0,8},{8,0},{16,24},{24,16},{32,40},{40,32},{48,56},{56,48},{64,72... | collective-permute-start | bytes 983048 | tf_op jit(solution)/shard_map/ppermute | solution.py:517
